TPU v7x, 32 devices: a whole 2x2x4 slice. The times are simulated.
32 devices in a mesh: groups: 2 (over y), loop: 4 (over x, core), rows: 4 (over z).
Axes of the slice: x: 2, y: 2, z: 4, core: 2. Of those that a mesh axis runs over, the one named last changes fastest.
Arguments:
- image_feats: float32 [4096, 1152], P(('groups', 'loop', 'rows')), parts along dimension 0, may hold values from -1 to 1
- text_feats: float32 [4096, 1152], P(('groups', 'loop', 'rows')), parts along dimension 0, may hold values from -1 to 1
- log_scale: float32 [1], replicated, may hold values from 2 to 2.5
- bias: float32 [1], replicated, may hold values from -10 to -8
Outputs:
- grad_image: float32 [4096, 1152], P(('groups', 'loop', 'rows')), parts along dimension 0
- grad_text: float32 [4096, 1152], P(('groups', 'loop', 'rows')), parts along dimension 0
- scalars: float32 [6], P('groups'), parts along dimension 0
There are 2 independent parts, one for each index of `groups`. A program takes and returns all parts, laid end to end along the dimension named above; an argument that names none is the same for every part. Nothing has to cross between parts.
All inputs are finite; a program needn't handle non-finite values.
Results may differ from a plain program's by a relative error of at most 0.0045.
Values may be sent and summed in bfloat16 or wider, within the bound.
No kernel may reach another device: no remote copies, remote signals or barrier semaphores. Data moves between devices by JAX's collectives and lax.ppermute only.
A program may use at most 64 MiB of HBM per device.

v0:
```python
import jax
import jax.numpy as jnp
from jax import lax
from jax.sharding import PartitionSpec as P

EPSILON = 1e-06


def from_behind(value, axis, steps):
    count = lax.axis_size(axis)
    pairs = [(source, (source + steps) % count) for source in range(count)]
    return lax.ppermute(value, axis, pairs)


def unit_rows(features):
    inverse = lax.rsqrt(jnp.sum(features * features, axis=1, keepdims=True) + EPSILON)
    return (features * inverse, inverse)


def through_norm(unit, inverse, grad_unit):
    return (grad_unit - unit * jnp.sum(unit * grad_unit, axis=1, keepdims=True)) * inverse


def shards(image_feats, text_feats, log_scale, bias):
    loop_count = lax.axis_size("loop")
    rank_count = lax.axis_size("rows")
    loop_index = lax.axis_index("loop")
    rank_index = lax.axis_index("rows")
    rows_dev = image_feats.shape[0]
    feature_dim = image_feats.shape[1]
    image_unit, image_inv = unit_rows(image_feats)
    text_unit, text_inv = unit_rows(text_feats)
    image_low = image_unit.astype(jnp.bfloat16)
    text_low = text_unit.astype(jnp.bfloat16)
    logit_scale = jnp.exp(log_scale[0])
    logit_bias = bias[0]
    images = lax.all_gather(image_low, "rows", axis=0, tiled=True)
    block_rows = rank_count * rows_dev
    image_ids = loop_index * block_rows + lax.broadcasted_iota(jnp.int32, (block_rows, 1), 0)
    text_offsets = lax.broadcasted_iota(jnp.int32, (1, rows_dev), 1)

    def tile_terms(text_rows, anchor):
        scores = lax.dot_general(
            images, text_rows, (((1,), (1,)), ((), ())), preferred_element_type=jnp.float32
        )
        logits = logit_scale * scores + logit_bias
        text_ids = (anchor * rank_count + rank_index) * rows_dev + text_offsets
        label_sign = jnp.where(image_ids == text_ids, 1.0, -1.0).astype(jnp.float32)
        pair_grad = -label_sign * jax.nn.sigmoid(-label_sign * logits)
        tile_stats = jnp.stack(
            [
                -jnp.sum(jax.nn.log_sigmoid(label_sign * logits)),
                jnp.sum(pair_grad * logit_scale * scores),
                jnp.sum(pair_grad),
            ]
        )
        grad_low = pair_grad.astype(jnp.bfloat16)
        image_term = logit_scale * jnp.dot(grad_low, text_rows, preferred_element_type=jnp.float32)
        text_term = logit_scale * lax.dot_general(
            grad_low, images, (((0,), (0,)), ((), ())), preferred_element_type=jnp.float32
        )
        return (image_term, text_term, tile_stats)

    def visit(text_rows, partial_value, shared, anchor):
        image_acc, totals, text_store = shared
        image_term, text_term, tile_stats = tile_terms(text_rows, anchor)
        image_acc = image_acc + image_term
        totals = totals + tile_stats
        text_store = lax.dynamic_update_index_in_dim(text_store, text_term, anchor, 0)
        return (partial_value, (image_acc, totals, text_store))

    def advance(text_rows, partial_value, stride):
        return (from_behind(text_rows, "loop", stride), partial_value)

    zero_text = jnp.zeros((rows_dev, feature_dim), jnp.float32)
    store_shape = (loop_count, rows_dev, feature_dim)
    shared = (
        jnp.zeros((block_rows, feature_dim), jnp.float32),
        jnp.zeros((3,), jnp.float32),
        jnp.zeros(store_shape, jnp.float32),
    )
    ahead_partial, shared = visit(text_low, zero_text, shared, loop_index)
    hops_ahead = loop_count - 1
    hops_behind = 0

    def both_step(step_index, loop_state):
        ahead_rows, ahead_partial, behind_rows, behind_partial, shared = loop_state
        ahead_rows, ahead_partial = advance(ahead_rows, ahead_partial, 1)
        behind_rows, behind_partial = advance(behind_rows, behind_partial, -1)
        ahead_anchor = jnp.mod(loop_index - step_index - 1, loop_count)
        behind_anchor = jnp.mod(loop_index + step_index + 1, loop_count)
        ahead_partial, shared = visit(ahead_rows, ahead_partial, shared, ahead_anchor)
        behind_partial, shared = visit(behind_rows, behind_partial, shared, behind_anchor)
        return (ahead_rows, ahead_partial, behind_rows, behind_partial, shared)

    def ahead_step(step_index, loop_state):
        ahead_rows, ahead_partial, behind_rows, behind_partial, shared = loop_state
        ahead_rows, ahead_partial = advance(ahead_rows, ahead_partial, 1)
        ahead_anchor = jnp.mod(loop_index - step_index - 1, loop_count)
        ahead_partial, shared = visit(ahead_rows, ahead_partial, shared, ahead_anchor)
        return (ahead_rows, ahead_partial, behind_rows, behind_partial, shared)

    loop_state = (text_low, ahead_partial, text_low, zero_text, shared)
    loop_state = lax.fori_loop(hops_behind, hops_ahead, ahead_step, loop_state)
    ahead_rows, ahead_partial, behind_rows, behind_partial, shared = loop_state
    image_acc, totals, text_store = shared
    text_grad_unit = lax.psum_scatter(
        text_store.reshape(loop_count * rows_dev, feature_dim),
        "loop",
        scatter_dimension=0,
        tiled=True,
    )
    image_grad_unit = lax.psum_scatter(image_acc, "rows", scatter_dimension=0, tiled=True)
    totals = lax.psum(totals, ("loop", "rows"))
    scalars = totals / (loop_count * block_rows)
    grad_image = through_norm(image_unit, image_inv, image_grad_unit)
    grad_text = through_norm(text_unit, text_inv, text_grad_unit)
    return (grad_image, grad_text, scalars)


def solution(mesh):
    in_specs = (P(("groups", "loop", "rows"), None), P(("groups", "loop", "rows"), None), P(), P())
    out_specs = (
        P(("groups", "loop", "rows"), None),
        P(("groups", "loop", "rows"), None),
        P("groups"),
    )
    return jax.shard_map(shards, mesh=mesh, in_specs=in_specs, out_specs=out_specs, check_vma=False)
```

profile of v0, /device:TPU:0, one launch (start us, length us, event | category | flops | bytes accessed | tf_op | source)
XLA Modules:
  0.0 191.5 jit_solution(3019514366734472820)
XLA Ops:
  7.2 0.0 copy-start.3
  7.2 0.0 all-gather.2.cloned.1.call-start
  7.2 1.2 multiply_reduce_fusion.3
  8.5 1.9 multiply_convert_fusion
  10.4 0.0 all-gather.2.cloned.1.call-update
  10.4 0.0 reduce-scatter.3.cloned.1.call-start
  11.8 1.2 multiply_reduce_fusion.4
  13.0 0.0 copy-done.3
  13.0 0.1 multiply_convert_fusion.1
  13.1 30.6 %all-gather.2.cloned.1.call-done = bf16[512,1152]{1,0:T(8,128)(2,1)} async-done(((bf16[128,1152]{1,0:T(8,128)(2,1)}), bf16[512,1152]{1,0:T(8,128)(2,1)}) %all-gather.2.cloned.1.call-update) | async-done | bytes 1179664 | tf_op jit(solution)/shard_map/all_gather | solution.py:37
  43.7 2.7 %fusion.30 = (f32[]{:T(128)}, f32[]{:T(128)}, f32[]{:T(128)}, f32[512,128]{1,0:T(8,128)S(1)}) fusion(f32[]{:T(128)} %bitcast.49, f32[]{:T(128)} %bitcast, s32[128]{0:T(128)S(1)} %iota_add_fusion.3, s32[512]{0:T(512)S(1)} %iota_add_fusion.2, bf16[512,1152]{1,0:T(8,128)(2,1)} %all-gather.2.cloned.1.call-done, bf16[128,1152]{1,0:T(8,128)(2,1)S(1)} %multiply_convert_fusion.1), kind=kOutput, calls=%fused_computation.49 | convolution fusion | flops 152502272 | bytes 1739284 | tf_op jit(solution)/shard_map/dot_general | solution.py:43
  46.3 0.0 copy-start.4
  46.4 0.5 convolution_multiply_fusion.2
  46.9 2.0 %pad_maximum_fusion = f32[3]{0:T(128)S(1)} fusion(f32[1]{0:T(128)} %bitcast.4, f32[1]{0:T(128)} %bitcast.3, f32[1]{0:T(128)} %bitcast.2), kind=kLoop, calls=%fused_computation.55 | loop fusion | flops 6 | bytes 24 | tf_op jit(solution)/shard_map/stack | solution.py:50
  48.9 0.2 broadcast_in_dim.51
  49.0 0.0 copy-done.4
  49.0 0.5 fusion.22
  49.5 0.0 copy-start.1
  49.6 1.4 copy-done.1
  50.9 45.8 %while.22 = (s32[]{:T(128)}, bf16[128,1152]{1,0:T(8,128)(2,1)S(1)}, f32[512,1152]{1,0:T(8,128)S(1)}, f32[3]{0:T(128)S(1)}, f32[4,128,1152]{2,1,0:T(8,128)}, /*in...) while((s32[]{:T(128)}, bf16[128,1152]{1,0:T(8,128)(2,1)S(1)}, ...), condition=%wide.region_9.10_spmd.clone, body=%wide.region_5.9_spmd.clone.sunk | while | flops 457261696 | bytes 15544312 | solution.py:104
  50.9 0.0 collective-permute-start
  50.9 0.0 copy-start.5
  51.0 6.1 %collective-permute-done = bf16[128,1152]{1,0:T(8,128)(2,1)S(1)} collective-permute-done((bf16[128,1152]{1,0:T(8,128)(2,1)S(1)}, bf16[128,1152]{1,0:T(8,128)(2,1)S(1)}, u32[]{:S(2)}, u32[]{:S(2)}) %collective-permute-start) | collective-permute-done | bytes 294944 | tf_op jit(solution)/shard_map/while/body/eval_jaxpr/ppermute | solution.py:12
  57.1 3.3 %fusion.61 = (f32[]{:T(128)}, f32[]{:T(128)}, f32[]{:T(128)}, f32[512,128]{1,0:T(8,128)S(1)}) fusion(f32[]{:T(128)} %get-tuple-element.470, f32[]{:T(128)} %get-tuple-element.466, s32[128]{0:T(128)S(1)} %fusion.60, s32[512]{0:T(512)S(1)} %bitcast.52, bf16[512,1152]{1,0:T(8,128)(2,1)} %get-tuple-element.469, ...), kind=kOutput, calls=%fused_computation.17.clone.1 | convolution fusion | flops 152502272 | bytes 1739284 | tf_op jit(solution)/shard_map/while/body/eval_jaxpr/dot_general | solution.py:43
  60.3 0.0 copy-done.5
  60.4 2.0 %fusion.63 = f32[4,128,1152]{2,1,0:T(8,128)} fusion(f32[4,128,1152]{2,1,0:T(8,128)} %get-tuple-element.448, s32[]{:T(128)S(6)} %select_n.147, bf16[512,1152]{1,0:T(8,128)(2,1)S(1)} %copy-done.5, f32[]{:T(128)} %get-tuple-element.466, f32[512,128]{1,0:T(8,128)S(1)} %get-tuple-element.423, f32[]{:T(128)} %get-tuple-element.470, s32[128]{0:T(128)S(1)} %fusion.60, ...), kind=kOutput, calls=%fused_computation.6.clone.1 | convolution fusion | flops 151863296 | bytes 2035716 | tf_op jit(solution)/shard_map/while/body/eval_jaxpr/dot_general | solution.py:59
  62.3 1.9 %maximum_add_fusion.2 = f32[3]{0:T(128)S(1)} fusion(f32[3]{0:T(128)S(1)} %get-tuple-element.447, f32[1]{0:T(128)} %bitcast.45, f32[1]{0:T(128)} %bitcast.46, f32[1]{0:T(128)} %bitcast.47), kind=kLoop, calls=%fused_computation.23.clone.1 | loop fusion | flops 9 | bytes 36 | tf_op jit(solution)/shard_map/while/body/eval_jaxpr/add | solution.py:68
  64.3 1.9 fusion.62
  66.2 0.1 collective-permute-start
  66.3 0.0 copy-start.5
  66.3 6.1 %collective-permute-done = bf16[128,1152]{1,0:T(8,128)(2,1)S(1)} collective-permute-done((bf16[128,1152]{1,0:T(8,128)(2,1)S(1)}, bf16[128,1152]{1,0:T(8,128)(2,1)S(1)}, u32[]{:S(2)}, u32[]{:S(2)}) %collective-permute-start) | collective-permute-done | bytes 294944 | tf_op jit(solution)/shard_map/while/body/eval_jaxpr/ppermute | solution.py:12
  72.4 3.3 %fusion.61 = (f32[]{:T(128)}, f32[]{:T(128)}, f32[]{:T(128)}, f32[512,128]{1,0:T(8,128)S(1)}) fusion(f32[]{:T(128)} %get-tuple-element.470, f32[]{:T(128)} %get-tuple-element.466, s32[128]{0:T(128)S(1)} %fusion.60, s32[512]{0:T(512)S(1)} %bitcast.52, bf16[512,1152]{1,0:T(8,128)(2,1)} %get-tuple-element.469, ...), kind=kOutput, calls=%fused_computation.17.clone.1 | convolution fusion | flops 152502272 | bytes 1739284 | tf_op jit(solution)/shard_map/while/body/eval_jaxpr/dot_general | solution.py:43
  75.6 0.0 copy-done.5
  75.7 2.0 %fusion.63 = f32[4,128,1152]{2,1,0:T(8,128)} fusion(f32[4,128,1152]{2,1,0:T(8,128)} %get-tuple-element.448, s32[]{:T(128)S(6)} %select_n.147, bf16[512,1152]{1,0:T(8,128)(2,1)S(1)} %copy-done.5, f32[]{:T(128)} %get-tuple-element.466, f32[512,128]{1,0:T(8,128)S(1)} %get-tuple-element.423, f32[]{:T(128)} %get-tuple-element.470, s32[128]{0:T(128)S(1)} %fusion.60, ...), kind=kOutput, calls=%fused_computation.6.clone.1 | convolution fusion | flops 151863296 | bytes 2035716 | tf_op jit(solution)/shard_map/while/body/eval_jaxpr/dot_general | solution.py:59
  77.6 1.9 %maximum_add_fusion.2 = f32[3]{0:T(128)S(1)} fusion(f32[3]{0:T(128)S(1)} %get-tuple-element.447, f32[1]{0:T(128)} %bitcast.45, f32[1]{0:T(128)} %bitcast.46, f32[1]{0:T(128)} %bitcast.47), kind=kLoop, calls=%fused_computation.23.clone.1 | loop fusion | flops 9 | bytes 36 | tf_op jit(solution)/shard_map/while/body/eval_jaxpr/add | solution.py:68
  79.6 1.9 fusion.62
  81.5 0.1 collective-permute-start
  81.6 0.0 copy-start.5
  81.6 6.1 %collective-permute-done = bf16[128,1152]{1,0:T(8,128)(2,1)S(1)} collective-permute-done((bf16[128,1152]{1,0:T(8,128)(2,1)S(1)}, bf16[128,1152]{1,0:T(8,128)(2,1)S(1)}, u32[]{:S(2)}, u32[]{:S(2)}) %collective-permute-start) | collective-permute-done | bytes 294944 | tf_op jit(solution)/shard_map/while/body/eval_jaxpr/ppermute | solution.py:12
  87.7 3.3 %fusion.61 = (f32[]{:T(128)}, f32[]{:T(128)}, f32[]{:T(128)}, f32[512,128]{1,0:T(8,128)S(1)}) fusion(f32[]{:T(128)} %get-tuple-element.470, f32[]{:T(128)} %get-tuple-element.466, s32[128]{0:T(128)S(1)} %fusion.60, s32[512]{0:T(512)S(1)} %bitcast.52, bf16[512,1152]{1,0:T(8,128)(2,1)} %get-tuple-element.469, ...), kind=kOutput, calls=%fused_computation.17.clone.1 | convolution fusion | flops 152502272 | bytes 1739284 | tf_op jit(solution)/shard_map/while/body/eval_jaxpr/dot_general | solution.py:43
  91.0 0.0 copy-done.5
  91.0 2.0 %fusion.63 = f32[4,128,1152]{2,1,0:T(8,128)} fusion(f32[4,128,1152]{2,1,0:T(8,128)} %get-tuple-element.448, s32[]{:T(128)S(6)} %select_n.147, bf16[512,1152]{1,0:T(8,128)(2,1)S(1)} %copy-done.5, f32[]{:T(128)} %get-tuple-element.466, f32[512,128]{1,0:T(8,128)S(1)} %get-tuple-element.423, f32[]{:T(128)} %get-tuple-element.470, s32[128]{0:T(128)S(1)} %fusion.60, ...), kind=kOutput, calls=%fused_computation.6.clone.1 | convolution fusion | flops 151863296 | bytes 2035716 | tf_op jit(solution)/shard_map/while/body/eval_jaxpr/dot_general | solution.py:59
  92.9 1.9 %maximum_add_fusion.2 = f32[3]{0:T(128)S(1)} fusion(f32[3]{0:T(128)S(1)} %get-tuple-element.447, f32[1]{0:T(128)} %bitcast.45, f32[1]{0:T(128)} %bitcast.46, f32[1]{0:T(128)} %bitcast.47), kind=kLoop, calls=%fused_computation.23.clone.1 | loop fusion | flops 9 | bytes 36 | tf_op jit(solution)/shard_map/while/body/eval_jaxpr/add | solution.py:68
  94.9 1.9 fusion.62
  96.8 0.0 copy-start
  96.8 0.0 copy-start.2
  96.8 1.4 copy-done
  98.2 0.0 reduce-scatter.3.cloned.1.call-update
  98.2 0.0 reduce-scatter.5.cloned.1.call-start
  98.3 0.7 reduce-scatter.5.cloned.1.call-update
  99.0 32.6 %psum.7 = f32[3]{0:T(128)S(1)} all-reduce(f32[3]{0:T(128)S(1)} %get-tuple-element.295), channel_id=1, replica_groups=mesh['groups'=2,'loop'=4,'rows'=4] {'loop','rows'}, use_global_device_ids=true, to_apply=%region_14.15 | all-reduce | flops 3 | bytes 24 | tf_op jit(solution)/shard_map/psum | solution.py:114
  131.5 0.5 broadcast_multiply_fusion
  132.1 14.5 %reduce-scatter.3.cloned.1.call-done = f32[128,1152]{1,0:T(8,128)} async-done(((f32[512,1152]{1,0:T(8,128)}), f32[128,1152]{1,0:T(8,128)}) %reduce-scatter.3.cloned.1.call-update) | async-done | bytes 589840 | tf_op jit(solution)/shard_map/reduce_scatter | solution.py:113
  146.5 0.0 copy-done.2
  146.5 1.3 multiply_reduce_fusion.2
  147.8 2.1 %subtract_multiply_fusion.1 = f32[128,1152]{1,0:T(8,128)} fusion(f32[128,1152]{1,0:T(8,128)} %reduce-scatter.3.cloned.1.call-done, f32[128,1152]{1,0:T(8,128)S(1)} %copy-done.2, f32[128]{0:T(128)S(1)} %multiply_reduce_fusion.2, f32[128]{0:T(128)S(1)} %add_rsqrt_fusion), kind=kLoop, calls=%fused_computation.34 | loop fusion | flops 589824 | bytes 1770496 | tf_op jit(solution)/shard_map/mul | solution.py:21
  149.9 31.8 %reduce-scatter.5.cloned.1.call-done = f32[128,1152]{1,0:T(8,128)} async-done(((f32[512,1152]{1,0:T(8,128)}), f32[128,1152]{1,0:T(8,128)}) %reduce-scatter.5.cloned.1.call-update) | async-done | bytes 589840 | tf_op jit(solution)/shard_map/reduce_scatter | solution.py:107
  181.7 1.3 multiply_reduce_fusion.1
  183.0 2.1 %subtract_multiply_fusion = f32[128,1152]{1,0:T(8,128)} fusion(f32[128,1152]{1,0:T(8,128)} %reduce-scatter.5.cloned.1.call-done, f32[128,1152]{1,0:T(8,128)S(1)} %copy-done.3, f32[128]{0:T(128)S(1)} %multiply_reduce_fusion.1, f32[128]{0:T(128)S(1)} %add_rsqrt_fusion.1), kind=kLoop, calls=%fused_computation.32 | loop fusion | flops 589824 | bytes 1770496 | tf_op jit(solution)/shard_map/mul | solution.py:21
  (13 shorter events, 0.1 us)
Async XLA Ops:
  7.2 5.8 %copy-start.3 = (f32[128,1152]{1,0:T(8,128)S(1)}, f32[128,1152]{1,0:T(8,128)}, u32[]{:S(2)}) copy-start(f32[128,1152]{1,0:T(8,128)} %param.7) | copy-start | bytes 1769476
  7.2 36.5 %all-gather.2.cloned.1.call-start = ((), (), s32[]{:S(2)}) async-start(), calls=%async_computation.2 | async-start | bytes 1474560 | tf_op jit(solution)/shard_map/all_gather | solution.py:37
  10.4 136.2 %reduce-scatter.3.cloned.1.call-start = ((), (), s32[]{:S(2)}) async-start(), calls=%async_computation.3 | async-start | bytes 2949120 | tf_op jit(solution)/shard_map/reduce_scatter | solution.py:113
  46.3 2.7 %copy-start.4 = (bf16[512,1152]{1,0:T(8,128)(2,1)S(1)}, bf16[512,1152]{1,0:T(8,128)(2,1)}, u32[]{:S(2)}) copy-start(bf16[512,1152]{1,0:T(8,128)(2,1)} %all-gather.2.cloned.1.call-done) | copy-start | bytes 3538948
  49.5 1.4 copy-start.1
  50.9 6.1 %collective-permute-start = (bf16[128,1152]{1,0:T(8,128)(2,1)S(1)}, bf16[128,1152]{1,0:T(8,128)(2,1)S(1)}, u32[]{:S(2)}, u32[]{:S(2)}) collective-permute-start(bf16[128,1152]{1,0:T(8,128)(2,1)S(1)} %get-tuple-element.445), channel_id=1, source_target_pairs={{0,4},{4,8},{8,12},{12,0},{1,5},{5,9},{9,13},{13,1},{2,6},{6,10},{... | collective-permute-start | bytes 884744 | tf_op jit(solution)/shard_map/while/body/eval_jaxpr/ppermute | solution.py:12
  50.9 9.4 %copy-start.5 = (bf16[512,1152]{1,0:T(8,128)(2,1)S(1)}, bf16[512,1152]{1,0:T(8,128)(2,1)}, u32[]{:S(2)}) copy-start(bf16[512,1152]{1,0:T(8,128)(2,1)} %get-tuple-element.469) | copy-start | bytes 3538948 | tf_op jit(solution)/shard_map/while
  66.2 6.2 %collective-permute-start = (bf16[128,1152]{1,0:T(8,128)(2,1)S(1)}, bf16[128,1152]{1,0:T(8,128)(2,1)S(1)}, u32[]{:S(2)}, u32[]{:S(2)}) collective-permute-start(bf16[128,1152]{1,0:T(8,128)(2,1)S(1)} %get-tuple-element.445), channel_id=1, source_target_pairs={{0,4},{4,8},{8,12},{12,0},{1,5},{5,9},{9,13},{13,1},{2,6},{6,10},{... | collective-permute-start | bytes 884744 | tf_op jit(solution)/shard_map/while/body/eval_jaxpr/ppermute | solution.py:12
  66.3 9.4 %copy-start.5 = (bf16[512,1152]{1,0:T(8,128)(2,1)S(1)}, bf16[512,1152]{1,0:T(8,128)(2,1)}, u32[]{:S(2)}) copy-start(bf16[512,1152]{1,0:T(8,128)(2,1)} %get-tuple-element.469) | copy-start | bytes 3538948 | tf_op jit(solution)/shard_map/while
  81.5 6.2 %collective-permute-start = (bf16[128,1152]{1,0:T(8,128)(2,1)S(1)}, bf16[128,1152]{1,0:T(8,128)(2,1)S(1)}, u32[]{:S(2)}, u32[]{:S(2)}) collective-permute-start(bf16[128,1152]{1,0:T(8,128)(2,1)S(1)} %get-tuple-element.445), channel_id=1, source_target_pairs={{0,4},{4,8},{8,12},{12,0},{1,5},{5,9},{9,13},{13,1},{2,6},{6,10},{... | collective-permute-start | bytes 884744 | tf_op jit(solution)/shard_map/while/body/eval_jaxpr/ppermute | solution.py:12
  81.6 9.4 %copy-start.5 = (bf16[512,1152]{1,0:T(8,128)(2,1)S(1)}, bf16[512,1152]{1,0:T(8,128)(2,1)}, u32[]{:S(2)}) copy-start(bf16[512,1152]{1,0:T(8,128)(2,1)} %get-tuple-element.469) | copy-start | bytes 3538948 | tf_op jit(solution)/shard_map/while
  96.8 1.4 copy-start
  96.8 49.7 %copy-start.2 = (f32[128,1152]{1,0:T(8,128)S(1)}, f32[128,1152]{1,0:T(8,128)}, u32[]{:S(2)}) copy-start(f32[128,1152]{1,0:T(8,128)} %param.6) | copy-start | bytes 1769476
  98.2 83.5 %reduce-scatter.5.cloned.1.call-start = ((), (), s32[]{:S(2)}) async-start(), calls=%async_computation.4 | async-start | bytes 2949120 | tf_op jit(solution)/shard_map/reduce_scatter | solution.py:107
Sparse Core Ops, SparseCore 0:
  10.5 33.1 all-gather.1
  98.3 48.1 reduce-scatter.2
  149.1 32.5 reduce-scatter.4
where the time goes:
time: 192 us
  waiting for transfers between devices  95.8 us (50%)
  blocking collectives  32.6 us (17%)
  matrix products  25.1 us (13%)
  other arithmetic  19.4 us (10%)
  between operations  15.2 us (8%)
  local copies, waits for them, and re-layouts  3.03 us (2%)
    psum x1, blocking collectives, shards(): totals = lax.psum(totals, ('loop', 'rows'))  32.6 us
    reduce_scatter x1, waiting for transfers between devices, shards(): lax.psum_scatter(text_store.reshape(loop_count * rows_dev, feature_dim),...  31.8 us
    all_gather x1, waiting for transfers between devices, shards(): images = lax.all_gather(image_low, 'rows', axis=0, tiled=True)  30.6 us
    ppermute x3, waiting for transfers between devices, from_behind(): return lax.ppermute(value, axis, pairs)  18.3 us
    reduce_scatter x1, waiting for transfers between devices, shards(): lax.psum_scatter(image_acc, 'rows', scatter_dimension=0, tiled=True)  14.5 us
    dot_general x4, matrix products, tile_terms(): lax.dot_general(images, text_rows, (((1,), (1,)), ((), ())), preferred_el...  12.4 us
    dot_general x4, matrix products, tile_terms(): lax.dot_general(grad_low, images, (((0,), (0,)), ((), ())), preferred_ele...  6.46 us
    dot_general x4, matrix products, tile_terms(): jnp.dot(grad_low, text_rows, preferred_element_type=jnp.float32)  6.17 us
  transfers between devices with their start and end apart: 6, of which 6 were waited for; matrix products, arithmetic and copies ran while one was open for 3% of the time, Pallas kernels for 0%

commit v1 on v0

v1 whole, which is shorter than its diff:
```python
import jax
import jax.numpy as jnp
from jax import lax
from jax.experimental import pallas as pl
from jax.experimental.pallas import tpu as pltpu
from jax.sharding import PartitionSpec as P

EPSILON = 1e-06
TILE_BLOCKS = 4
VMEM = pl.BlockSpec(memory_space=pltpu.VMEM)
SMEM = pl.BlockSpec(memory_space=pltpu.SMEM)
PARAMS = pltpu.CompilerParams(vmem_limit_bytes=24 * 1024 * 1024)
ROW_DOT = (((1,), (1,)), ((), ()))
COL_DOT = (((0,), (0,)), ((), ()))


def call(kernel, outs, flops, *args, smem=0):
    nbytes = sum(a.size * a.dtype.itemsize for a in (*args, *outs))
    single = len(outs) == 1
    return pl.pallas_call(
        kernel,
        out_shape=outs[0] if single else tuple(outs),
        in_specs=[SMEM] * smem + [VMEM] * (len(args) - smem),
        out_specs=VMEM if single else tuple([VMEM] * len(outs)),
        compiler_params=PARAMS,
        cost_estimate=pl.CostEstimate(flops=flops, bytes_accessed=nbytes, transcendentals=0),
    )(*args)


def normalize_kernel(feats_ref, low_ref):
    feats = feats_ref[...]
    inverse = lax.rsqrt(jnp.sum(feats * feats, axis=1, keepdims=True) + EPSILON)
    low_ref[...] = (feats * inverse).astype(low_ref.dtype)


def normalize(feats):
    out = jax.ShapeDtypeStruct(feats.shape, jnp.bfloat16)
    return call(normalize_kernel, [out], 4 * feats.size, feats)


def tile_kernel(has_own, n_image, n_text, *refs):
    scale_ref, bias_ref = refs[:2]
    images = jnp.concatenate([r[...] for r in refs[2 : 2 + n_image]], axis=0)
    texts = jnp.concatenate([r[...] for r in refs[2 + n_image : 2 + n_image + n_text]], axis=0)
    outs = refs[2 + n_image + n_text :]
    image_outs, text_outs, stats_ref = outs[:n_image], outs[n_image:-1], outs[-1]
    rows = image_outs[0].shape[0]
    scores = lax.dot_general(images, texts, ROW_DOT, preferred_element_type=jnp.float32)
    scaled = scale_ref[0] * scores
    logits = scaled + bias_ref[0]
    if has_own:
        row = lax.broadcasted_iota(jnp.int32, logits.shape, 0)
        col = lax.broadcasted_iota(jnp.int32, logits.shape, 1)
        sign = jnp.where((row == col) & (row < rows), 1.0, -1.0).astype(jnp.float32)
    else:
        sign = jnp.full(logits.shape, -1.0, jnp.float32)
    against = -sign * logits
    small = jnp.exp(-jnp.abs(against))
    above = jnp.where(against >= 0, 1.0, small) / (1.0 + small)
    pair_grad = -sign * above
    loss = jnp.maximum(against, 0.0) + jnp.log1p(small)
    which = lax.broadcasted_iota(jnp.int32, stats_ref.shape, 0)
    stats_ref[...] = jnp.where(
        which == 0,
        jnp.sum(loss),
        jnp.where(which == 1, jnp.sum(pair_grad * scaled), jnp.sum(pair_grad)),
    )
    grad_low = pair_grad.astype(jnp.bfloat16)
    image_grad = jnp.dot(grad_low, texts, preferred_element_type=jnp.float32)
    for i, ref in enumerate(image_outs):
        ref[...] = image_grad[i * rows : (i + 1) * rows].astype(ref.dtype)
    text_grad = lax.dot_general(grad_low, images, COL_DOT, preferred_element_type=jnp.float32)
    for i, ref in enumerate(text_outs):
        ref[...] = text_grad[i * rows : (i + 1) * rows].astype(ref.dtype)


def tile(has_own, scale, bias, images, texts, image_types, text_types):
    shape = images[0].shape
    outs = [jax.ShapeDtypeStruct(shape, t) for t in (*image_types, *text_types)]
    outs.append(jax.ShapeDtypeStruct((8, 128), jnp.float32))
    flops = 6 * len(images) * len(texts) * shape[0] * shape[0] * shape[1]
    n_image, n_text = len(images), len(texts)

    def kernel(*refs):
        tile_kernel(has_own, n_image, n_text, *refs)

    got = call(kernel, outs, flops, scale, bias, *images, *texts, smem=2)
    return got[:n_image], got[n_image:-1], got[-1]


def add_kernel(*refs):
    total = refs[0][...].astype(jnp.float32)
    for ref in refs[1:-1]:
        total = total + ref[...].astype(jnp.float32)
    refs[-1][...] = total.astype(refs[-1].dtype)


def add_low(*parts):
    out = jax.ShapeDtypeStruct(parts[0].shape, jnp.bfloat16)
    return call(add_kernel, [out], parts[0].size * len(parts), *parts)


def finish_kernel(scale_ref, feats_ref, *refs):
    feats = feats_ref[...]
    inverse = lax.rsqrt(jnp.sum(feats * feats, axis=1, keepdims=True) + EPSILON)
    unit = feats * inverse
    total = refs[0][...].astype(jnp.float32)
    for ref in refs[1:-1]:
        total = total + ref[...].astype(jnp.float32)
    grad = scale_ref[0] * total
    refs[-1][...] = (grad - unit * jnp.sum(unit * grad, axis=1, keepdims=True)) * inverse


def finish(scale, feats, parts):
    out = jax.ShapeDtypeStruct(feats.shape, jnp.float32)
    return call(finish_kernel, [out], 10 * feats.size, scale, feats, *parts, smem=1)


class Ranks:
    def __init__(self, mesh):
        loop, rows = mesh.shape["loop"], mesh.shape["rows"]
        core = 2 if loop % 2 == 0 else 1
        low = 2 if rows % 2 == 0 else 1
        self.sizes = {"x": loop // core, "core": core, "high": rows // low, "low": low}

    def shift(self, value, part, steps):
        n = self.sizes[part]
        steps %= n
        if steps == 0:
            return value
        s = self.sizes
        if part in ("x", "core"):
            axis, inner = "loop", s["core"]
            outer = s["x"]
        else:
            axis, inner = "rows", s["low"]
            outer = s["high"]
        pairs = []
        for a in range(outer):
            for b in range(inner):
                if part in ("x", "high"):
                    to = ((a + steps) % n) * inner + b
                else:
                    to = a * inner + (b + steps) % n
                pairs.append((a * inner + b, to))
        return lax.ppermute(value, axis, pairs)


def gather(ranks, own, far, near):
    held = [ranks.shift(own, far, k) for k in range(ranks.sizes[far])]
    return [[ranks.shift(b, near, k) for k in range(ranks.sizes[near])] for b in held]


def scatter(ranks, partial, far, near):
    n_near, n_far = ranks.sizes[near], ranks.sizes[far]
    got = [None] * n_far
    for f in [*range(1, n_far), 0]:
        got[f] = [ranks.shift(partial[f][k], near, -k) for k in range(n_near)]
    sums = [*got[0]]
    for f in range(1, n_far):
        sums.append(ranks.shift(add_low(*got[f]), far, -f))
    return sums


def sum_everywhere(ranks, value):
    for part in ("core", "x", "low", "high"):
        value = sum([ranks.shift(value, part, k) for k in range(1, ranks.sizes[part])], value)
    return value


def solution(mesh):
    ranks = Ranks(mesh)
    batch_devices = mesh.shape["loop"] * mesh.shape["rows"]

    def shards(image_feats, text_feats, log_scale, bias):
        scale = jnp.exp(log_scale)
        image_low = normalize(image_feats)
        text_low = normalize(text_feats)
        images = gather(ranks, image_low, "low", "x")
        texts = gather(ranks, text_low, "high", "core")
        image_keys = [(f, k) for f in range(len(images)) for k in range(len(images[0]))]
        text_keys = [(f, k) for f in range(len(texts)) for k in range(len(texts[0]))]
        image_part, text_part, stats = {}, {}, None
        one_tile = len(image_keys) <= TILE_BLOCKS and len(text_keys) <= TILE_BLOCKS

        def part_type(key):
            wide = key == (0, 0) or not one_tile
            return jnp.float32 if wide else jnp.bfloat16

        for i in range(0, len(image_keys), TILE_BLOCKS):
            for j in range(0, len(text_keys), TILE_BLOCKS):
                ik, tk = image_keys[i : i + TILE_BLOCKS], text_keys[j : j + TILE_BLOCKS]
                image_term, text_term, tile_stats = tile(
                    i == 0 and j == 0,
                    scale,
                    bias,
                    [images[f][k] for f, k in ik],
                    [texts[f][k] for f, k in tk],
                    [part_type(key) for key in ik],
                    [part_type(key) for key in tk],
                )
                for key, term in zip(ik, image_term):
                    image_part[key] = image_part[key] + term if key in image_part else term
                for key, term in zip(tk, text_term):
                    text_part[key] = text_part[key] + term if key in text_part else term
                stats = tile_stats if stats is None else stats + tile_stats

        def nested(part, like):
            return [
                [part[f, k] if (f, k) == (0, 0) else part[f, k].astype(jnp.bfloat16) for k in range(len(like[0]))]
                for f in range(len(like))
            ]

        image_sums = scatter(ranks, nested(image_part, images), "low", "x")
        text_sums = scatter(ranks, nested(text_part, texts), "high", "core")
        stats = sum_everywhere(ranks, stats)
        scalars = stats[:3, 0] / (batch_devices * image_feats.shape[0])
        grad_image = finish(scale, image_feats, image_sums)
        grad_text = finish(scale, text_feats, text_sums)
        return grad_image, grad_text, scalars

    rows_spec = P(("groups", "loop", "rows"), None)
    return jax.shard_map(
        shards,
        mesh=mesh,
        in_specs=(rows_spec, rows_spec, P(), P()),
        out_specs=(rows_spec, rows_spec, P("groups")),
        check_vma=False,
    )
```

time: 192 us -> 63.4 us (0.33)
  waiting for transfers between devices: 95.8 us -> 34.4 us
  blocking collectives: 32.6 us -> 0 us
  matrix products: 25.1 us -> 0 us
  starting transfers between devices: 0.24 us -> 19.4 us
  other arithmetic: 19.4 us -> 0.64 us
  between operations: 15.2 us -> 2.05 us
  Pallas kernels: 0 us -> 5.67 us
    reduce_scatter x2 -> x0, waiting for transfers between devices: 46.3 us -> none  [the longest x1 31.8 us: shards(): lax.psum_scatter(text_store.reshape(loop_count * rows_dev, feature_dim),...]
    psum x1 -> x0, blocking collectives: 32.6 us -> none  [shards(): totals = lax.psum(totals, ('loop', 'rows'))]
    all_gather x1 -> x0, waiting for transfers between devices: 30.6 us -> none  [shards(): images = lax.all_gather(image_low, 'rows', axis=0, tiled=True)]
    dot_general x12 -> x0, matrix products: 25.1 us -> none  [the longest x4 12.4 us: tile_terms(): lax.dot_general(images, text_rows, (((1,), (1,)), ((), ())), preferred_el...]
    ppermute x3 -> x16, starting transfers between devices: 0.12 us -> 19.4 us  [shift(): return lax.ppermute(value, axis, pairs)]
    ppermute x3 -> x16, waiting for transfers between devices: 18.3 us -> 34.4 us  [shift(): return lax.ppermute(value, axis, pairs)]
    add x11 -> x4, other arithmetic: 5.83 us -> 0.01 us  [sum_everywhere(): sum([ranks.shift(value, part, k) for k in range(1, ranks.sizes[part])], v...]
    pallas_call x0 -> x7, Pallas kernels: none -> 5.67 us  [call(): pl.pallas_call(kernel, out_shape=outs[0] if single else tuple(outs), in_s...]
  transfers between devices with their start and end apart: 6 -> 16, of which waited for: 6 -> 8; matrix products, arithmetic and copies ran while one was open for 3% -> 1% of each run, Pallas kernels for 0% -> 2%
where the time goes in v1:
time: 63.4 us; the launch traced here: 63.2 us
  waiting for transfers between devices  34.4 us (54%)
  starting transfers between devices  19.4 us (31%)
  Pallas kernels  5.67 us (9%)
  between operations  2.05 us (3%)
  local copies, waits for them, and re-layouts  1.13 us (2%)
  other arithmetic  0.64 us (1%)
    ppermute x16, waiting for transfers between devices, shift(): return lax.ppermute(value, axis, pairs)  34.4 us
    ppermute x16, starting transfers between devices, shift(): return lax.ppermute(value, axis, pairs)  19.4 us
    pallas_call x7, Pallas kernels, call(): pl.pallas_call(kernel, out_shape=outs[0] if single else tuple(outs), in_s...  5.67 us
  transfers between devices with their start and end apart: 16, of which 8 were waited for; matrix products, arithmetic and copies ran while one was open for 1% of the time, Pallas kernels for 2%

profile of v1, /device:TPU:0, one launch (start us, length us, event | category | flops | bytes accessed | tf_op | source)
XLA Modules:
  0.0 63.2 jit_solution(1657270769514982240)
XLA Ops:
  0.6 0.0 copy-start
  0.6 0.0 copy-start.1
  0.7 1.1 %copy-done.1 = f32[128,1152]{1,0:T(8,128)S(1)} copy-done((f32[128,1152]{1,0:T(8,128)S(1)}, f32[128,1152]{1,0:T(8,128)}, u32[]{:S(2)}) %copy-start.1) | copy-done | bytes 589848
  1.8 0.1 shard_map.68.refs_6_
  1.9 4.1 %collective-permute-start.4 = (bf16[128,1152]{1,0:T(8,128)(2,1)S(1)}, bf16[128,1152]{1,0:T(8,128)(2,1)S(1)}, u32[]{:S(2)}, u32[]{:S(2)}) collective-permute-start(bf16[128,1152]{1,0:T(8,128)(2,1)S(1)} %shard_map.68.refs_6_), channel_id=1, source_target_pairs={{0,2},{1,3},{2,0},{3,1},{4,6},{5,7},{6,4},{7,5},{8,10},{9,11},{10,... | collective-permute-start | bytes 884744 | tf_op jit(solution)/shard_map/ppermute | solution.py:146
  6.0 0.0 copy-done
  6.0 0.1 shard_map.67.refs_2_
  6.1 1.6 %collective-permute-start.1 = (bf16[128,1152]{1,0:T(8,128)(2,1)S(1)}, bf16[128,1152]{1,0:T(8,128)(2,1)S(1)}, u32[]{:S(2)}, u32[]{:S(2)}) collective-permute-start(bf16[128,1152]{1,0:T(8,128)(2,1)S(1)} %shard_map.67.refs_2_), channel_id=1, source_target_pairs={{0,1},{1,0},{2,3},{3,2},{4,5},{5,4},{6,7},{7,6},{8,9},{9,8},{10,11... | collective-permute-start | bytes 884744 | tf_op jit(solution)/shard_map/ppermute | solution.py:146
  7.8 0.0 collective-permute-start.3
  7.8 1.5 %collective-permute-start = (bf16[128,1152]{1,0:T(8,128)(2,1)S(1)}, bf16[128,1152]{1,0:T(8,128)(2,1)S(1)}, u32[]{:S(2)}, u32[]{:S(2)}) collective-permute-start(bf16[128,1152]{1,0:T(8,128)(2,1)S(1)} %shard_map.67.refs_2_), channel_id=1, source_target_pairs={{0,8},{4,12},{8,0},{12,4},{1,9},{5,13},{9,1},{13,5},{2,10},{6,14},... | collective-permute-start | bytes 884744 | tf_op jit(solution)/shard_map/ppermute | solution.py:146
  9.3 10.2 %collective-permute-done.4.refs_8_ = bf16[128,1152]{1,0:T(8,128)(2,1)S(1)} collective-permute-done((bf16[128,1152]{1,0:T(8,128)(2,1)S(1)}, bf16[128,1152]{1,0:T(8,128)(2,1)S(1)}, u32[]{:S(2)}, u32[]{:S(2)}) %collective-permute-start.4) | collective-permute-done | bytes 294944 | tf_op jit(solution)/shard_map/ppermute | solution.py:146
  19.4 0.0 collective-permute-start.5
  19.4 0.4 collective-permute-done.1.refs_4_
  19.8 1.5 %collective-permute-start.2 = (bf16[128,1152]{1,0:T(8,128)(2,1)S(1)}, bf16[128,1152]{1,0:T(8,128)(2,1)S(1)}, u32[]{:S(2)}, u32[]{:S(2)}) collective-permute-start(bf16[128,1152]{1,0:T(8,128)(2,1)S(1)} %collective-permute-done.1.refs_4_), channel_id=1, source_target_pairs={{0,8},{4,12},{8,0},{12,4},{1,9},{5,13},{9,1},{13,5},{2,10},{6,14},... | collective-permute-start | bytes 884744 | tf_op jit(solution)/shard_map/ppermute | solution.py:146
  22.7 0.0 collective-permute-done.3.refs_7_
  22.7 0.0 collective-permute-done.refs_3_
  22.7 0.0 collective-permute-done.5.refs_9_
  22.7 6.1 %collective-permute-done.2.refs_5_ = bf16[128,1152]{1,0:T(8,128)(2,1)S(1)} collective-permute-done((bf16[128,1152]{1,0:T(8,128)(2,1)S(1)}, bf16[128,1152]{1,0:T(8,128)(2,1)S(1)}, u32[]{:S(2)}, u32[]{:S(2)}) %collective-permute-start.2) | collective-permute-done | bytes 294944 | tf_op jit(solution)/shard_map/ppermute | solution.py:146
  28.9 3.0 %shard_map.69 = (f32[128,1152]{1,0:T(8,128)S(1)}, bf16[128,1152]{1,0:T(8,128)(2,1)S(1)}, bf16[128,1152]{1,0:T(8,128)(2,1)S(1)}, bf16[128,1152]{1,0:T(8,128)(2,1)...) custom-call(f32[1]{0:T(128)S(6)} %exp.3.refs_0_.scale_ref, ...), custom_call_target="tpu_custom_call" | custom-call | flops 1811939328 | bytes 5312520 | tf_op jit(solution)/shard_map/pallas_call | solution.py:20
  31.9 1.6 %collective-permute-start.7 = (bf16[128,1152]{1,0:T(8,128)(2,1)S(1)}, bf16[128,1152]{1,0:T(8,128)(2,1)S(1)}, u32[]{:S(2)}, u32[]{:S(2)}) collective-permute-start(bf16[128,1152]{1,0:T(8,128)(2,1)S(1)} %get-tuple-element.15), channel_id=1, source_target_pairs={{0,8},{4,12},{8,0},{12,4},{1,9},{5,13},{9,1},{13,5},{2,10},{6,14},... | collective-permute-start | bytes 884744 | tf_op jit(solution)/shard_map/ppermute | solution.py:146
  33.5 0.0 collective-permute-start.10
  33.5 0.5 collective-permute-start.6
  34.0 7.9 %collective-permute-done.7.refs_1_ = bf16[128,1152]{1,0:T(8,128)(2,1)S(1)} collective-permute-done((bf16[128,1152]{1,0:T(8,128)(2,1)S(1)}, bf16[128,1152]{1,0:T(8,128)(2,1)S(1)}, u32[]{:S(2)}, u32[]{:S(2)}) %collective-permute-start.7) | collective-permute-done | bytes 294944 | tf_op jit(solution)/shard_map/ppermute | solution.py:146
  41.9 0.1 shard_map.70
  42.0 0.7 %collective-permute-start.8 = (bf16[128,1152]{1,0:T(8,128)(2,1)S(1)}, bf16[128,1152]{1,0:T(8,128)(2,1)S(1)}, u32[]{:S(2)}, u32[]{:S(2)}) collective-permute-start(bf16[128,1152]{1,0:T(8,128)(2,1)S(1)} %shard_map.70), channel_id=1, source_target_pairs={{0,1},{1,0},{2,3},{3,2},{4,5},{5,4},{6,7},{7,6},{8,9},{9,8},{10,11... | collective-permute-start | bytes 884744 | tf_op jit(solution)/shard_map/ppermute | solution.py:146
  42.7 0.0 collective-permute-start.9
  42.7 0.0 collective-permute-done.10.refs_1_
  42.7 0.1 shard_map.72
  42.8 3.4 %collective-permute-start.11 = (bf16[128,1152]{1,0:T(8,128)(2,1)S(1)}, bf16[128,1152]{1,0:T(8,128)(2,1)S(1)}, u32[]{:S(2)}, u32[]{:S(2)}) collective-permute-start(bf16[128,1152]{1,0:T(8,128)(2,1)S(1)} %shard_map.72), channel_id=1, source_target_pairs={{0,2},{1,3},{2,0},{3,1},{4,6},{5,7},{6,4},{7,5},{8,10},{9,11},{10,... | collective-permute-start | bytes 884744 | tf_op jit(solution)/shard_map/ppermute | solution.py:146
  46.2 0.2 collective-permute-start.12
  46.4 0.9 %collective-permute-done.12 = f32[8,128]{1,0:T(8,128)S(1)} collective-permute-done((f32[8,128]{1,0:T(8,128)S(1)}, f32[8,128]{1,0:T(8,128)S(1)}, u32[]{:S(2)}, u32[]{:S(2)}) %collective-permute-start.12) | collective-permute-done | bytes 4128 | tf_op jit(solution)/shard_map/ppermute | solution.py:146
  47.3 1.5 %collective-permute-start.13 = (f32[8,128]{1,0:T(8,128)S(1)}, f32[8,128]{1,0:T(8,128)S(1)}, u32[]{:S(2)}, u32[]{:S(2)}) collective-permute-start(f32[8,128]{1,0:T(8,128)S(1)} %add.12), channel_id=1, source_target_pairs={{0,8},{4,12},{8,0},{12,4},{1,9},{5,13},{9,1},{13,5},{2,10},{6,14},... | collective-permute-start | bytes 12296 | tf_op jit(solution)/shard_map/ppermute | solution.py:146
  48.8 2.1 %collective-permute-done.13 = f32[8,128]{1,0:T(8,128)S(1)} collective-permute-done((f32[8,128]{1,0:T(8,128)S(1)}, f32[8,128]{1,0:T(8,128)S(1)}, u32[]{:S(2)}, u32[]{:S(2)}) %collective-permute-start.13) | collective-permute-done | bytes 4128 | tf_op jit(solution)/shard_map/ppermute | solution.py:146
  50.9 0.1 collective-permute-start.14
  51.0 3.5 %collective-permute-done.14 = f32[8,128]{1,0:T(8,128)S(1)} collective-permute-done((f32[8,128]{1,0:T(8,128)S(1)}, f32[8,128]{1,0:T(8,128)S(1)}, u32[]{:S(2)}, u32[]{:S(2)}) %collective-permute-start.14) | collective-permute-done | bytes 4128 | tf_op jit(solution)/shard_map/ppermute | solution.py:146
  54.6 2.6 %collective-permute-start.15 = (f32[8,128]{1,0:T(8,128)S(1)}, f32[8,128]{1,0:T(8,128)S(1)}, u32[]{:S(2)}, u32[]{:S(2)}) collective-permute-start(f32[8,128]{1,0:T(8,128)S(1)} %add.14), channel_id=1, source_target_pairs={{0,2},{1,3},{2,0},{3,1},{4,6},{5,7},{6,4},{7,5},{8,10},{9,11},{10,... | collective-permute-start | bytes 12296 | tf_op jit(solution)/shard_map/ppermute | solution.py:146
  57.1 3.2 %collective-permute-done.15 = f32[8,128]{1,0:T(8,128)S(1)} collective-permute-done((f32[8,128]{1,0:T(8,128)S(1)}, f32[8,128]{1,0:T(8,128)S(1)}, u32[]{:S(2)}, u32[]{:S(2)}) %collective-permute-start.15) | collective-permute-done | bytes 4128 | tf_op jit(solution)/shard_map/ppermute | solution.py:146
  60.3 0.6 multiply_reduce_fusion
  61.0 0.0 collective-permute-done.6.refs_1_
  61.0 0.0 collective-permute-done.8.refs_2_
  61.0 0.0 copy-start.2
  61.0 1.1 %shard_map.71 = f32[128,1152]{1,0:T(8,128)} custom-call(f32[1]{0:T(128)S(6)} %exp.3.refs_0_.scale_ref, f32[128,1152]{1,0:T(8,128)S(1)} %copy-done, f32[128,1152]{1,0:T(8,128)S(1)} %get-tuple-element.12.refs_0_, bf16[128,1152]{1,0:T(8,128)(2,1)S(1)} %collective-permute-done.6.refs_1_, bf16[128,1152]{1,0:T(8,128)(2,1)S(1)} %collective-permute-done.8.refs_2_), custom_call_target="tpu_custom_call" | custom-call | flops 1474560 | bytes 2359300 | tf_op jit(solution)/shard_map/pallas_call | solution.py:20
  62.1 0.0 collective-permute-done.9.refs_1_
  62.1 0.0 collective-permute-done.11.refs_2_
  62.1 0.0 copy-done.2
  62.1 1.1 %shard_map.73 = f32[128,1152]{1,0:T(8,128)} custom-call(f32[1]{0:T(128)S(6)} %exp.3.refs_0_.scale_ref, f32[128,1152]{1,0:T(8,128)S(1)} %copy-done.2, f32[128,1152]{1,0:T(8,128)S(1)} %get-tuple-element.16.refs_0_, bf16[128,1152]{1,0:T(8,128)(2,1)S(1)} %collective-permute-done.9.refs_1_, bf16[128,1152]{1,0:T(8,128)(2,1)S(1)} %collective-permute-done.11.refs_2_), custom_call_target="tpu_custom_call" | custom-call | flops 1474560 | bytes 2359300 | tf_op jit(solution)/shard_map/pallas_call | solution.py:20
  (4 shorter events, 0.0 us)
Async XLA Ops:
  0.6 5.4 %copy-start = (f32[128,1152]{1,0:T(8,128)S(1)}, f32[128,1152]{1,0:T(8,128)}, u32[]{:S(2)}) copy-start(f32[128,1152]{1,0:T(8,128)} %feats_ref.6) | copy-start | bytes 1769476
  0.6 1.1 %copy-start.1 = (f32[128,1152]{1,0:T(8,128)S(1)}, f32[128,1152]{1,0:T(8,128)}, u32[]{:S(2)}) copy-start(f32[128,1152]{1,0:T(8,128)} %feats_ref.7) | copy-start | bytes 1769476
  1.9 17.5 %collective-permute-start.4 = (bf16[128,1152]{1,0:T(8,128)(2,1)S(1)}, bf16[128,1152]{1,0:T(8,128)(2,1)S(1)}, u32[]{:S(2)}, u32[]{:S(2)}) collective-permute-start(bf16[128,1152]{1,0:T(8,128)(2,1)S(1)} %shard_map.68.refs_6_), channel_id=1, source_target_pairs={{0,2},{1,3},{2,0},{3,1},{4,6},{5,7},{6,4},{7,5},{8,10},{9,11},{10,... | collective-permute-start | bytes 884744 | tf_op jit(solution)/shard_map/ppermute | solution.py:146
  6.1 13.7 %collective-permute-start.1 = (bf16[128,1152]{1,0:T(8,128)(2,1)S(1)}, bf16[128,1152]{1,0:T(8,128)(2,1)S(1)}, u32[]{:S(2)}, u32[]{:S(2)}) collective-permute-start(bf16[128,1152]{1,0:T(8,128)(2,1)S(1)} %shard_map.67.refs_2_), channel_id=1, source_target_pairs={{0,1},{1,0},{2,3},{3,2},{4,5},{5,4},{6,7},{7,6},{8,9},{9,8},{10,11... | collective-permute-start | bytes 884744 | tf_op jit(solution)/shard_map/ppermute | solution.py:146
  7.8 14.9 %collective-permute-start.3 = (bf16[128,1152]{1,0:T(8,128)(2,1)S(1)}, bf16[128,1152]{1,0:T(8,128)(2,1)S(1)}, u32[]{:S(2)}, u32[]{:S(2)}) collective-permute-start(bf16[128,1152]{1,0:T(8,128)(2,1)S(1)} %shard_map.68.refs_6_), channel_id=1, source_target_pairs={{0,4},{4,0},{8,12},{12,8},{1,5},{5,1},{9,13},{13,9},{2,6},{6,2},{1... | collective-permute-start | bytes 884744 | tf_op jit(solution)/shard_map/ppermute | solution.py:146
  7.8 14.9 %collective-permute-start = (bf16[128,1152]{1,0:T(8,128)(2,1)S(1)}, bf16[128,1152]{1,0:T(8,128)(2,1)S(1)}, u32[]{:S(2)}, u32[]{:S(2)}) collective-permute-start(bf16[128,1152]{1,0:T(8,128)(2,1)S(1)} %shard_map.67.refs_2_), channel_id=1, source_target_pairs={{0,8},{4,12},{8,0},{12,4},{1,9},{5,13},{9,1},{13,5},{2,10},{6,14},... | collective-permute-start | bytes 884744 | tf_op jit(solution)/shard_map/ppermute | solution.py:146
  19.4 3.3 %collective-permute-start.5 = (bf16[128,1152]{1,0:T(8,128)(2,1)S(1)}, bf16[128,1152]{1,0:T(8,128)(2,1)S(1)}, u32[]{:S(2)}, u32[]{:S(2)}) collective-permute-start(bf16[128,1152]{1,0:T(8,128)(2,1)S(1)} %collective-permute-done.4.refs_8_), channel_id=1, source_target_pairs={{0,4},{4,0},{8,12},{12,8},{1,5},{5,1},{9,13},{13,9},{2,6},{6,2},{1... | collective-permute-start | bytes 884744 | tf_op jit(solution)/shard_map/ppermute | solution.py:146
  19.8 9.0 %collective-permute-start.2 = (bf16[128,1152]{1,0:T(8,128)(2,1)S(1)}, bf16[128,1152]{1,0:T(8,128)(2,1)S(1)}, u32[]{:S(2)}, u32[]{:S(2)}) collective-permute-start(bf16[128,1152]{1,0:T(8,128)(2,1)S(1)} %collective-permute-done.1.refs_4_), channel_id=1, source_target_pairs={{0,8},{4,12},{8,0},{12,4},{1,9},{5,13},{9,1},{13,5},{2,10},{6,14},... | collective-permute-start | bytes 884744 | tf_op jit(solution)/shard_map/ppermute | solution.py:146
  31.9 10.0 %collective-permute-start.7 = (bf16[128,1152]{1,0:T(8,128)(2,1)S(1)}, bf16[128,1152]{1,0:T(8,128)(2,1)S(1)}, u32[]{:S(2)}, u32[]{:S(2)}) collective-permute-start(bf16[128,1152]{1,0:T(8,128)(2,1)S(1)} %get-tuple-element.15), channel_id=1, source_target_pairs={{0,8},{4,12},{8,0},{12,4},{1,9},{5,13},{9,1},{13,5},{2,10},{6,14},... | collective-permute-start | bytes 884744 | tf_op jit(solution)/shard_map/ppermute | solution.py:146
  33.5 9.2 %collective-permute-start.10 = (bf16[128,1152]{1,0:T(8,128)(2,1)S(1)}, bf16[128,1152]{1,0:T(8,128)(2,1)S(1)}, u32[]{:S(2)}, u32[]{:S(2)}) collective-permute-start(bf16[128,1152]{1,0:T(8,128)(2,1)S(1)} %get-tuple-element.19), channel_id=1, source_target_pairs={{0,4},{4,0},{8,12},{12,8},{1,5},{5,1},{9,13},{13,9},{2,6},{6,2},{1... | collective-permute-start | bytes 884744 | tf_op jit(solution)/shard_map/ppermute | solution.py:146
  33.5 27.5 %collective-permute-start.6 = (bf16[128,1152]{1,0:T(8,128)(2,1)S(1)}, bf16[128,1152]{1,0:T(8,128)(2,1)S(1)}, u32[]{:S(2)}, u32[]{:S(2)}) collective-permute-start(bf16[128,1152]{1,0:T(8,128)(2,1)S(1)} %get-tuple-element.13), channel_id=1, source_target_pairs={{0,8},{4,12},{8,0},{12,4},{1,9},{5,13},{9,1},{13,5},{2,10},{6,14},... | collective-permute-start | bytes 884744 | tf_op jit(solution)/shard_map/ppermute | solution.py:146
  42.0 19.0 %collective-permute-start.8 = (bf16[128,1152]{1,0:T(8,128)(2,1)S(1)}, bf16[128,1152]{1,0:T(8,128)(2,1)S(1)}, u32[]{:S(2)}, u32[]{:S(2)}) collective-permute-start(bf16[128,1152]{1,0:T(8,128)(2,1)S(1)} %shard_map.70), channel_id=1, source_target_pairs={{0,1},{1,0},{2,3},{3,2},{4,5},{5,4},{6,7},{7,6},{8,9},{9,8},{10,11... | collective-permute-start | bytes 884744 | tf_op jit(solution)/shard_map/ppermute | solution.py:146
  42.7 19.4 %collective-permute-start.9 = (bf16[128,1152]{1,0:T(8,128)(2,1)S(1)}, bf16[128,1152]{1,0:T(8,128)(2,1)S(1)}, u32[]{:S(2)}, u32[]{:S(2)}) collective-permute-start(bf16[128,1152]{1,0:T(8,128)(2,1)S(1)} %get-tuple-element.17), channel_id=1, source_target_pairs={{0,4},{4,0},{8,12},{12,8},{1,5},{5,1},{9,13},{13,9},{2,6},{6,2},{1... | collective-permute-start | bytes 884744 | tf_op jit(solution)/shard_map/ppermute | solution.py:146
  42.8 19.4 %collective-permute-start.11 = (bf16[128,1152]{1,0:T(8,128)(2,1)S(1)}, bf16[128,1152]{1,0:T(8,128)(2,1)S(1)}, u32[]{:S(2)}, u32[]{:S(2)}) collective-permute-start(bf16[128,1152]{1,0:T(8,128)(2,1)S(1)} %shard_map.72), channel_id=1, source_target_pairs={{0,2},{1,3},{2,0},{3,1},{4,6},{5,7},{6,4},{7,5},{8,10},{9,11},{10,... | collective-permute-start | bytes 884744 | tf_op jit(solution)/shard_map/ppermute | solution.py:146
  46.2 1.2 %collective-permute-start.12 = (f32[8,128]{1,0:T(8,128)S(1)}, f32[8,128]{1,0:T(8,128)S(1)}, u32[]{:S(2)}, u32[]{:S(2)}) collective-permute-start(f32[8,128]{1,0:T(8,128)S(1)} %get-tuple-element.20), channel_id=1, source_target_pairs={{0,4},{4,0},{8,12},{12,8},{1,5},{5,1},{9,13},{13,9},{2,6},{6,2},{1... | collective-permute-start | bytes 12296 | tf_op jit(solution)/shard_map/ppermute | solution.py:146
  47.3 3.6 %collective-permute-start.13 = (f32[8,128]{1,0:T(8,128)S(1)}, f32[8,128]{1,0:T(8,128)S(1)}, u32[]{:S(2)}, u32[]{:S(2)}) collective-permute-start(f32[8,128]{1,0:T(8,128)S(1)} %add.12), channel_id=1, source_target_pairs={{0,8},{4,12},{8,0},{12,4},{1,9},{5,13},{9,1},{13,5},{2,10},{6,14},... | collective-permute-start | bytes 12296 | tf_op jit(solution)/shard_map/ppermute | solution.py:146
  50.9 3.6 %collective-permute-start.14 = (f32[8,128]{1,0:T(8,128)S(1)}, f32[8,128]{1,0:T(8,128)S(1)}, u32[]{:S(2)}, u32[]{:S(2)}) collective-permute-start(f32[8,128]{1,0:T(8,128)S(1)} %add.13), channel_id=1, source_target_pairs={{0,1},{1,0},{2,3},{3,2},{4,5},{5,4},{6,7},{7,6},{8,9},{9,8},{10,11... | collective-permute-start | bytes 12296 | tf_op jit(solution)/shard_map/ppermute | solution.py:146
  54.6 5.8 %collective-permute-start.15 = (f32[8,128]{1,0:T(8,128)S(1)}, f32[8,128]{1,0:T(8,128)S(1)}, u32[]{:S(2)}, u32[]{:S(2)}) collective-permute-start(f32[8,128]{1,0:T(8,128)S(1)} %add.14), channel_id=1, source_target_pairs={{0,2},{1,3},{2,0},{3,1},{4,6},{5,7},{6,4},{7,5},{8,10},{9,11},{10,... | collective-permute-start | bytes 12296 | tf_op jit(solution)/shard_map/ppermute | solution.py:146
  61.0 1.1 %copy-start.2 = (f32[128,1152]{1,0:T(8,128)S(1)}, f32[128,1152]{1,0:T(8,128)}, u32[]{:S(2)}) copy-start(f32[128,1152]{1,0:T(8,128)} %feats_ref.7) | copy-start | bytes 1769476

commit v2 on v1

v2 whole, which is shorter than its diff:
```python
import functools

import jax
import jax.numpy as jnp
from jax import lax
from jax.experimental import pallas as pl
from jax.experimental.pallas import tpu as pltpu
from jax.sharding import PartitionSpec as P

EPSILON = 1e-06
TILE_BLOCKS = 4
FIRST = 4 * 10**9
VMEM = pl.BlockSpec(memory_space=pltpu.VMEM)
SMEM = pl.BlockSpec(memory_space=pltpu.SMEM)
PARAMS = pltpu.CompilerParams(vmem_limit_bytes=24 * 1024 * 1024)
ROW_DOT = (((1,), (1,)), ((), ()))
COL_DOT = (((0,), (0,)), ((), ()))
LOW, WIDE = jnp.bfloat16, jnp.float32


def array(shape, dtype):
    return jax.ShapeDtypeStruct(shape, dtype)


def call(kernel, outs, flops, *args, smem=0):
    nbytes = sum(a.size * a.dtype.itemsize for a in (*args, *outs))
    single = len(outs) == 1
    return pl.pallas_call(
        kernel,
        out_shape=outs[0] if single else tuple(outs),
        in_specs=[SMEM] * smem + [VMEM] * (len(args) - smem),
        out_specs=VMEM if single else tuple([VMEM] * len(outs)),
        compiler_params=PARAMS,
        cost_estimate=pl.CostEstimate(flops=flops, bytes_accessed=nbytes, transcendentals=0),
    )(*args)


def normalize_kernel(feats_ref, *refs):
    feats = feats_ref[...]
    inverse = lax.rsqrt(jnp.sum(feats * feats, axis=1, keepdims=True) + EPSILON)
    refs[-1][...] = (feats * inverse).astype(LOW)


def normalize(feats, *others):
    return call(normalize_kernel, [array(feats.shape, LOW)], 4 * feats.size, feats, *others)


def token_kernel(*refs):
    refs[-1][...] = jnp.zeros(refs[-1].shape, WIDE)


def token(*others):
    return call(token_kernel, [array((8, 128), WIDE)], 1024, *others)


def tile_kernel(has_own, n_image, n_text, *refs):
    scale_ref, bias_ref = refs[:2]
    texts = jnp.concatenate([r[...] for r in refs[2 : 2 + n_text]], axis=0)
    images = jnp.concatenate([r[...] for r in refs[2 + n_text : 2 + n_text + n_image]], axis=0)
    outs = refs[-1 - n_image - n_text :]
    image_outs, text_outs, stats_ref = outs[:n_image], outs[n_image:-1], outs[-1]
    own = image_outs[0].shape[0]
    scores = lax.dot_general(images, texts, ROW_DOT, preferred_element_type=WIDE)
    scaled = scale_ref[0] * scores
    logits = scaled + bias_ref[0]
    if has_own:
        row = lax.broadcasted_iota(jnp.int32, logits.shape, 0)
        col = lax.broadcasted_iota(jnp.int32, logits.shape, 1)
        sign = jnp.where((row == col) & (row < own), 1.0, -1.0).astype(WIDE)
    else:
        sign = jnp.full(logits.shape, -1.0, WIDE)
    against = -sign * logits
    small = jnp.exp(-jnp.abs(against))
    above = jnp.where(against >= 0, 1.0, small) / (1.0 + small)
    pair_grad = -sign * above
    loss = jnp.maximum(against, 0.0) + jnp.log1p(small)
    which = lax.broadcasted_iota(jnp.int32, stats_ref.shape, 0)
    stats_ref[...] = jnp.where(
        which == 0,
        jnp.sum(loss),
        jnp.where(which == 1, jnp.sum(pair_grad * scaled), jnp.sum(pair_grad)),
    )
    grad_low = pair_grad.astype(LOW)

    def spread(value, refs):
        at = 0
        for ref in refs:
            rows = ref.shape[0]
            ref[...] = value[at : at + rows].astype(ref.dtype)
            at += rows

    spread(lax.dot_general(grad_low, images, COL_DOT, preferred_element_type=WIDE), text_outs)
    spread(jnp.dot(grad_low, texts, preferred_element_type=WIDE), image_outs)


def tile(has_own, scale, bias, images, texts, image_types, text_types, *others):
    outs = [array(v.shape, t) for v, t in zip((*images, *texts), (*image_types, *text_types))]
    outs.append(array((8, 128), WIDE))
    n_image, n_text = len(images), len(texts)
    rows_i, rows_t = sum(v.shape[0] for v in images), sum(v.shape[0] for v in texts)
    flops = 6 * rows_i * rows_t * images[0].shape[1]
    kernel = functools.partial(tile_kernel, has_own, n_image, n_text)
    got = call(kernel, outs, flops, scale, bias, *texts, *images, *others, smem=2)
    return got[:n_image], got[n_image:-1], got[-1]


def add_kernel(count, *refs):
    total = refs[0][...].astype(WIDE)
    for ref in refs[1:count]:
        total = total + ref[...].astype(WIDE)
    refs[-1][...] = total.astype(refs[-1].dtype)


def add_low(parts, *others):
    kernel = functools.partial(add_kernel, len(parts))
    return call(kernel, [array(parts[0].shape, LOW)], parts[0].size * len(parts), *parts, *others)


def add_wide(parts, *others):
    kernel = functools.partial(add_kernel, len(parts))
    return call(kernel, [array(parts[0].shape, WIDE)], parts[0].size * len(parts), *parts, *others)


def finish_kernel(count, scale_ref, feats_ref, *refs):
    feats = feats_ref[...]
    inverse = lax.rsqrt(jnp.sum(feats * feats, axis=1, keepdims=True) + EPSILON)
    unit = feats * inverse
    total = refs[0][...].astype(WIDE)
    for ref in refs[1:count]:
        total = total + ref[...].astype(WIDE)
    grad = scale_ref[0] * total
    refs[-2][...] = (grad - unit * jnp.sum(unit * grad, axis=1, keepdims=True)) * inverse
    refs[-1][...] = jnp.zeros(refs[-1].shape, WIDE)


def finish(scale, feats, parts, *others, flops=0):
    kernel = functools.partial(finish_kernel, len(parts))
    outs = [array(feats.shape, WIDE), array((8, 128), WIDE)]
    return call(kernel, outs, 10 * feats.size + flops, scale, feats, *parts, *others, smem=1)


def mean_kernel(count, batch, *refs):
    total = refs[0][...]
    for ref in refs[1:count]:
        total = total + ref[...]
    total = total / batch
    for i in range(3):
        refs[-1][i] = total[i, 0]


def mean_stats(batch, parts, *others):
    return pl.pallas_call(
        functools.partial(mean_kernel, len(parts), float(batch)),
        out_shape=array((3,), WIDE),
        in_specs=[VMEM] * (len(parts) + len(others)),
        out_specs=SMEM,
        compiler_params=PARAMS,
    )(*parts, *others)


class Ranks:
    def __init__(self, mesh):
        loop, rows = mesh.shape["loop"], mesh.shape["rows"]
        core = 2 if loop % 2 == 0 else 1
        low = 2 if rows % 2 == 0 else 1
        self.x, self.core, self.high, self.low = loop // core, core, rows // low, low

    def loop_shift(self, value, x=0, core=0):
        pairs = []
        for a in range(self.x):
            for b in range(self.core):
                to = (a + x) % self.x * self.core + (b + core) % self.core
                pairs.append((a * self.core + b, to))
        return lax.ppermute(value, "loop", pairs)

    def rows_shift(self, value, high=0, low=0):
        pairs = []
        for a in range(self.high):
            for b in range(self.low):
                to = (a + high) % self.high * self.low + (b + low) % self.low
                pairs.append((a * self.low + b, to))
        return lax.ppermute(value, "rows", pairs)


def solution(mesh):
    ranks = Ranks(mesh)
    devices = mesh.shape["loop"] * mesh.shape["rows"]

    def shards(image_feats, text_feats, log_scale, bias):
        rows_dev = image_feats.shape[0]
        scale = jnp.exp(log_scale)
        image_low = normalize(image_feats)
        text_low = normalize(text_feats, image_low)

        images = {(0, 0): image_low}
        for low in range(1, ranks.low):
            images[low, 0] = ranks.rows_shift(image_low, low=low)
        for x in range(1, ranks.x):
            images[0, x] = ranks.loop_shift(image_low, x=x)
        first = token(*images.values())
        for low in range(1, ranks.low):
            for x in range(1, ranks.x):
                images[low, x] = ranks.loop_shift(images[low, 0], x=x)
        second = token(first, *images.values())
        texts = {(0, 0): text_low}
        for high in range(1, ranks.high):
            texts[high, 0] = ranks.rows_shift(text_low, high, high)
        for high in range(ranks.high):
            for core in range(1, ranks.core):
                texts[high, core] = ranks.loop_shift(texts[high, 0], core=core)

        image_keys, text_keys = list(images), list(texts)

        def chunks(keys, arrays):
            out, rows = [[]], 0
            for key in keys:
                if rows + arrays[key].shape[0] > TILE_BLOCKS * rows_dev:
                    out.append([])
                    rows = 0
                out[-1].append(key)
                rows += arrays[key].shape[0]
            return out

        image_chunks, text_chunks = chunks(image_keys, images), chunks(text_keys, texts)
        one_tile = len(image_chunks) == 1 and len(text_chunks) == 1
        image_part, text_part, stats = {}, {}, None

        def part_type(key):
            return LOW if one_tile and key[1] != 0 else WIDE

        for i, ik in enumerate(image_chunks):
            for j, tk in enumerate(text_chunks):
                image_term, text_term, tile_stats = tile(
                    i == 0 and j == 0,
                    scale,
                    bias,
                    [images[key] for key in ik],
                    [texts[key] for key in tk],
                    [part_type(key) for key in ik],
                    [part_type(key) for key in tk],
                    second,
                )
                for key, term in zip(ik, image_term):
                    image_part[key] = image_part[key] + term if key in image_part else term
                for key, term in zip(tk, text_term):
                    text_part[key] = text_part[key] + term if key in text_part else term
                stats = tile_stats if stats is None else stats + tile_stats

        def sent(part, key):
            return part[key].astype(LOW)

        stats = [stats, *[ranks.rows_shift(stats, low=k) for k in range(1, ranks.low)]]
        text_sums, totals = [text_part[0, 0]], []
        for high in range(1, ranks.high):
            got = [ranks.loop_shift(sent(text_part, (high, c)), core=-c) for c in range(1, ranks.core)]
            totals.append(add_low([text_part[high, 0], *got], *stats[1:]))
            text_sums.append(ranks.rows_shift(totals[-1], -high, -high))
        for core in range(1, ranks.core):
            text_sums.append(ranks.loop_shift(sent(text_part, (0, core)), core=-core))
        stats = add_wide(stats, *totals)
        steps = [(x, c) for x in range(ranks.x) for c in range(ranks.core)][1:]
        stats = add_wide([stats, *[ranks.loop_shift(stats, x=x, core=c) for x, c in steps]])
        stats = [stats, *[ranks.rows_shift(stats, high=h) for h in range(1, ranks.high)]]
        image_sums = [image_part[0, 0]]
        for x in range(1, ranks.x):
            image_sums.append(ranks.loop_shift(sent(image_part, (0, x)), x=-x))
        for low in range(1, ranks.low):
            got = [ranks.loop_shift(sent(image_part, (low, x)), x=-x) for x in range(1, ranks.x)]
            total = add_low([image_part[low, 0], *got], *totals)
            image_sums.append(ranks.rows_shift(total, low=-low))
        grad_text, done = finish(scale, text_feats, text_sums, flops=FIRST)
        grad_image, done = finish(scale, image_feats, image_sums, done)
        return grad_image, grad_text, mean_stats(devices * rows_dev, stats, done)

    rows_spec = P(("groups", "loop", "rows"), None)
    return jax.shard_map(
        shards,
        mesh=mesh,
        in_specs=(rows_spec, rows_spec, P(), P()),
        out_specs=(rows_spec, rows_spec, P("groups")),
        check_vma=False,
    )
```

time: 63.4 us -> 52 us (0.82)
  waiting for transfers between devices: 34.4 us -> 20.3 us
  starting transfers between devices: 19.4 us -> 22.2 us
  other arithmetic: 0.64 us -> 0 us
    ppermute x16 -> x17, waiting for transfers between devices: 34.4 us -> 20.3 us  [the longest x6 15.5 us: rows_shift(): return lax.ppermute(value, 'rows', pairs)]
    ppermute x16 -> x17, starting transfers between devices: 19.4 us -> 22.2 us  [the longest x6 15.2 us: rows_shift(): return lax.ppermute(value, 'rows', pairs)]
    pallas_call x7 -> x11, Pallas kernels: 5.67 us -> 5.68 us  [call(): pl.pallas_call(kernel, out_shape=outs[0] if single else tuple(outs), in_s...]
  transfers between devices with their start and end apart: 16 -> 17, of which waited for: 8 -> 9; matrix products, arithmetic and copies ran while one was open for 1% -> 0% of each run, Pallas kernels for 2% -> 5%
where the time goes in v2:
time: 52 us; the launch traced here: 51.9 us
  starting transfers between devices  22.2 us (43%)
  waiting for transfers between devices  20.3 us (39%)
  Pallas kernels  6.23 us (12%)
  between operations  2.05 us (4%)
  local copies, waits for them, and re-layouts  1.07 us (2%)
    ppermute x6, waiting for transfers between devices, rows_shift(): return lax.ppermute(value, 'rows', pairs)  15.5 us
    ppermute x6, starting transfers between devices, rows_shift(): return lax.ppermute(value, 'rows', pairs)  15.2 us
    ppermute x11, starting transfers between devices, loop_shift(): return lax.ppermute(value, 'loop', pairs)  7.01 us
    pallas_call x11, Pallas kernels, call(): pl.pallas_call(kernel, out_shape=outs[0] if single else tuple(outs), in_s...  5.68 us
    ppermute x11, waiting for transfers between devices, loop_shift(): return lax.ppermute(value, 'loop', pairs)  4.79 us
    unnamed x6, local copies, waits for them, and re-layouts  1.07 us
  transfers between devices with their start and end apart: 17, of which 9 were waited for; matrix products, arithmetic and copies ran while one was open for 0% of the time, Pallas kernels for 5%

profile of v2, /device:TPU:0, one launch (start us, length us, event | category | flops | bytes accessed | tf_op | source)
XLA Modules:
  0.0 51.9 jit_solution(4003829166232793257)
XLA Ops:
  0.6 0.0 copy-start
  0.6 1.1 %copy-done = f32[128,1152]{1,0:T(8,128)S(1)} copy-done((f32[128,1152]{1,0:T(8,128)S(1)}, f32[128,1152]{1,0:T(8,128)}, u32[]{:S(2)}) %copy-start) | copy-done | bytes 589848
  1.7 0.0 copy-start.2
  1.7 0.1 shard_map.67.refs_0_.refs_1_.refs_6_
  1.8 3.1 %collective-permute-start.3 = (bf16[128,1152]{1,0:T(8,128)(2,1)S(1)}, bf16[128,1152]{1,0:T(8,128)(2,1)S(1)}, u32[]{:S(2)}, u32[]{:S(2)}) collective-permute-start(bf16[128,1152]{1,0:T(8,128)(2,1)S(1)} %shard_map.67.refs_0_.refs_1_.refs_6_), channel_id=1, source_target_pairs={{0,1},{1,0},{2,3},{3,2},{4,5},{5,4},{6,7},{7,6},{8,9},{9,8},{10,11... | collective-permute-start | bytes 884744 | tf_op jit(solution)/shard_map/ppermute | solution.py:182
  4.9 0.0 copy-done.2
  4.9 0.1 shard_map.68.refs_2_
  5.1 2.9 %collective-permute-start = (bf16[128,1152]{1,0:T(8,128)(2,1)S(1)}, bf16[128,1152]{1,0:T(8,128)(2,1)S(1)}, u32[]{:S(2)}, u32[]{:S(2)}) collective-permute-start(bf16[128,1152]{1,0:T(8,128)(2,1)S(1)} %shard_map.68.refs_2_), channel_id=1, source_target_pairs={{0,3},{1,2},{2,1},{3,0},{4,7},{5,6},{6,5},{7,4},{8,11},{9,10},{10,... | collective-permute-start | bytes 884744 | tf_op jit(solution)/shard_map/ppermute | solution.py:182
  8.0 1.5 %collective-permute-start.4 = (bf16[128,1152]{1,0:T(8,128)(2,1)S(1)}, bf16[128,1152]{1,0:T(8,128)(2,1)S(1)}, u32[]{:S(2)}, u32[]{:S(2)}) collective-permute-start(bf16[128,1152]{1,0:T(8,128)(2,1)S(1)} %shard_map.67.refs_0_.refs_1_.refs_6_), channel_id=1, source_target_pairs={{0,8},{4,12},{8,0},{12,4},{1,9},{5,13},{9,1},{13,5},{2,10},{6,14},... | collective-permute-start | bytes 884744 | tf_op jit(solution)/shard_map/ppermute | solution.py:174
  9.5 2.8 %collective-permute-done.3.refs_1_.refs_2_.refs_7_ = bf16[128,1152]{1,0:T(8,128)(2,1)S(1)} collective-permute-done((bf16[128,1152]{1,0:T(8,128)(2,1)S(1)}, bf16[128,1152]{1,0:T(8,128)(2,1)S(1)}, u32[]{:S(2)}, u32[]{:S(2)}) %collective-permute-start.3) | collective-permute-done | bytes 294944 | tf_op jit(solution)/shard_map/ppermute | solution.py:182
  12.3 1.5 %collective-permute-start.5 = (bf16[128,1152]{1,0:T(8,128)(2,1)S(1)}, bf16[128,1152]{1,0:T(8,128)(2,1)S(1)}, u32[]{:S(2)}, u32[]{:S(2)}) collective-permute-start(bf16[128,1152]{1,0:T(8,128)(2,1)S(1)} %collective-permute-done.3.refs_1_.refs_2_.refs_7_), channel_id=1, source_target_pairs={{0,8},{4,12},{8,0},{12,4},{1,9},{5,13},{9,1},{13,5},{2,10},{6,14},... | collective-permute-start | bytes 884744 | tf_op jit(solution)/shard_map/ppermute | solution.py:174
  13.8 0.0 collective-permute-start.1
  13.8 6.7 %collective-permute-done.refs_3_ = bf16[128,1152]{1,0:T(8,128)(2,1)S(1)} collective-permute-done((bf16[128,1152]{1,0:T(8,128)(2,1)S(1)}, bf16[128,1152]{1,0:T(8,128)(2,1)S(1)}, u32[]{:S(2)}, u32[]{:S(2)}) %collective-permute-start) | collective-permute-done | bytes 294944 | tf_op jit(solution)/shard_map/ppermute | solution.py:182
  20.5 0.0 collective-permute-start.2
  21.9 0.0 collective-permute-done.4.refs_2_.refs_3_.refs_8_
  21.9 0.9 %collective-permute-done.5.refs_4_.refs_9_ = bf16[128,1152]{1,0:T(8,128)(2,1)S(1)} collective-permute-done((bf16[128,1152]{1,0:T(8,128)(2,1)S(1)}, bf16[128,1152]{1,0:T(8,128)(2,1)S(1)}, u32[]{:S(2)}, u32[]{:S(2)}) %collective-permute-start.5) | collective-permute-done | bytes 294944 | tf_op jit(solution)/shard_map/ppermute | solution.py:174
  22.8 0.0 collective-permute-done.1.refs_4_
  22.8 0.0 collective-permute-done.2.refs_5_
  22.8 3.0 %shard_map.71 = (f32[128,1152]{1,0:T(8,128)S(1)}, f32[128,1152]{1,0:T(8,128)S(1)}, bf16[128,1152]{1,0:T(8,128)(2,1)S(1)}, bf16[128,1152]{1,0:T(8,128)(2,1)S(1)},...) custom-call(f32[1]{0:T(128)S(6)} %exp.3.refs_0_.scale_ref, ...), custom_call_target="tpu_custom_call" | custom-call | flops 1811939328 | bytes 5906440 | tf_op jit(solution)/shard_map/pallas_call | solution.py:28
  25.9 0.1 collective-permute-start.8
  25.9 1.6 %collective-permute-start.7 = (bf16[128,1152]{1,0:T(8,128)(2,1)S(1)}, bf16[128,1152]{1,0:T(8,128)(2,1)S(1)}, u32[]{:S(2)}, u32[]{:S(2)}) collective-permute-start(bf16[128,1152]{1,0:T(8,128)(2,1)S(1)} %get-tuple-element.19), channel_id=1, source_target_pairs={{0,8},{4,12},{8,0},{12,4},{1,9},{5,13},{9,1},{13,5},{2,10},{6,14},... | collective-permute-start | bytes 884744 | tf_op jit(solution)/shard_map/ppermute | solution.py:174
  27.5 0.4 collective-permute-start.9
  27.9 0.0 collective-permute-start.12
  27.9 3.2 %collective-permute-done.9.refs_2_.refs_1_ = f32[8,128]{1,0:T(8,128)S(1)} collective-permute-done((f32[8,128]{1,0:T(8,128)S(1)}, f32[8,128]{1,0:T(8,128)S(1)}, u32[]{:S(2)}, u32[]{:S(2)}) %collective-permute-start.9) | collective-permute-done | bytes 4128 | tf_op jit(solution)/shard_map/ppermute | solution.py:182
  31.1 0.0 collective-permute-done.8.refs_1_
  31.1 0.1 shard_map.72.refs_2_
  31.2 6.0 %collective-permute-start.11 = (bf16[128,1152]{1,0:T(8,128)(2,1)S(1)}, bf16[128,1152]{1,0:T(8,128)(2,1)S(1)}, u32[]{:S(2)}, u32[]{:S(2)}) collective-permute-start(bf16[128,1152]{1,0:T(8,128)(2,1)S(1)} %shard_map.72.refs_2_), channel_id=1, source_target_pairs={{0,3},{1,2},{2,1},{3,0},{4,7},{5,6},{6,5},{7,4},{8,11},{9,10},{10,... | collective-permute-start | bytes 884744 | tf_op jit(solution)/shard_map/ppermute | solution.py:182
  37.2 0.0 collective-permute-start.15
  37.2 0.7 %collective-permute-start.14 = (f32[8,128]{1,0:T(8,128)S(1)}, f32[8,128]{1,0:T(8,128)S(1)}, u32[]{:S(2)}, u32[]{:S(2)}) collective-permute-start(f32[8,128]{1,0:T(8,128)S(1)} %shard_map.76.refs_0_), channel_id=1, source_target_pairs={{0,8},{4,12},{8,0},{12,4},{1,9},{5,13},{9,1},{13,5},{2,10},{6,14},... | collective-permute-start | bytes 12296 | tf_op jit(solution)/shard_map/ppermute | solution.py:174
  37.9 0.0 collective-permute-done.7.refs_1_
  37.9 1.2 %collective-permute-start.13 = (f32[8,128]{1,0:T(8,128)S(1)}, f32[8,128]{1,0:T(8,128)S(1)}, u32[]{:S(2)}, u32[]{:S(2)}) collective-permute-start(f32[8,128]{1,0:T(8,128)S(1)} %shard_map.76.refs_0_), channel_id=1, source_target_pairs={{0,4},{4,0},{8,12},{12,8},{1,5},{5,1},{9,13},{13,9},{2,6},{6,2},{1... | collective-permute-start | bytes 12296 | tf_op jit(solution)/shard_map/ppermute | solution.py:174
  39.1 0.1 shard_map.73
  39.1 1.1 %collective-permute-done.15.refs_3_ = f32[8,128]{1,0:T(8,128)S(1)} collective-permute-done((f32[8,128]{1,0:T(8,128)S(1)}, f32[8,128]{1,0:T(8,128)S(1)}, u32[]{:S(2)}, u32[]{:S(2)}) %collective-permute-start.15) | collective-permute-done | bytes 4128 | tf_op jit(solution)/shard_map/ppermute | solution.py:174
  40.2 0.5 %collective-permute-start.6 = (bf16[128,1152]{1,0:T(8,128)(2,1)S(1)}, bf16[128,1152]{1,0:T(8,128)(2,1)S(1)}, u32[]{:S(2)}, u32[]{:S(2)}) collective-permute-start(bf16[128,1152]{1,0:T(8,128)(2,1)S(1)} %get-tuple-element.17), channel_id=1, source_target_pairs={{0,8},{4,12},{8,0},{12,4},{1,9},{5,13},{9,1},{13,5},{2,10},{6,14},... | collective-permute-start | bytes 884744 | tf_op jit(solution)/shard_map/ppermute | solution.py:174
  40.8 0.1 collective-permute-done.14.refs_2_
  40.8 0.0 collective-permute-start.10
  40.8 0.0 collective-permute-done.13.refs_1_
  40.8 2.8 %collective-permute-start.16 = (f32[8,128]{1,0:T(8,128)S(1)}, f32[8,128]{1,0:T(8,128)S(1)}, u32[]{:S(2)}, u32[]{:S(2)}) collective-permute-start(f32[8,128]{1,0:T(8,128)S(1)} %shard_map.77.refs_0_), channel_id=1, source_target_pairs={{0,2},{1,3},{2,0},{3,1},{4,6},{5,7},{6,4},{7,5},{8,10},{9,11},{10,... | collective-permute-start | bytes 12296 | tf_op jit(solution)/shard_map/ppermute | solution.py:182
  43.7 0.0 collective-permute-done.12.refs_2_
  43.7 1.0 %collective-permute-done.11.refs_1_ = bf16[128,1152]{1,0:T(8,128)(2,1)S(1)} collective-permute-done((bf16[128,1152]{1,0:T(8,128)(2,1)S(1)}, bf16[128,1152]{1,0:T(8,128)(2,1)S(1)}, u32[]{:S(2)}, u32[]{:S(2)}) %collective-permute-start.11) | collective-permute-done | bytes 294944 | tf_op jit(solution)/shard_map/ppermute | solution.py:182
  44.7 0.0 copy-start.1
  44.7 1.1 %shard_map.74 = (f32[128,1152]{1,0:T(8,128)}, f32[8,128]{1,0:T(8,128)S(1)}) custom-call(f32[1]{0:T(128)S(6)} %exp.3.refs_0_.scale_ref, f32[128,1152]{1,0:T(8,128)S(1)} %copy-done.2, f32[128,1152]{1,0:T(8,128)S(1)} %get-tuple-element.23.refs_0_, bf16[128,1152]{1,0:T(8,128)(2,1)S(1)} %collective-permute-done.11.refs_1_, ...), custom_call_target="tpu_custom_call" | custom-call | flops 4001474560 | bytes 2363396 | tf_op jit(solution)/shard_map/pallas_call | solution.py:28
  45.8 2.7 %collective-permute-done.6.refs_1_ = bf16[128,1152]{1,0:T(8,128)(2,1)S(1)} collective-permute-done((bf16[128,1152]{1,0:T(8,128)(2,1)S(1)}, bf16[128,1152]{1,0:T(8,128)(2,1)S(1)}, u32[]{:S(2)}, u32[]{:S(2)}) %collective-permute-start.6) | collective-permute-done | bytes 294944 | tf_op jit(solution)/shard_map/ppermute | solution.py:174
  48.5 1.7 %collective-permute-done.10.refs_2_ = bf16[128,1152]{1,0:T(8,128)(2,1)S(1)} collective-permute-done((bf16[128,1152]{1,0:T(8,128)(2,1)S(1)}, bf16[128,1152]{1,0:T(8,128)(2,1)S(1)}, u32[]{:S(2)}, u32[]{:S(2)}) %collective-permute-start.10) | collective-permute-done | bytes 294944 | tf_op jit(solution)/shard_map/ppermute | solution.py:182
  50.2 0.0 copy-done.1
  50.2 1.1 %shard_map.75 = (f32[128,1152]{1,0:T(8,128)}, f32[8,128]{1,0:T(8,128)S(1)}) custom-call(f32[1]{0:T(128)S(6)} %exp.3.refs_0_.scale_ref, f32[128,1152]{1,0:T(8,128)S(1)} %copy-done.1, f32[128,1152]{1,0:T(8,128)S(1)} %get-tuple-element.16.refs_0_, bf16[128,1152]{1,0:T(8,128)(2,1)S(1)} %collective-permute-done.6.refs_1_, ...), custom_call_target="tpu_custom_call" | custom-call | flops 1474560 | bytes 2367492 | tf_op jit(solution)/shard_map/pallas_call | solution.py:28
  51.3 0.0 collective-permute-done.16.refs_1_
  51.3 0.6 %shard_map.78 = f32[3]{0:T(128)} custom-call(f32[8,128]{1,0:T(8,128)S(1)} %shard_map.77.refs_0_, f32[8,128]{1,0:T(8,128)S(1)} %collective-permute-done.16.refs_1_, f32[8,128]{1,0:T(8,128)S(1)} %get-tuple-element.28.refs_2_), custom_call_target="tpu_custom_call" | custom-call | tf_op jit(solution)/shard_map/pallas_call | solution.py:152
  (4 shorter events, 0.0 us)
Async XLA Ops:
  0.6 1.1 %copy-start = (f32[128,1152]{1,0:T(8,128)S(1)}, f32[128,1152]{1,0:T(8,128)}, u32[]{:S(2)}) copy-start(f32[128,1152]{1,0:T(8,128)} %feats_ref.7) | copy-start | bytes 1769476
  1.7 3.2 %copy-start.2 = (f32[128,1152]{1,0:T(8,128)S(1)}, f32[128,1152]{1,0:T(8,128)}, u32[]{:S(2)}) copy-start(f32[128,1152]{1,0:T(8,128)} %feats_ref.6) | copy-start | bytes 1769476
  1.8 10.5 %collective-permute-start.3 = (bf16[128,1152]{1,0:T(8,128)(2,1)S(1)}, bf16[128,1152]{1,0:T(8,128)(2,1)S(1)}, u32[]{:S(2)}, u32[]{:S(2)}) collective-permute-start(bf16[128,1152]{1,0:T(8,128)(2,1)S(1)} %shard_map.67.refs_0_.refs_1_.refs_6_), channel_id=1, source_target_pairs={{0,1},{1,0},{2,3},{3,2},{4,5},{5,4},{6,7},{7,6},{8,9},{9,8},{10,11... | collective-permute-start | bytes 884744 | tf_op jit(solution)/shard_map/ppermute | solution.py:182
  5.1 15.5 %collective-permute-start = (bf16[128,1152]{1,0:T(8,128)(2,1)S(1)}, bf16[128,1152]{1,0:T(8,128)(2,1)S(1)}, u32[]{:S(2)}, u32[]{:S(2)}) collective-permute-start(bf16[128,1152]{1,0:T(8,128)(2,1)S(1)} %shard_map.68.refs_2_), channel_id=1, source_target_pairs={{0,3},{1,2},{2,1},{3,0},{4,7},{5,6},{6,5},{7,4},{8,11},{9,10},{10,... | collective-permute-start | bytes 884744 | tf_op jit(solution)/shard_map/ppermute | solution.py:182
  8.0 13.9 %collective-permute-start.4 = (bf16[128,1152]{1,0:T(8,128)(2,1)S(1)}, bf16[128,1152]{1,0:T(8,128)(2,1)S(1)}, u32[]{:S(2)}, u32[]{:S(2)}) collective-permute-start(bf16[128,1152]{1,0:T(8,128)(2,1)S(1)} %shard_map.67.refs_0_.refs_1_.refs_6_), channel_id=1, source_target_pairs={{0,8},{4,12},{8,0},{12,4},{1,9},{5,13},{9,1},{13,5},{2,10},{6,14},... | collective-permute-start | bytes 884744 | tf_op jit(solution)/shard_map/ppermute | solution.py:174
  12.3 10.5 %collective-permute-start.5 = (bf16[128,1152]{1,0:T(8,128)(2,1)S(1)}, bf16[128,1152]{1,0:T(8,128)(2,1)S(1)}, u32[]{:S(2)}, u32[]{:S(2)}) collective-permute-start(bf16[128,1152]{1,0:T(8,128)(2,1)S(1)} %collective-permute-done.3.refs_1_.refs_2_.refs_7_), channel_id=1, source_target_pairs={{0,8},{4,12},{8,0},{12,4},{1,9},{5,13},{9,1},{13,5},{2,10},{6,14},... | collective-permute-start | bytes 884744 | tf_op jit(solution)/shard_map/ppermute | solution.py:174
  13.8 9.0 %collective-permute-start.1 = (bf16[128,1152]{1,0:T(8,128)(2,1)S(1)}, bf16[128,1152]{1,0:T(8,128)(2,1)S(1)}, u32[]{:S(2)}, u32[]{:S(2)}) collective-permute-start(bf16[128,1152]{1,0:T(8,128)(2,1)S(1)} %shard_map.68.refs_2_), channel_id=1, source_target_pairs={{0,4},{4,0},{8,12},{12,8},{1,5},{5,1},{9,13},{13,9},{2,6},{6,2},{1... | collective-permute-start | bytes 884744 | tf_op jit(solution)/shard_map/ppermute | solution.py:174
  20.5 2.3 %collective-permute-start.2 = (bf16[128,1152]{1,0:T(8,128)(2,1)S(1)}, bf16[128,1152]{1,0:T(8,128)(2,1)S(1)}, u32[]{:S(2)}, u32[]{:S(2)}) collective-permute-start(bf16[128,1152]{1,0:T(8,128)(2,1)S(1)} %collective-permute-done.refs_3_), channel_id=1, source_target_pairs={{0,4},{4,0},{8,12},{12,8},{1,5},{5,1},{9,13},{13,9},{2,6},{6,2},{1... | collective-permute-start | bytes 884744 | tf_op jit(solution)/shard_map/ppermute | solution.py:174
  25.9 5.2 %collective-permute-start.8 = (bf16[128,1152]{1,0:T(8,128)(2,1)S(1)}, bf16[128,1152]{1,0:T(8,128)(2,1)S(1)}, u32[]{:S(2)}, u32[]{:S(2)}) collective-permute-start(bf16[128,1152]{1,0:T(8,128)(2,1)S(1)} %get-tuple-element.21), channel_id=1, source_target_pairs={{0,4},{4,0},{8,12},{12,8},{1,5},{5,1},{9,13},{13,9},{2,6},{6,2},{1... | collective-permute-start | bytes 884744 | tf_op jit(solution)/shard_map/ppermute | solution.py:174
  25.9 11.9 %collective-permute-start.7 = (bf16[128,1152]{1,0:T(8,128)(2,1)S(1)}, bf16[128,1152]{1,0:T(8,128)(2,1)S(1)}, u32[]{:S(2)}, u32[]{:S(2)}) collective-permute-start(bf16[128,1152]{1,0:T(8,128)(2,1)S(1)} %get-tuple-element.19), channel_id=1, source_target_pairs={{0,8},{4,12},{8,0},{12,4},{1,9},{5,13},{9,1},{13,5},{2,10},{6,14},... | collective-permute-start | bytes 884744 | tf_op jit(solution)/shard_map/ppermute | solution.py:174
  27.5 3.6 %collective-permute-start.9 = (f32[8,128]{1,0:T(8,128)S(1)}, f32[8,128]{1,0:T(8,128)S(1)}, u32[]{:S(2)}, u32[]{:S(2)}) collective-permute-start(f32[8,128]{1,0:T(8,128)S(1)} %get-tuple-element.22.refs_0_), channel_id=1, source_target_pairs={{0,1},{1,0},{2,3},{3,2},{4,5},{5,4},{6,7},{7,6},{8,9},{9,8},{10,11... | collective-permute-start | bytes 12296 | tf_op jit(solution)/shard_map/ppermute | solution.py:182
  27.9 15.8 %collective-permute-start.12 = (bf16[128,1152]{1,0:T(8,128)(2,1)S(1)}, bf16[128,1152]{1,0:T(8,128)(2,1)S(1)}, u32[]{:S(2)}, u32[]{:S(2)}) collective-permute-start(bf16[128,1152]{1,0:T(8,128)(2,1)S(1)} %get-tuple-element.24), channel_id=1, source_target_pairs={{0,4},{4,0},{8,12},{12,8},{1,5},{5,1},{9,13},{13,9},{2,6},{6,2},{1... | collective-permute-start | bytes 884744 | tf_op jit(solution)/shard_map/ppermute | solution.py:174
  31.2 13.5 %collective-permute-start.11 = (bf16[128,1152]{1,0:T(8,128)(2,1)S(1)}, bf16[128,1152]{1,0:T(8,128)(2,1)S(1)}, u32[]{:S(2)}, u32[]{:S(2)}) collective-permute-start(bf16[128,1152]{1,0:T(8,128)(2,1)S(1)} %shard_map.72.refs_2_), channel_id=1, source_target_pairs={{0,3},{1,2},{2,1},{3,0},{4,7},{5,6},{6,5},{7,4},{8,11},{9,10},{10,... | collective-permute-start | bytes 884744 | tf_op jit(solution)/shard_map/ppermute | solution.py:182
  37.2 3.0 %collective-permute-start.15 = (f32[8,128]{1,0:T(8,128)S(1)}, f32[8,128]{1,0:T(8,128)S(1)}, u32[]{:S(2)}, u32[]{:S(2)}) collective-permute-start(f32[8,128]{1,0:T(8,128)S(1)} %shard_map.76.refs_0_), channel_id=1, source_target_pairs={{0,12},{4,8},{8,4},{12,0},{1,13},{5,9},{9,5},{13,1},{2,14},{6,10},... | collective-permute-start | bytes 12296 | tf_op jit(solution)/shard_map/ppermute | solution.py:174
  37.2 3.6 %collective-permute-start.14 = (f32[8,128]{1,0:T(8,128)S(1)}, f32[8,128]{1,0:T(8,128)S(1)}, u32[]{:S(2)}, u32[]{:S(2)}) collective-permute-start(f32[8,128]{1,0:T(8,128)S(1)} %shard_map.76.refs_0_), channel_id=1, source_target_pairs={{0,8},{4,12},{8,0},{12,4},{1,9},{5,13},{9,1},{13,5},{2,10},{6,14},... | collective-permute-start | bytes 12296 | tf_op jit(solution)/shard_map/ppermute | solution.py:174
  37.9 3.0 %collective-permute-start.13 = (f32[8,128]{1,0:T(8,128)S(1)}, f32[8,128]{1,0:T(8,128)S(1)}, u32[]{:S(2)}, u32[]{:S(2)}) collective-permute-start(f32[8,128]{1,0:T(8,128)S(1)} %shard_map.76.refs_0_), channel_id=1, source_target_pairs={{0,4},{4,0},{8,12},{12,8},{1,5},{5,1},{9,13},{13,9},{2,6},{6,2},{1... | collective-permute-start | bytes 12296 | tf_op jit(solution)/shard_map/ppermute | solution.py:174
  40.2 8.2 %collective-permute-start.6 = (bf16[128,1152]{1,0:T(8,128)(2,1)S(1)}, bf16[128,1152]{1,0:T(8,128)(2,1)S(1)}, u32[]{:S(2)}, u32[]{:S(2)}) collective-permute-start(bf16[128,1152]{1,0:T(8,128)(2,1)S(1)} %get-tuple-element.17), channel_id=1, source_target_pairs={{0,8},{4,12},{8,0},{12,4},{1,9},{5,13},{9,1},{13,5},{2,10},{6,14},... | collective-permute-start | bytes 884744 | tf_op jit(solution)/shard_map/ppermute | solution.py:174
  40.8 9.3 %collective-permute-start.10 = (bf16[128,1152]{1,0:T(8,128)(2,1)S(1)}, bf16[128,1152]{1,0:T(8,128)(2,1)S(1)}, u32[]{:S(2)}, u32[]{:S(2)}) collective-permute-start(bf16[128,1152]{1,0:T(8,128)(2,1)S(1)} %shard_map.73), channel_id=1, source_target_pairs={{0,1},{1,0},{2,3},{3,2},{4,5},{5,4},{6,7},{7,6},{8,9},{9,8},{10,11... | collective-permute-start | bytes 884744 | tf_op jit(solution)/shard_map/ppermute | solution.py:182
  40.8 10.5 %collective-permute-start.16 = (f32[8,128]{1,0:T(8,128)S(1)}, f32[8,128]{1,0:T(8,128)S(1)}, u32[]{:S(2)}, u32[]{:S(2)}) collective-permute-start(f32[8,128]{1,0:T(8,128)S(1)} %shard_map.77.refs_0_), channel_id=1, source_target_pairs={{0,2},{1,3},{2,0},{3,1},{4,6},{5,7},{6,4},{7,5},{8,10},{9,11},{10,... | collective-permute-start | bytes 12296 | tf_op jit(solution)/shard_map/ppermute | solution.py:182
  44.7 5.5 %copy-start.1 = (f32[128,1152]{1,0:T(8,128)S(1)}, f32[128,1152]{1,0:T(8,128)}, u32[]{:S(2)}) copy-start(f32[128,1152]{1,0:T(8,128)} %feats_ref.7) | copy-start | bytes 1769476

commit v3 on v2

v3 whole, which is shorter than its diff:
```python
import functools

import jax
import jax.numpy as jnp
from jax import lax
from jax.experimental import pallas as pl
from jax.experimental.pallas import tpu as pltpu
from jax.sharding import PartitionSpec as P

EPSILON = 1e-06
IMAGE_TILE, TEXT_TILE = 8, 2
FIRST = 10**9
AHEAD = 12 * 10**9
VMEM = pl.BlockSpec(memory_space=pltpu.VMEM)
SMEM = pl.BlockSpec(memory_space=pltpu.SMEM)
PARAMS = pltpu.CompilerParams(vmem_limit_bytes=24 * 1024 * 1024)
ROW_DOT = (((1,), (1,)), ((), ()))
COL_DOT = (((0,), (0,)), ((), ()))
LOW, WIDE = jnp.bfloat16, jnp.float32


def array(shape, dtype):
    return jax.ShapeDtypeStruct(shape, dtype)


def call(kernel, outs, flops, *args, smem=0):
    nbytes = sum(a.size * a.dtype.itemsize for a in (*args, *outs))
    single = len(outs) == 1
    return pl.pallas_call(
        kernel,
        out_shape=outs[0] if single else tuple(outs),
        in_specs=[SMEM] * smem + [VMEM] * (len(args) - smem),
        out_specs=VMEM if single else tuple([VMEM] * len(outs)),
        compiler_params=PARAMS,
        cost_estimate=pl.CostEstimate(flops=flops, bytes_accessed=nbytes, transcendentals=0),
    )(*args)


def normalize_kernel(feats_ref, *refs):
    feats = feats_ref[...]
    inverse = lax.rsqrt(jnp.sum(feats * feats, axis=1, keepdims=True) + EPSILON)
    refs[-1][...] = (feats * inverse).astype(LOW)


def normalize(feats, *others):
    return call(normalize_kernel, [array(feats.shape, LOW)], 4 * feats.size, feats, *others)


def token_kernel(*refs):
    refs[-1][...] = jnp.zeros(refs[-1].shape, WIDE)


def token(*others, flops=0):
    return call(token_kernel, [array((8, 128), WIDE)], 1024 + flops, *others)


def joined(refs):
    return jnp.concatenate([r[...] for r in refs], axis=0)


def spread(value, refs):
    at = 0
    for ref in refs:
        rows = ref.shape[0]
        ref[...] = value[at : at + rows].astype(ref.dtype)
        at += rows


def score_kernel(own, n_image, n_text, *refs):
    scale_ref, bias_ref = refs[:2]
    texts = joined(refs[2 : 2 + n_text])
    images = joined(refs[2 + n_text : 2 + n_text + n_image])
    grad_ref, stats_ref = refs[-2:]
    scores = lax.dot_general(images, texts, ROW_DOT, preferred_element_type=WIDE)
    scaled = scale_ref[0] * scores
    logits = scaled + bias_ref[0]
    if own:
        row = lax.broadcasted_iota(jnp.int32, logits.shape, 0)
        col = lax.broadcasted_iota(jnp.int32, logits.shape, 1)
        sign = jnp.where((row == col) & (row < own), 1.0, -1.0).astype(WIDE)
    else:
        sign = jnp.full(logits.shape, -1.0, WIDE)
    against = -sign * logits
    small = jnp.exp(-jnp.abs(against))
    above = jnp.where(against >= 0, 1.0, small) / (1.0 + small)
    pair_grad = -sign * above
    loss = jnp.maximum(against, 0.0) + jnp.log1p(small)
    which = lax.broadcasted_iota(jnp.int32, stats_ref.shape, 0)
    stats_ref[...] = jnp.where(
        which == 0,
        jnp.sum(loss),
        jnp.where(which == 1, jnp.sum(pair_grad * scaled), jnp.sum(pair_grad)),
    )
    grad_ref[...] = pair_grad.astype(LOW)


def score_tile(own, scale, bias, images, texts, *others):
    rows_i, rows_t = sum(v.shape[0] for v in images), sum(v.shape[0] for v in texts)
    outs = [array((rows_i, rows_t), LOW), array((8, 128), WIDE)]
    kernel = functools.partial(score_kernel, own, len(images), len(texts))
    flops = 2 * rows_i * rows_t * images[0].shape[1]
    return call(kernel, outs, flops, scale, bias, *texts, *images, *others, smem=2)


def image_kernel(at, rows, n_text, n_out, grad_ref, *refs):
    texts = joined(refs[:n_text])
    spread(jnp.dot(grad_ref[at : at + rows], texts, preferred_element_type=WIDE), refs[-n_out:])


def image_tile(at, pair_grad, texts, outs, *others):
    rows = sum(out.shape[0] for out in outs)
    kernel = functools.partial(image_kernel, at, rows, len(texts), len(outs))
    flops = 2 * rows * pair_grad.shape[1] * texts[0].shape[1]
    got = call(kernel, outs, flops, pair_grad, *texts, *others)
    return list(got) if len(outs) > 1 else [got]


def text_kernel(n_image, n_out, grad_ref, *refs):
    images = joined(refs[:n_image])
    text_grad = lax.dot_general(grad_ref[...], images, COL_DOT, preferred_element_type=WIDE)
    spread(text_grad, refs[-n_out:])


def text_tile(pair_grad, images, outs, *others):
    kernel = functools.partial(text_kernel, len(images), len(outs))
    flops = 2 * pair_grad.size * images[0].shape[1]
    got = call(kernel, outs, flops, pair_grad, *images, *others)
    return list(got) if len(outs) > 1 else [got]


def added_up(parts):
    return add(parts[0].shape, WIDE, [(v, 0) for v in parts])


def block(ref, at, rows):
    return ref[...] if ref.shape[0] == rows else ref[at : at + rows]


def add_kernel(places, *refs):
    rows = refs[-1].shape[0]
    total = block(refs[0], places[0], rows).astype(WIDE)
    for ref, at in zip(refs[1:], places[1:]):
        total = total + block(ref, at, rows).astype(WIDE)
    refs[-1][...] = total.astype(refs[-1].dtype)


def add(shape, dtype, parts, *others):
    kernel = functools.partial(add_kernel, [at for _, at in parts])
    flops = len(parts) * shape[0] * shape[1]
    return call(kernel, [array(shape, dtype)], flops, *(v for v, _ in parts), *others)


def finish_kernel(places, scale_ref, feats_ref, *refs):
    feats = feats_ref[...]
    rows = feats.shape[0]
    inverse = lax.rsqrt(jnp.sum(feats * feats, axis=1, keepdims=True) + EPSILON)
    unit = feats * inverse
    total = block(refs[0], places[0], rows).astype(WIDE)
    for ref, at in zip(refs[1:], places[1:]):
        total = total + block(ref, at, rows).astype(WIDE)
    grad = scale_ref[0] * total
    refs[-2][...] = (grad - unit * jnp.sum(unit * grad, axis=1, keepdims=True)) * inverse
    refs[-1][...] = jnp.zeros(refs[-1].shape, WIDE)


def finish(scale, feats, parts, *others, flops=0):
    kernel = functools.partial(finish_kernel, [at for _, at in parts])
    outs = [array(feats.shape, WIDE), array((8, 128), WIDE)]
    args = [v for v, _ in parts]
    return call(kernel, outs, 10 * feats.size + flops, scale, feats, *args, *others, smem=1)


def mean_kernel(count, batch, *refs):
    total = refs[0][...]
    for ref in refs[1:count]:
        total = total + ref[...]
    total = total / batch
    for i in range(3):
        refs[-1][i] = total[i, 0]


def mean_stats(batch, parts, *others):
    return pl.pallas_call(
        functools.partial(mean_kernel, len(parts), float(batch)),
        out_shape=array((3,), WIDE),
        in_specs=[VMEM] * (len(parts) + len(others)),
        out_specs=SMEM,
        compiler_params=PARAMS,
    )(*parts, *others)


class Ranks:
    def __init__(self, mesh):
        loop, rows = mesh.shape["loop"], mesh.shape["rows"]
        core = 2 if loop % 2 == 0 else 1
        low = 2 if rows % 2 == 0 else 1
        self.x, self.core, self.high, self.low = loop // core, core, rows // low, low

    def loop_shift(self, value, x=0, core=0):
        pairs = []
        for a in range(self.x):
            for b in range(self.core):
                to = (a + x) % self.x * self.core + (b + core) % self.core
                pairs.append((a * self.core + b, to))
        return lax.ppermute(value, "loop", pairs)

    def rows_shift(self, value, high=0, low=0, keep=lambda distance: True):
        pairs = []
        for a in range(self.high):
            for b in range(self.low):
                to = (a + high) % self.high * self.low + (b + low) % self.low
                if keep(abs(a * self.low + b - to)):
                    pairs.append((a * self.low + b, to))
        return lax.ppermute(value, "rows", pairs)


def near(distance):
    return distance <= 1


def far(distance):
    return distance > 1


def solution(mesh):
    ranks = Ranks(mesh)
    devices = mesh.shape["loop"] * mesh.shape["rows"]

    def shards(image_feats, text_feats, log_scale, bias):
        rows_dev = image_feats.shape[0]
        scale = jnp.exp(log_scale)
        text_low = normalize(text_feats)
        image_low = normalize(image_feats, text_low)

        texts, halves = {0: text_low}, {}
        for high in range(1, ranks.high):
            halves[high] = [ranks.rows_shift(text_low, high, high, keep) for keep in (near, far)]
        order = token(*(h[0] for h in halves.values()))
        images = {(0, 0, 0): image_low}
        for low in range(1, ranks.low):
            images[low, 0, 0] = ranks.rows_shift(image_low, low=low)
        for low in range(ranks.low):
            for x in range(1, ranks.x):
                images[low, x, 0] = ranks.loop_shift(images[low, 0, 0], x=x)
        order = token(*(images[low, 0, 0] for low in range(ranks.low)), order)
        order = token(*(images[0, x, 0] for x in range(ranks.x)), order)
        for high, got in halves.items():
            texts[high] = add(text_low.shape, LOW, [(v, 0) for v in got], order)
        arrived = token(*texts.values(), order, flops=AHEAD)
        for low in range(ranks.low):
            for x in range(ranks.x):
                if low and x:
                    images[low, x, 0] = add(image_low.shape, LOW, [(images[low, x, 0], 0)], arrived)
                for core in range(1, ranks.core):
                    images[low, x, core] = ranks.loop_shift(images[low, x, 0], core=core)

        groups = [[(low, x, 0)] for low in range(ranks.low) for x in range(ranks.x)]
        for core in range(1, ranks.core):
            groups += [[(low, x, core) for x in range(ranks.x)] for low in range(ranks.low)]
        blocks = sum(len(g) for g in groups)
        if blocks > IMAGE_TILE or len(texts) > TEXT_TILE:
            groups = [[key] for g in groups for key in g]
        one_tile = blocks <= IMAGE_TILE and len(texts) <= TEXT_TILE
        per_tile = len(groups) if one_tile else IMAGE_TILE
        parts, text_parts, tiles, stats = {}, {}, [], None

        def added(store, key, value):
            store[key] = store[key] + value if key in store else value

        for i in range(0, len(groups), per_tile):
            some = groups[i : i + per_tile]
            held = [images[key] for g in some for key in g]
            outs = [
                array((len(g) * rows_dev, image_low.shape[1]), LOW if one_tile and g[0][2] else WIDE) for g in some
            ]
            for j in range(0, len(texts), TEXT_TILE):
                keys = list(texts)[j : j + TEXT_TILE]
                own = rows_dev if i == 0 and j == 0 else 0
                pair = [texts[k] for k in keys]
                pair_grad, tile_stats = score_tile(own, scale, bias, held, pair, arrived)
                tiles.append((keys, pair_grad, held, some, outs))
                stats = tile_stats if stats is None else stats + tile_stats

        def image_grads(wanted, *others):
            for keys, pair_grad, _, some, outs in tiles:
                chosen = [i for i, g in enumerate(some) if bool(g[0][2]) == wanted]
                if chosen:
                    at = sum(len(g) for g in some[: chosen[0]]) * rows_dev
                    got = image_tile(at, pair_grad, [texts[k] for k in keys], [outs[i] for i in chosen], *others)
                    for i, value in zip(chosen, got):
                        added(parts, tuple(some[i]), value)

        image_grads(True)
        for keys, pair_grad, held, _, _ in tiles:
            text_outs = [array(text_low.shape, LOW if one_tile and k else WIDE) for k in keys]
            for k, value in zip(keys, text_tile(pair_grad, held, text_outs)):
                added(text_parts, k, value)
        image_grads(False)
        stats = added_up([stats, *[ranks.loop_shift(stats, core=c) for c in range(1, ranks.core)]])
        stats = added_up([stats, *[ranks.loop_shift(stats, x=x) for x in range(1, ranks.x)]])
        for core in range(1, ranks.core):
            for low in reversed(range(ranks.low)):
                keys = [(low, x, core) for x in range(ranks.x)]
                if tuple(keys) not in parts:
                    parts[tuple(keys)] = jnp.concatenate([parts[(key,)].astype(LOW) for key in keys], axis=0)
        back = {
            (low, core): ranks.loop_shift(parts[tuple((low, x, core) for x in range(ranks.x))], core=-core)
            for low in reversed(range(ranks.low))
            for core in range(1, ranks.core)
        }

        def here(low, x):
            return [(parts[((low, x, 0),)], 0)] + [(back[low, c], x * rows_dev) for c in range(1, ranks.core)]

        shape = image_low.shape
        image_sums = here(0, 0)
        for low in range(1, ranks.low):
            got = [(ranks.loop_shift(add(shape, LOW, here(low, x)), x=-x), 0) for x in range(1, ranks.x)]
            image_sums.append((ranks.rows_shift(add(shape, LOW, here(low, 0) + got, stats), low=-low), 0))
        for x in range(1, ranks.x):
            image_sums.append((ranks.loop_shift(add(shape, LOW, here(0, x)), x=-x), 0))
        text_sums = [(text_parts[0], 0)]
        for high in range(1, ranks.high):
            text_sums.append((ranks.rows_shift(text_parts[high].astype(LOW), -high, -high), 0))
        steps = [(h, k) for h in range(ranks.high) for k in range(ranks.low)][1:]
        stats = [stats, *[ranks.rows_shift(stats, high=h, low=k) for h, k in steps]]
        grad_text, done = finish(scale, text_feats, text_sums, flops=FIRST)
        grad_image, done = finish(scale, image_feats, image_sums, done)
        return grad_image, grad_text, mean_stats(devices * rows_dev, stats, done)

    rows_spec = P(("groups", "loop", "rows"), None)
    return jax.shard_map(
        shards,
        mesh=mesh,
        in_specs=(rows_spec, rows_spec, P(), P()),
        out_specs=(rows_spec, rows_spec, P("groups")),
        check_vma=False,
    )
```

time: 52 us -> 51.2 us (0.985)
  waiting for transfers between devices: 20.3 us -> 14.8 us
  starting transfers between devices: 22.2 us -> 26.1 us
  Pallas kernels: 6.23 us -> 6.85 us
    ppermute x6 -> x8, waiting for transfers between devices: 15.5 us -> 9.16 us  [rows_shift(): return lax.ppermute(value, 'rows', pairs)]
    ppermute x6 -> x8, starting transfers between devices: 15.2 us -> 18.6 us  [rows_shift(): return lax.ppermute(value, 'rows', pairs)]
    ppermute x11 -> x12, waiting for transfers between devices: 4.79 us -> 5.62 us  [loop_shift(): return lax.ppermute(value, 'loop', pairs)]
    pallas_call x11 -> x19, Pallas kernels: 5.68 us -> 6.29 us  [call(): pl.pallas_call(kernel, out_shape=outs[0] if single else tuple(outs), in_s...]
    ppermute x11 -> x12, starting transfers between devices: 7.01 us -> 7.45 us  [loop_shift(): return lax.ppermute(value, 'loop', pairs)]
  transfers between devices with their start and end apart: 17 -> 20, of which waited for: 9 -> 7; matrix products, arithmetic and copies ran while one was open for 0% -> 0% of each run, Pallas kernels for 5% -> 8%
where the time goes in v3:
time: 51.2 us; the launch traced here: 51 us
  starting transfers between devices  26.1 us (51%)
  waiting for transfers between devices  14.8 us (29%)
  Pallas kernels  6.85 us (13%)
  between operations  2.15 us (4%)
  local copies, waits for them, and re-layouts  1.13 us (2%)
    ppermute x8, starting transfers between devices, rows_shift(): return lax.ppermute(value, 'rows', pairs)  18.6 us
    ppermute x8, waiting for transfers between devices, rows_shift(): return lax.ppermute(value, 'rows', pairs)  9.16 us
    ppermute x12, starting transfers between devices, loop_shift(): return lax.ppermute(value, 'loop', pairs)  7.45 us
    pallas_call x19, Pallas kernels, call(): pl.pallas_call(kernel, out_shape=outs[0] if single else tuple(outs), in_s...  6.29 us
    ppermute x12, waiting for transfers between devices, loop_shift(): return lax.ppermute(value, 'loop', pairs)  5.62 us
    unnamed x6, local copies, waits for them, and re-layouts  1.13 us
  transfers between devices with their start and end apart: 20, of which 7 were waited for; matrix products, arithmetic and copies ran while one was open for 0% of the time, Pallas kernels for 8%

profile of v3, /device:TPU:0, one launch (start us, length us, event | category | flops | bytes accessed | tf_op | source)
XLA Modules:
  0.0 51.0 jit_solution(1768713628212801907)
XLA Ops:
  0.6 0.0 copy-start
  0.6 0.0 copy-start.1
  0.7 1.1 %copy-done.1 = f32[128,1152]{1,0:T(8,128)S(1)} copy-done((f32[128,1152]{1,0:T(8,128)S(1)}, f32[128,1152]{1,0:T(8,128)}, u32[]{:S(2)}) %copy-start.1) | copy-done | bytes 589848
  1.8 0.1 shard_map.67.refs_0_.refs_2_
  1.9 0.7 %collective-permute-start = (bf16[128,1152]{1,0:T(8,128)(2,1)S(1)}, bf16[128,1152]{1,0:T(8,128)(2,1)S(1)}, u32[]{:S(2)}, u32[]{:S(2)}) collective-permute-start(bf16[128,1152]{1,0:T(8,128)(2,1)S(1)} %shard_map.67.refs_0_.refs_2_), channel_id=1, source_target_pairs={{1,2},{2,1},{5,6},{6,5},{9,10},{10,9},{13,14},{14,13},{17,18},{18,... | collective-permute-start | bytes 884744 | tf_op jit(solution)/shard_map/ppermute | solution.py:214
  2.6 0.0 copy-done
  2.6 0.1 shard_map.68.refs_0_.refs_4_
  2.7 5.9 %collective-permute-start.3 = (bf16[128,1152]{1,0:T(8,128)(2,1)S(1)}, bf16[128,1152]{1,0:T(8,128)(2,1)S(1)}, u32[]{:S(2)}, u32[]{:S(2)}) collective-permute-start(bf16[128,1152]{1,0:T(8,128)(2,1)S(1)} %shard_map.68.refs_0_.refs_4_), channel_id=1, source_target_pairs={{0,1},{1,0},{2,3},{3,2},{4,5},{5,4},{6,7},{7,6},{8,9},{9,8},{10,11... | collective-permute-start | bytes 884744 | tf_op jit(solution)/shard_map/ppermute | solution.py:214
  8.6 1.5 %collective-permute-start.2 = (bf16[128,1152]{1,0:T(8,128)(2,1)S(1)}, bf16[128,1152]{1,0:T(8,128)(2,1)S(1)}, u32[]{:S(2)}, u32[]{:S(2)}) collective-permute-start(bf16[128,1152]{1,0:T(8,128)(2,1)S(1)} %shard_map.68.refs_0_.refs_4_), channel_id=1, source_target_pairs={{0,8},{4,12},{8,0},{12,4},{1,9},{5,13},{9,1},{13,5},{2,10},{6,14},... | collective-permute-start | bytes 884744 | tf_op jit(solution)/shard_map/ppermute | solution.py:205
  10.1 3.2 %collective-permute-start.1 = (bf16[128,1152]{1,0:T(8,128)(2,1)S(1)}, bf16[128,1152]{1,0:T(8,128)(2,1)S(1)}, u32[]{:S(2)}, u32[]{:S(2)}) collective-permute-start(bf16[128,1152]{1,0:T(8,128)(2,1)S(1)} %shard_map.67.refs_0_.refs_2_), channel_id=1, source_target_pairs={{0,3},{3,0},{4,7},{7,4},{8,11},{11,8},{12,15},{15,12},{16,19},{19,... | collective-permute-start | bytes 884744 | tf_op jit(solution)/shard_map/ppermute | solution.py:214
  13.4 0.1 collective-permute-start.5
  13.5 0.0 collective-permute-done.refs_0_
  13.5 2.6 %collective-permute-done.3.refs_1_.refs_6_.refs_2_ = bf16[128,1152]{1,0:T(8,128)(2,1)S(1)} collective-permute-done((bf16[128,1152]{1,0:T(8,128)(2,1)S(1)}, bf16[128,1152]{1,0:T(8,128)(2,1)S(1)}, u32[]{:S(2)}, u32[]{:S(2)}) %collective-permute-start.3) | collective-permute-done | bytes 294944 | tf_op jit(solution)/shard_map/ppermute | solution.py:214
  16.1 1.5 %collective-permute-start.4 = (bf16[128,1152]{1,0:T(8,128)(2,1)S(1)}, bf16[128,1152]{1,0:T(8,128)(2,1)S(1)}, u32[]{:S(2)}, u32[]{:S(2)}) collective-permute-start(bf16[128,1152]{1,0:T(8,128)(2,1)S(1)} %collective-permute-done.3.refs_1_.refs_6_.refs_2_), channel_id=1, source_target_pairs={{0,8},{4,12},{8,0},{12,4},{1,9},{5,13},{9,1},{13,5},{2,10},{6,14},... | collective-permute-start | bytes 884744 | tf_op jit(solution)/shard_map/ppermute | solution.py:205
  17.6 0.0 collective-permute-done.2.refs_1_.refs_5_
  17.6 5.2 %collective-permute-done.1.refs_1_ = bf16[128,1152]{1,0:T(8,128)(2,1)S(1)} collective-permute-done((bf16[128,1152]{1,0:T(8,128)(2,1)S(1)}, bf16[128,1152]{1,0:T(8,128)(2,1)S(1)}, u32[]{:S(2)}, u32[]{:S(2)}) %collective-permute-start.1) | collective-permute-done | bytes 294944 | tf_op jit(solution)/shard_map/ppermute | solution.py:214
  22.7 0.1 shard_map.72.refs_1_.refs_3_
  22.8 0.1 collective-permute-start.7
  22.9 0.5 collective-permute-start.6
  23.4 0.0 collective-permute-done.4.refs_0_
  23.4 0.1 collective-permute-start.8
  24.9 0.0 collective-permute-done.5.refs_8_.refs_4_
  24.9 0.0 collective-permute-done.7.refs_10_.refs_6_
  24.9 0.0 collective-permute-done.6.refs_9_.refs_5_
  24.9 0.4 collective-permute-done.8.refs_11_.refs_7_
  25.3 1.6 %shard_map.75 = (bf16[1024,256]{1,0:T(8,128)(2,1)S(1)}, f32[8,128]{1,0:T(8,128)S(1)}) custom-call(f32[1]{0:T(128)S(6)} %exp.3.refs_0_.scale_ref, f32[1]{0:T(128)S(6)} %copy.8.refs_1_, bf16[128,1152]{1,0:T(8,128)(2,1)S(1)} %shard_map.67.refs_0_.refs_2_, bf16[128,1152]{1,0:T(8,128)(2,1)S(1)} %shard_map.72.refs_1_.refs_3_, ...), custom_call_target="tpu_custom_call" | custom-call | flops 603979776 | bytes 3481608 | tf_op jit(solution)/shard_map/pallas_call | solution.py:29
  27.0 0.5 shard_map.77
  27.5 0.2 collective-permute-start.10
  27.7 0.4 collective-permute-start.9
  28.1 0.5 shard_map.76
  28.6 1.0 %collective-permute-done.10.refs_1_ = bf16[256,1152]{1,0:T(8,128)(2,1)S(1)} collective-permute-done((bf16[256,1152]{1,0:T(8,128)(2,1)S(1)}, bf16[256,1152]{1,0:T(8,128)(2,1)S(1)}, u32[]{:S(2)}, u32[]{:S(2)}) %collective-permute-start.10) | collective-permute-done | bytes 589856 | tf_op jit(solution)/shard_map/ppermute | solution.py:205
  29.5 0.1 shard_map.78
  29.6 1.6 %collective-permute-start.11 = (bf16[128,1152]{1,0:T(8,128)(2,1)S(1)}, bf16[128,1152]{1,0:T(8,128)(2,1)S(1)}, u32[]{:S(2)}, u32[]{:S(2)}) collective-permute-start(bf16[128,1152]{1,0:T(8,128)(2,1)S(1)} %shard_map.78), channel_id=1, source_target_pairs={{0,8},{4,12},{8,0},{12,4},{1,9},{5,13},{9,1},{13,5},{2,10},{6,14},... | collective-permute-start | bytes 884744 | tf_op jit(solution)/shard_map/ppermute | solution.py:205
  31.2 0.9 %shard_map.83 = (f32[128,1152]{1,0:T(8,128)S(1)}, bf16[128,1152]{1,0:T(8,128)(2,1)S(1)}) custom-call(bf16[1024,256]{1,0:T(8,128)(2,1)S(1)} %get-tuple-element.17.grad_ref, bf16[128,1152]{1,0:T(8,128)(2,1)S(1)} %shard_map.68.refs_0_.refs_4_, bf16[128,1152]{1,0:T(8,128)(2,1)S(1)} %collective-permute-done.2.refs_1_.refs_5_, ...), custom_call_target="tpu_custom_call" | custom-call | flops 603979776 | bytes 3768320 | tf_op jit(solution)/shard_map/pallas_call | solution.py:29
  32.0 2.5 %collective-permute-start.16 = (bf16[128,1152]{1,0:T(8,128)(2,1)S(1)}, bf16[128,1152]{1,0:T(8,128)(2,1)S(1)}, u32[]{:S(2)}, u32[]{:S(2)}) collective-permute-start(bf16[128,1152]{1,0:T(8,128)(2,1)S(1)} %get-tuple-element.26), channel_id=1, source_target_pairs={{0,3},{1,2},{2,1},{3,0},{4,7},{5,6},{6,5},{7,4},{8,11},{9,10},{10,... | collective-permute-start | bytes 884744 | tf_op jit(solution)/shard_map/ppermute | solution.py:214
  34.6 0.0 collective-permute-start.12
  34.6 1.2 %collective-permute-done.12.refs_1_ = f32[8,128]{1,0:T(8,128)S(1)} collective-permute-done((f32[8,128]{1,0:T(8,128)S(1)}, f32[8,128]{1,0:T(8,128)S(1)}, u32[]{:S(2)}, u32[]{:S(2)}) %collective-permute-start.12) | collective-permute-done | bytes 4128 | tf_op jit(solution)/shard_map/ppermute | solution.py:205
  35.8 0.5 %collective-permute-start.13 = (f32[8,128]{1,0:T(8,128)S(1)}, f32[8,128]{1,0:T(8,128)S(1)}, u32[]{:S(2)}, u32[]{:S(2)}) collective-permute-start(f32[8,128]{1,0:T(8,128)S(1)} %shard_map.79.refs_0_), channel_id=1, source_target_pairs={{0,8},{4,12},{8,0},{12,4},{1,9},{5,13},{9,1},{13,5},{2,10},{6,14},... | collective-permute-start | bytes 12296 | tf_op jit(solution)/shard_map/ppermute | solution.py:205
  36.3 3.1 %collective-permute-done.13.refs_1_ = f32[8,128]{1,0:T(8,128)S(1)} collective-permute-done((f32[8,128]{1,0:T(8,128)S(1)}, f32[8,128]{1,0:T(8,128)S(1)}, u32[]{:S(2)}, u32[]{:S(2)}) %collective-permute-start.13) | collective-permute-done | bytes 4128 | tf_op jit(solution)/shard_map/ppermute | solution.py:205
  39.4 0.0 collective-permute-done.9.refs_1_
  39.4 0.1 shard_map.82
  39.4 1.0 %collective-permute-start.15 = (bf16[128,1152]{1,0:T(8,128)(2,1)S(1)}, bf16[128,1152]{1,0:T(8,128)(2,1)S(1)}, u32[]{:S(2)}, u32[]{:S(2)}) collective-permute-start(bf16[128,1152]{1,0:T(8,128)(2,1)S(1)} %shard_map.82), channel_id=1, source_target_pairs={{0,8},{4,12},{8,0},{12,4},{1,9},{5,13},{9,1},{13,5},{2,10},{6,14},... | collective-permute-start | bytes 884744 | tf_op jit(solution)/shard_map/ppermute | solution.py:205
  40.4 0.0 collective-permute-done.11.refs_2_
  40.4 0.0 copy-start.2
  40.4 0.1 shard_map.81
  40.5 1.9 %collective-permute-start.14 = (bf16[128,1152]{1,0:T(8,128)(2,1)S(1)}, bf16[128,1152]{1,0:T(8,128)(2,1)S(1)}, u32[]{:S(2)}, u32[]{:S(2)}) collective-permute-start(bf16[128,1152]{1,0:T(8,128)(2,1)S(1)} %shard_map.81), channel_id=1, source_target_pairs={{0,1},{1,0},{2,3},{3,2},{4,5},{5,4},{6,7},{7,6},{8,9},{9,8},{10,11... | collective-permute-start | bytes 884744 | tf_op jit(solution)/shard_map/ppermute | solution.py:214
  42.4 0.2 collective-permute-start.17
  42.6 1.7 %collective-permute-start.18 = (f32[8,128]{1,0:T(8,128)S(1)}, f32[8,128]{1,0:T(8,128)S(1)}, u32[]{:S(2)}, u32[]{:S(2)}) collective-permute-start(f32[8,128]{1,0:T(8,128)S(1)} %shard_map.80.refs_3_.refs_0_), channel_id=1, source_target_pairs={{0,2},{1,3},{2,0},{3,1},{4,6},{5,7},{6,4},{7,5},{8,10},{9,11},{10,... | collective-permute-start | bytes 12296 | tf_op jit(solution)/shard_map/ppermute | solution.py:214
  44.3 0.0 collective-permute-done.16.refs_1_
  44.3 2.5 %collective-permute-start.19 = (f32[8,128]{1,0:T(8,128)S(1)}, f32[8,128]{1,0:T(8,128)S(1)}, u32[]{:S(2)}, u32[]{:S(2)}) collective-permute-start(f32[8,128]{1,0:T(8,128)S(1)} %shard_map.80.refs_3_.refs_0_), channel_id=1, source_target_pairs={{0,3},{1,2},{2,1},{3,0},{4,7},{5,6},{6,5},{7,4},{8,11},{9,10},{10,... | collective-permute-start | bytes 12296 | tf_op jit(solution)/shard_map/ppermute | solution.py:214
  46.8 0.0 copy-done.2
  46.8 1.1 %shard_map.84 = (f32[128,1152]{1,0:T(8,128)}, f32[8,128]{1,0:T(8,128)S(1)}) custom-call(f32[1]{0:T(128)S(6)} %exp.3.refs_0_.scale_ref, f32[128,1152]{1,0:T(8,128)S(1)} %copy-done.2, f32[128,1152]{1,0:T(8,128)S(1)} %get-tuple-element.25.refs_0_, bf16[128,1152]{1,0:T(8,128)(2,1)S(1)} %collective-permute-done.16.refs_1_), custom_call_target="tpu_custom_call" | custom-call | flops 1001474560 | bytes 2068484 | tf_op jit(solution)/shard_map/pallas_call | solution.py:29
  47.9 0.0 collective-permute-done.15.refs_3_
  47.9 1.4 %collective-permute-done.14.refs_2_ = bf16[128,1152]{1,0:T(8,128)(2,1)S(1)} collective-permute-done((bf16[128,1152]{1,0:T(8,128)(2,1)S(1)}, bf16[128,1152]{1,0:T(8,128)(2,1)S(1)}, u32[]{:S(2)}, u32[]{:S(2)}) %collective-permute-start.14) | collective-permute-done | bytes 294944 | tf_op jit(solution)/shard_map/ppermute | solution.py:214
  49.3 1.1 %shard_map.85 = (f32[128,1152]{1,0:T(8,128)}, f32[8,128]{1,0:T(8,128)S(1)}) custom-call(f32[1]{0:T(128)S(6)} %exp.3.refs_0_.scale_ref, f32[128,1152]{1,0:T(8,128)S(1)} %copy-done, f32[128,1152]{1,0:T(8,128)S(1)} %get-tuple-element.18.refs_0_, bf16[256,1152]{1,0:T(8,128)(2,1)S(1)} %collective-permute-done.9.refs_1_, ...), custom_call_target="tpu_custom_call" | custom-call | flops 1474560 | bytes 2957316 | tf_op jit(solution)/shard_map/pallas_call | solution.py:29
  50.4 0.0 collective-permute-done.17.refs_1_
  50.4 0.0 collective-permute-done.18.refs_2_
  50.4 0.0 collective-permute-done.19.refs_3_
  50.4 0.6 %shard_map.86 = f32[3]{0:T(128)} custom-call(f32[8,128]{1,0:T(8,128)S(1)} %shard_map.80.refs_3_.refs_0_, f32[8,128]{1,0:T(8,128)S(1)} %collective-permute-done.17.refs_1_, f32[8,128]{1,0:T(8,128)S(1)} %collective-permute-done.18.refs_2_, f32[8,128]{1,0:T(8,128)S(1)} %collective-permute-done.19.refs_3_, f32[8,128]{1,0:T(8,128)S(1)} %get-tuple-element.30.refs_4_), custom_call_target="tpu_custom_call" | custom-call | tf_op jit(solution)/shard_map/pallas_call | solution.py:183
  (7 shorter events, 0.0 us)
Async XLA Ops:
  0.6 2.0 %copy-start = (f32[128,1152]{1,0:T(8,128)S(1)}, f32[128,1152]{1,0:T(8,128)}, u32[]{:S(2)}) copy-start(f32[128,1152]{1,0:T(8,128)} %feats_ref.7) | copy-start | bytes 1769476
  0.6 1.1 %copy-start.1 = (f32[128,1152]{1,0:T(8,128)S(1)}, f32[128,1152]{1,0:T(8,128)}, u32[]{:S(2)}) copy-start(f32[128,1152]{1,0:T(8,128)} %feats_ref.6) | copy-start | bytes 1769476
  1.9 11.6 %collective-permute-start = (bf16[128,1152]{1,0:T(8,128)(2,1)S(1)}, bf16[128,1152]{1,0:T(8,128)(2,1)S(1)}, u32[]{:S(2)}, u32[]{:S(2)}) collective-permute-start(bf16[128,1152]{1,0:T(8,128)(2,1)S(1)} %shard_map.67.refs_0_.refs_2_), channel_id=1, source_target_pairs={{1,2},{2,1},{5,6},{6,5},{9,10},{10,9},{13,14},{14,13},{17,18},{18,... | collective-permute-start | bytes 884744 | tf_op jit(solution)/shard_map/ppermute | solution.py:214
  2.7 13.3 %collective-permute-start.3 = (bf16[128,1152]{1,0:T(8,128)(2,1)S(1)}, bf16[128,1152]{1,0:T(8,128)(2,1)S(1)}, u32[]{:S(2)}, u32[]{:S(2)}) collective-permute-start(bf16[128,1152]{1,0:T(8,128)(2,1)S(1)} %shard_map.68.refs_0_.refs_4_), channel_id=1, source_target_pairs={{0,1},{1,0},{2,3},{3,2},{4,5},{5,4},{6,7},{7,6},{8,9},{9,8},{10,11... | collective-permute-start | bytes 884744 | tf_op jit(solution)/shard_map/ppermute | solution.py:214
  8.6 8.9 %collective-permute-start.2 = (bf16[128,1152]{1,0:T(8,128)(2,1)S(1)}, bf16[128,1152]{1,0:T(8,128)(2,1)S(1)}, u32[]{:S(2)}, u32[]{:S(2)}) collective-permute-start(bf16[128,1152]{1,0:T(8,128)(2,1)S(1)} %shard_map.68.refs_0_.refs_4_), channel_id=1, source_target_pairs={{0,8},{4,12},{8,0},{12,4},{1,9},{5,13},{9,1},{13,5},{2,10},{6,14},... | collective-permute-start | bytes 884744 | tf_op jit(solution)/shard_map/ppermute | solution.py:205
  10.1 12.6 %collective-permute-start.1 = (bf16[128,1152]{1,0:T(8,128)(2,1)S(1)}, bf16[128,1152]{1,0:T(8,128)(2,1)S(1)}, u32[]{:S(2)}, u32[]{:S(2)}) collective-permute-start(bf16[128,1152]{1,0:T(8,128)(2,1)S(1)} %shard_map.67.refs_0_.refs_2_), channel_id=1, source_target_pairs={{0,3},{3,0},{4,7},{7,4},{8,11},{11,8},{12,15},{15,12},{16,19},{19,... | collective-permute-start | bytes 884744 | tf_op jit(solution)/shard_map/ppermute | solution.py:214
  13.4 11.5 %collective-permute-start.5 = (bf16[128,1152]{1,0:T(8,128)(2,1)S(1)}, bf16[128,1152]{1,0:T(8,128)(2,1)S(1)}, u32[]{:S(2)}, u32[]{:S(2)}) collective-permute-start(bf16[128,1152]{1,0:T(8,128)(2,1)S(1)} %shard_map.68.refs_0_.refs_4_), channel_id=1, source_target_pairs={{0,4},{4,0},{8,12},{12,8},{1,5},{5,1},{9,13},{13,9},{2,6},{6,2},{1... | collective-permute-start | bytes 884744 | tf_op jit(solution)/shard_map/ppermute | solution.py:205
  16.1 7.3 %collective-permute-start.4 = (bf16[128,1152]{1,0:T(8,128)(2,1)S(1)}, bf16[128,1152]{1,0:T(8,128)(2,1)S(1)}, u32[]{:S(2)}, u32[]{:S(2)}) collective-permute-start(bf16[128,1152]{1,0:T(8,128)(2,1)S(1)} %collective-permute-done.3.refs_1_.refs_6_.refs_2_), channel_id=1, source_target_pairs={{0,8},{4,12},{8,0},{12,4},{1,9},{5,13},{9,1},{13,5},{2,10},{6,14},... | collective-permute-start | bytes 884744 | tf_op jit(solution)/shard_map/ppermute | solution.py:205
  22.8 2.1 %collective-permute-start.7 = (bf16[128,1152]{1,0:T(8,128)(2,1)S(1)}, bf16[128,1152]{1,0:T(8,128)(2,1)S(1)}, u32[]{:S(2)}, u32[]{:S(2)}) collective-permute-start(bf16[128,1152]{1,0:T(8,128)(2,1)S(1)} %collective-permute-done.3.refs_1_.refs_6_.refs_2_), channel_id=1, source_target_pairs={{0,4},{4,0},{8,12},{12,8},{1,5},{5,1},{9,13},{13,9},{2,6},{6,2},{1... | collective-permute-start | bytes 884744 | tf_op jit(solution)/shard_map/ppermute | solution.py:205
  22.9 2.0 %collective-permute-start.6 = (bf16[128,1152]{1,0:T(8,128)(2,1)S(1)}, bf16[128,1152]{1,0:T(8,128)(2,1)S(1)}, u32[]{:S(2)}, u32[]{:S(2)}) collective-permute-start(bf16[128,1152]{1,0:T(8,128)(2,1)S(1)} %collective-permute-done.2.refs_1_.refs_5_), channel_id=1, source_target_pairs={{0,4},{4,0},{8,12},{12,8},{1,5},{5,1},{9,13},{13,9},{2,6},{6,2},{1... | collective-permute-start | bytes 884744 | tf_op jit(solution)/shard_map/ppermute | solution.py:205
  23.4 1.9 %collective-permute-start.8 = (bf16[128,1152]{1,0:T(8,128)(2,1)S(1)}, bf16[128,1152]{1,0:T(8,128)(2,1)S(1)}, u32[]{:S(2)}, u32[]{:S(2)}) collective-permute-start(bf16[128,1152]{1,0:T(8,128)(2,1)S(1)} %shard_map.74.refs_7_.refs_3_), channel_id=1, source_target_pairs={{0,4},{4,0},{8,12},{12,8},{1,5},{5,1},{9,13},{13,9},{2,6},{6,2},{1... | collective-permute-start | bytes 884744 | tf_op jit(solution)/shard_map/ppermute | solution.py:205
  27.5 2.1 %collective-permute-start.10 = (bf16[256,1152]{1,0:T(8,128)(2,1)S(1)}, bf16[256,1152]{1,0:T(8,128)(2,1)S(1)}, u32[]{:S(2)}, u32[]{:S(2)}) collective-permute-start(bf16[256,1152]{1,0:T(8,128)(2,1)S(1)} %get-tuple-element.21), channel_id=1, source_target_pairs={{0,4},{4,0},{8,12},{12,8},{1,5},{5,1},{9,13},{13,9},{2,6},{6,2},{1... | collective-permute-start | bytes 1769480 | tf_op jit(solution)/shard_map/ppermute | solution.py:205
  27.7 11.7 %collective-permute-start.9 = (bf16[256,1152]{1,0:T(8,128)(2,1)S(1)}, bf16[256,1152]{1,0:T(8,128)(2,1)S(1)}, u32[]{:S(2)}, u32[]{:S(2)}) collective-permute-start(bf16[256,1152]{1,0:T(8,128)(2,1)S(1)} %get-tuple-element.19), channel_id=1, source_target_pairs={{0,4},{4,0},{8,12},{12,8},{1,5},{5,1},{9,13},{13,9},{2,6},{6,2},{1... | collective-permute-start | bytes 1769480 | tf_op jit(solution)/shard_map/ppermute | solution.py:205
  29.6 10.8 %collective-permute-start.11 = (bf16[128,1152]{1,0:T(8,128)(2,1)S(1)}, bf16[128,1152]{1,0:T(8,128)(2,1)S(1)}, u32[]{:S(2)}, u32[]{:S(2)}) collective-permute-start(bf16[128,1152]{1,0:T(8,128)(2,1)S(1)} %shard_map.78), channel_id=1, source_target_pairs={{0,8},{4,12},{8,0},{12,4},{1,9},{5,13},{9,1},{13,5},{2,10},{6,14},... | collective-permute-start | bytes 884744 | tf_op jit(solution)/shard_map/ppermute | solution.py:205
  32.0 12.3 %collective-permute-start.16 = (bf16[128,1152]{1,0:T(8,128)(2,1)S(1)}, bf16[128,1152]{1,0:T(8,128)(2,1)S(1)}, u32[]{:S(2)}, u32[]{:S(2)}) collective-permute-start(bf16[128,1152]{1,0:T(8,128)(2,1)S(1)} %get-tuple-element.26), channel_id=1, source_target_pairs={{0,3},{1,2},{2,1},{3,0},{4,7},{5,6},{6,5},{7,4},{8,11},{9,10},{10,... | collective-permute-start | bytes 884744 | tf_op jit(solution)/shard_map/ppermute | solution.py:214
  34.6 1.2 %collective-permute-start.12 = (f32[8,128]{1,0:T(8,128)S(1)}, f32[8,128]{1,0:T(8,128)S(1)}, u32[]{:S(2)}, u32[]{:S(2)}) collective-permute-start(f32[8,128]{1,0:T(8,128)S(1)} %get-tuple-element.23.refs_0_), channel_id=1, source_target_pairs={{0,4},{4,0},{8,12},{12,8},{1,5},{5,1},{9,13},{13,9},{2,6},{6,2},{1... | collective-permute-start | bytes 12296 | tf_op jit(solution)/shard_map/ppermute | solution.py:205
  35.8 3.6 %collective-permute-start.13 = (f32[8,128]{1,0:T(8,128)S(1)}, f32[8,128]{1,0:T(8,128)S(1)}, u32[]{:S(2)}, u32[]{:S(2)}) collective-permute-start(f32[8,128]{1,0:T(8,128)S(1)} %shard_map.79.refs_0_), channel_id=1, source_target_pairs={{0,8},{4,12},{8,0},{12,4},{1,9},{5,13},{9,1},{13,5},{2,10},{6,14},... | collective-permute-start | bytes 12296 | tf_op jit(solution)/shard_map/ppermute | solution.py:205
  39.4 8.5 %collective-permute-start.15 = (bf16[128,1152]{1,0:T(8,128)(2,1)S(1)}, bf16[128,1152]{1,0:T(8,128)(2,1)S(1)}, u32[]{:S(2)}, u32[]{:S(2)}) collective-permute-start(bf16[128,1152]{1,0:T(8,128)(2,1)S(1)} %shard_map.82), channel_id=1, source_target_pairs={{0,8},{4,12},{8,0},{12,4},{1,9},{5,13},{9,1},{13,5},{2,10},{6,14},... | collective-permute-start | bytes 884744 | tf_op jit(solution)/shard_map/ppermute | solution.py:205
  40.4 6.4 %copy-start.2 = (f32[128,1152]{1,0:T(8,128)S(1)}, f32[128,1152]{1,0:T(8,128)}, u32[]{:S(2)}) copy-start(f32[128,1152]{1,0:T(8,128)} %feats_ref.6) | copy-start | bytes 1769476
  40.5 8.7 %collective-permute-start.14 = (bf16[128,1152]{1,0:T(8,128)(2,1)S(1)}, bf16[128,1152]{1,0:T(8,128)(2,1)S(1)}, u32[]{:S(2)}, u32[]{:S(2)}) collective-permute-start(bf16[128,1152]{1,0:T(8,128)(2,1)S(1)} %shard_map.81), channel_id=1, source_target_pairs={{0,1},{1,0},{2,3},{3,2},{4,5},{5,4},{6,7},{7,6},{8,9},{9,8},{10,11... | collective-permute-start | bytes 884744 | tf_op jit(solution)/shard_map/ppermute | solution.py:214
  42.4 8.0 %collective-permute-start.17 = (f32[8,128]{1,0:T(8,128)S(1)}, f32[8,128]{1,0:T(8,128)S(1)}, u32[]{:S(2)}, u32[]{:S(2)}) collective-permute-start(f32[8,128]{1,0:T(8,128)S(1)} %shard_map.80.refs_3_.refs_0_), channel_id=1, source_target_pairs={{0,1},{1,0},{2,3},{3,2},{4,5},{5,4},{6,7},{7,6},{8,9},{9,8},{10,11... | collective-permute-start | bytes 12296 | tf_op jit(solution)/shard_map/ppermute | solution.py:214
  42.6 7.8 %collective-permute-start.18 = (f32[8,128]{1,0:T(8,128)S(1)}, f32[8,128]{1,0:T(8,128)S(1)}, u32[]{:S(2)}, u32[]{:S(2)}) collective-permute-start(f32[8,128]{1,0:T(8,128)S(1)} %shard_map.80.refs_3_.refs_0_), channel_id=1, source_target_pairs={{0,2},{1,3},{2,0},{3,1},{4,6},{5,7},{6,4},{7,5},{8,10},{9,11},{10,... | collective-permute-start | bytes 12296 | tf_op jit(solution)/shard_map/ppermute | solution.py:214
  44.3 6.1 %collective-permute-start.19 = (f32[8,128]{1,0:T(8,128)S(1)}, f32[8,128]{1,0:T(8,128)S(1)}, u32[]{:S(2)}, u32[]{:S(2)}) collective-permute-start(f32[8,128]{1,0:T(8,128)S(1)} %shard_map.80.refs_3_.refs_0_), channel_id=1, source_target_pairs={{0,3},{1,2},{2,1},{3,0},{4,7},{5,6},{6,5},{7,4},{8,11},{9,10},{10,... | collective-permute-start | bytes 12296 | tf_op jit(solution)/shard_map/ppermute | solution.py:214

commit v4 on v3

--- a/solution.py
+++ b/solution.py
@@ -50,8 +50,8 @@
     refs[-1][...] = jnp.zeros(refs[-1].shape, WIDE)
 
 
-def token(*others, flops=0):
-    return call(token_kernel, [array((8, 128), WIDE)], 1024 + flops, *others)
+def token(*others, flops=0, smem=0):
+    return call(token_kernel, [array((8, 128), WIDE)], 1024 + flops, *others, smem=smem)
 
 
 def joined(refs):
@@ -102,29 +102,29 @@
     return call(kernel, outs, flops, scale, bias, *texts, *images, *others, smem=2)
 
 
-def image_kernel(at, rows, n_text, n_out, grad_ref, *refs):
-    texts = joined(refs[:n_text])
-    spread(jnp.dot(grad_ref[at : at + rows], texts, preferred_element_type=WIDE), refs[-n_out:])
-
-
-def image_tile(at, pair_grad, texts, outs, *others):
+def image_kernel(at, rows, n_grad, n_text, n_out, *refs):
+    grads, texts = joined(refs[:n_grad])[at : at + rows], joined(refs[n_grad : n_grad + n_text])
+    spread(jnp.dot(grads, texts, preferred_element_type=WIDE), refs[-n_out:])
+
+
+def image_tile(at, pair_grads, texts, outs, *others):
     rows = sum(out.shape[0] for out in outs)
-    kernel = functools.partial(image_kernel, at, rows, len(texts), len(outs))
-    flops = 2 * rows * pair_grad.shape[1] * texts[0].shape[1]
-    got = call(kernel, outs, flops, pair_grad, *texts, *others)
+    kernel = functools.partial(image_kernel, at, rows, len(pair_grads), len(texts), len(outs))
+    flops = 2 * rows * pair_grads[0].shape[1] * texts[0].shape[1]
+    got = call(kernel, outs, flops, *pair_grads, *texts, *others)
     return list(got) if len(outs) > 1 else [got]
 
 
-def text_kernel(n_image, n_out, grad_ref, *refs):
-    images = joined(refs[:n_image])
-    text_grad = lax.dot_general(grad_ref[...], images, COL_DOT, preferred_element_type=WIDE)
+def text_kernel(n_grad, n_image, n_out, *refs):
+    grads, images = joined(refs[:n_grad]), joined(refs[n_grad : n_grad + n_image])
+    text_grad = lax.dot_general(grads, images, COL_DOT, preferred_element_type=WIDE)
     spread(text_grad, refs[-n_out:])
 
 
-def text_tile(pair_grad, images, outs, *others):
-    kernel = functools.partial(text_kernel, len(images), len(outs))
-    flops = 2 * pair_grad.size * images[0].shape[1]
-    got = call(kernel, outs, flops, pair_grad, *images, *others)
+def text_tile(pair_grads, images, outs, *others):
+    kernel = functools.partial(text_kernel, len(pair_grads), len(images), len(outs))
+    flops = 2 * sum(v.size for v in pair_grads) * images[0].shape[1]
+    got = call(kernel, outs, flops, *pair_grads, *images, *others)
     return list(got) if len(outs) > 1 else [got]
 
 
@@ -243,7 +243,7 @@
             for x in range(1, ranks.x):
                 images[low, x, 0] = ranks.loop_shift(images[low, 0, 0], x=x)
         order = token(*(images[low, 0, 0] for low in range(ranks.low)), order)
-        order = token(*(images[0, x, 0] for x in range(ranks.x)), order)
+        order = token(scale, bias, *(images[0, x, 0] for x in range(ranks.x)), order, smem=2)
         for high, got in halves.items():
             texts[high] = add(text_low.shape, LOW, [(v, 0) for v in got], order)
         arrived = token(*texts.values(), order, flops=AHEAD)
@@ -262,7 +262,7 @@
             groups = [[key] for g in groups for key in g]
         one_tile = blocks <= IMAGE_TILE and len(texts) <= TEXT_TILE
         per_tile = len(groups) if one_tile else IMAGE_TILE
-        parts, text_parts, tiles, stats = {}, {}, [], None
+        parts, text_parts, tiles, stats = {}, {}, [], []
 
         def added(store, key, value):
             store[key] = store[key] + value if key in store else value
@@ -277,9 +277,10 @@
                 keys = list(texts)[j : j + TEXT_TILE]
                 own = rows_dev if i == 0 and j == 0 else 0
                 pair = [texts[k] for k in keys]
-                pair_grad, tile_stats = score_tile(own, scale, bias, held, pair, arrived)
-                tiles.append((keys, pair_grad, held, some, outs))
-                stats = tile_stats if stats is None else stats + tile_stats
+                cuts = [held[:-1], held[-1:]] if len(held) > 1 else [held]
+                got = [score_tile(own if not n else 0, scale, bias, c, pair, arrived) for n, c in enumerate(cuts)]
+                tiles.append((keys, [g for g, _ in got], held, some, outs))
+                stats += [s for _, s in got]
 
         def image_grads(wanted, *others):
             for keys, pair_grad, _, some, outs in tiles:
@@ -296,6 +297,7 @@
             for k, value in zip(keys, text_tile(pair_grad, held, text_outs)):
                 added(text_parts, k, value)
         image_grads(False)
+        stats = added_up(stats)
         stats = added_up([stats, *[ranks.loop_shift(stats, core=c) for c in range(1, ranks.core)]])
         stats = added_up([stats, *[ranks.loop_shift(stats, x=x) for x in range(1, ranks.x)]])
         for core in range(1, ranks.core):
@@ -313,19 +315,23 @@
             return [(parts[((low, x, 0),)], 0)] + [(back[low, c], x * rows_dev) for c in range(1, ranks.core)]
 
         shape = image_low.shape
-        image_sums = here(0, 0)
+        image_sums, ahead = here(0, 0), []
         for low in range(1, ranks.low):
-            got = [(ranks.loop_shift(add(shape, LOW, here(low, x)), x=-x), 0) for x in range(1, ranks.x)]
-            image_sums.append((ranks.rows_shift(add(shape, LOW, here(low, 0) + got, stats), low=-low), 0))
+            got = [
+                (ranks.loop_shift(add(shape, LOW, here(low, x), *text_parts.values()), x=-x), 0)
+                for x in range(1, ranks.x)
+            ]
+            ahead.append(ranks.rows_shift(add(shape, LOW, here(low, 0) + got, stats), low=-low))
         for x in range(1, ranks.x):
             image_sums.append((ranks.loop_shift(add(shape, LOW, here(0, x)), x=-x), 0))
+        image_sums += [(v, 0) for v in ahead]
         text_sums = [(text_parts[0], 0)]
         for high in range(1, ranks.high):
             text_sums.append((ranks.rows_shift(text_parts[high].astype(LOW), -high, -high), 0))
         steps = [(h, k) for h in range(ranks.high) for k in range(ranks.low)][1:]
         stats = [stats, *[ranks.rows_shift(stats, high=h, low=k) for h, k in steps]]
         grad_text, done = finish(scale, text_feats, text_sums, flops=FIRST)
-        grad_image, done = finish(scale, image_feats, image_sums, done)
+        grad_image, done = finish(scale, image_feats, image_sums, token(done, *ahead))
         return grad_image, grad_text, mean_stats(devices * rows_dev, stats, done)
 
     rows_spec = P(("groups", "loop", "rows"), None)

time: 51.2 us -> 50.1 us (0.979)
  waiting for transfers between devices: 14.8 us -> 13.7 us
    ppermute x8, waiting for transfers between devices: 9.16 us -> 6.51 us  [rows_shift(): return lax.ppermute(value, 'rows', pairs)]
    ppermute x12, waiting for transfers between devices: 5.62 us -> 7.21 us  [loop_shift(): return lax.ppermute(value, 'loop', pairs)]
    ppermute x8, starting transfers between devices: 18.6 us -> 17.7 us  [rows_shift(): return lax.ppermute(value, 'rows', pairs)]
    pallas_call x19 -> x22, Pallas kernels: 6.29 us -> 6.73 us  [call(): pl.pallas_call(kernel, out_shape=outs[0] if single else tuple(outs), in_s...]
  transfers between devices with their start and end apart: 20 -> 20, of which waited for: 7 -> 9; matrix products, arithmetic and copies ran while one was open for 0% -> 0% of each run, Pallas kernels for 8% -> 11%
where the time goes in v4:
time: 50.1 us; the launch traced here: 49.9 us
  starting transfers between devices  25.6 us (51%)
  waiting for transfers between devices  13.7 us (27%)
  Pallas kernels  7.29 us (15%)
  between operations  2.15 us (4%)
  local copies, waits for them, and re-layouts  1.13 us (2%)
    ppermute x8, starting transfers between devices, rows_shift(): return lax.ppermute(value, 'rows', pairs)  17.7 us
    ppermute x12, starting transfers between devices, loop_shift(): return lax.ppermute(value, 'loop', pairs)  7.88 us
    ppermute x12, waiting for transfers between devices, loop_shift(): return lax.ppermute(value, 'loop', pairs)  7.21 us
    pallas_call x22, Pallas kernels, call(): pl.pallas_call(kernel, out_shape=outs[0] if single else tuple(outs), in_s...  6.73 us
    ppermute x8, waiting for transfers between devices, rows_shift(): return lax.ppermute(value, 'rows', pairs)  6.51 us
    unnamed x6, local copies, waits for them, and re-layouts  1.13 us
  transfers between devices with their start and end apart: 20, of which 9 were waited for; matrix products, arithmetic and copies ran while one was open for 0% of the time, Pallas kernels for 11%

profile of v4, /device:TPU:0, one launch (start us, length us, event | category | flops | bytes accessed | tf_op | source)
XLA Modules:
  0.0 49.9 jit_solution(11812973813085206154)
XLA Ops:
  0.6 0.0 copy-start
  0.6 0.0 copy-start.1
  0.7 1.1 %copy-done.1 = f32[128,1152]{1,0:T(8,128)S(1)} copy-done((f32[128,1152]{1,0:T(8,128)S(1)}, f32[128,1152]{1,0:T(8,128)}, u32[]{:S(2)}) %copy-start.1) | copy-done | bytes 589848
  1.8 0.1 shard_map.67.refs_0_.refs_2_
  1.9 0.7 %collective-permute-start = (bf16[128,1152]{1,0:T(8,128)(2,1)S(1)}, bf16[128,1152]{1,0:T(8,128)(2,1)S(1)}, u32[]{:S(2)}, u32[]{:S(2)}) collective-permute-start(bf16[128,1152]{1,0:T(8,128)(2,1)S(1)} %shard_map.67.refs_0_.refs_2_), channel_id=1, source_target_pairs={{1,2},{2,1},{5,6},{6,5},{9,10},{10,9},{13,14},{14,13},{17,18},{18,... | collective-permute-start | bytes 884744 | tf_op jit(solution)/shard_map/ppermute | solution.py:214
  2.6 0.0 copy-done
  2.6 0.1 shard_map.68.refs_0_.refs_2_.refs_4_
  2.7 5.9 %collective-permute-start.3 = (bf16[128,1152]{1,0:T(8,128)(2,1)S(1)}, bf16[128,1152]{1,0:T(8,128)(2,1)S(1)}, u32[]{:S(2)}, u32[]{:S(2)}) collective-permute-start(bf16[128,1152]{1,0:T(8,128)(2,1)S(1)} %shard_map.68.refs_0_.refs_2_.refs_4_), channel_id=1, source_target_pairs={{0,1},{1,0},{2,3},{3,2},{4,5},{5,4},{6,7},{7,6},{8,9},{9,8},{10,11... | collective-permute-start | bytes 884744 | tf_op jit(solution)/shard_map/ppermute | solution.py:214
  8.6 1.5 %collective-permute-start.2 = (bf16[128,1152]{1,0:T(8,128)(2,1)S(1)}, bf16[128,1152]{1,0:T(8,128)(2,1)S(1)}, u32[]{:S(2)}, u32[]{:S(2)}) collective-permute-start(bf16[128,1152]{1,0:T(8,128)(2,1)S(1)} %shard_map.68.refs_0_.refs_2_.refs_4_), channel_id=1, source_target_pairs={{0,8},{4,12},{8,0},{12,4},{1,9},{5,13},{9,1},{13,5},{2,10},{6,14},... | collective-permute-start | bytes 884744 | tf_op jit(solution)/shard_map/ppermute | solution.py:205
  10.1 3.2 %collective-permute-start.1 = (bf16[128,1152]{1,0:T(8,128)(2,1)S(1)}, bf16[128,1152]{1,0:T(8,128)(2,1)S(1)}, u32[]{:S(2)}, u32[]{:S(2)}) collective-permute-start(bf16[128,1152]{1,0:T(8,128)(2,1)S(1)} %shard_map.67.refs_0_.refs_2_), channel_id=1, source_target_pairs={{0,3},{3,0},{4,7},{7,4},{8,11},{11,8},{12,15},{15,12},{16,19},{19,... | collective-permute-start | bytes 884744 | tf_op jit(solution)/shard_map/ppermute | solution.py:214
  13.4 0.1 collective-permute-start.5
  14.8 0.0 collective-permute-done.refs_0_
  14.8 1.3 %collective-permute-done.3.refs_1_.refs_6_.refs_4_ = bf16[128,1152]{1,0:T(8,128)(2,1)S(1)} collective-permute-done((bf16[128,1152]{1,0:T(8,128)(2,1)S(1)}, bf16[128,1152]{1,0:T(8,128)(2,1)S(1)}, u32[]{:S(2)}, u32[]{:S(2)}) %collective-permute-start.3) | collective-permute-done | bytes 294944 | tf_op jit(solution)/shard_map/ppermute | solution.py:214
  16.1 1.5 %collective-permute-start.4 = (bf16[128,1152]{1,0:T(8,128)(2,1)S(1)}, bf16[128,1152]{1,0:T(8,128)(2,1)S(1)}, u32[]{:S(2)}, u32[]{:S(2)}) collective-permute-start(bf16[128,1152]{1,0:T(8,128)(2,1)S(1)} %collective-permute-done.3.refs_1_.refs_6_.refs_4_), channel_id=1, source_target_pairs={{0,8},{4,12},{8,0},{12,4},{1,9},{5,13},{9,1},{13,5},{2,10},{6,14},... | collective-permute-start | bytes 884744 | tf_op jit(solution)/shard_map/ppermute | solution.py:205
  17.6 0.0 collective-permute-start.7
  17.6 0.0 collective-permute-done.2.refs_3_.refs_5_
  17.6 0.5 %collective-permute-start.6 = (bf16[128,1152]{1,0:T(8,128)(2,1)S(1)}, bf16[128,1152]{1,0:T(8,128)(2,1)S(1)}, u32[]{:S(2)}, u32[]{:S(2)}) collective-permute-start(bf16[128,1152]{1,0:T(8,128)(2,1)S(1)} %collective-permute-done.2.refs_3_.refs_5_), channel_id=1, source_target_pairs={{0,4},{4,0},{8,12},{12,8},{1,5},{5,1},{9,13},{13,9},{2,6},{6,2},{1... | collective-permute-start | bytes 884744 | tf_op jit(solution)/shard_map/ppermute | solution.py:205
  18.1 4.6 %collective-permute-done.1.refs_1_ = bf16[128,1152]{1,0:T(8,128)(2,1)S(1)} collective-permute-done((bf16[128,1152]{1,0:T(8,128)(2,1)S(1)}, bf16[128,1152]{1,0:T(8,128)(2,1)S(1)}, u32[]{:S(2)}, u32[]{:S(2)}) %collective-permute-start.1) | collective-permute-done | bytes 294944 | tf_op jit(solution)/shard_map/ppermute | solution.py:214
  22.7 0.1 shard_map.72.refs_1_.refs_3_
  22.8 1.5 %collective-permute-done.4.refs_0_ = bf16[128,1152]{1,0:T(8,128)(2,1)S(1)} collective-permute-done((bf16[128,1152]{1,0:T(8,128)(2,1)S(1)}, bf16[128,1152]{1,0:T(8,128)(2,1)S(1)}, u32[]{:S(2)}, u32[]{:S(2)}) %collective-permute-start.4) | collective-permute-done | bytes 294944 | tf_op jit(solution)/shard_map/ppermute | solution.py:205
  24.3 0.1 collective-permute-start.8
  24.4 0.0 collective-permute-done.5.refs_8_.refs_6_
  24.4 0.0 collective-permute-done.7.refs_10_.refs_8_
  24.4 0.0 collective-permute-done.6.refs_9_.refs_7_
  24.4 1.5 %shard_map.75 = (bf16[896,256]{1,0:T(8,128)(2,1)S(1)}, f32[8,128]{1,0:T(8,128)S(1)}) custom-call(f32[1]{0:T(128)S(6)} %exp.3.refs_0_.scale_ref, f32[1]{0:T(128)S(6)} %copy.8.refs_1_, bf16[128,1152]{1,0:T(8,128)(2,1)S(1)} %shard_map.67.refs_0_.refs_2_, bf16[128,1152]{1,0:T(8,128)(2,1)S(1)} %shard_map.72.refs_1_.refs_3_, ...), custom_call_target="tpu_custom_call" | custom-call | flops 528482304 | bytes 3121160 | tf_op jit(solution)/shard_map/pallas_call | solution.py:29
  25.9 0.1 collective-permute-done.8.refs_4_.refs_9_
  26.0 0.6 %shard_map.76 = (bf16[128,256]{1,0:T(8,128)(2,1)S(1)}, f32[8,128]{1,0:T(8,128)S(1)}) custom-call(f32[1]{0:T(128)S(6)} %exp.3.refs_0_.scale_ref, f32[1]{0:T(128)S(6)} %copy.8.refs_1_, bf16[128,1152]{1,0:T(8,128)(2,1)S(1)} %shard_map.67.refs_0_.refs_2_, bf16[128,1152]{1,0:T(8,128)(2,1)S(1)} %shard_map.72.refs_1_.refs_3_, ...), custom_call_target="tpu_custom_call" | custom-call | flops 75497472 | bytes 958472 | tf_op jit(solution)/shard_map/pallas_call | solution.py:29
  26.5 0.5 %shard_map.78 = (bf16[256,1152]{1,0:T(8,128)(2,1)S(1)}, bf16[256,1152]{1,0:T(8,128)(2,1)S(1)}) custom-call(bf16[896,256]{1,0:T(8,128)(2,1)S(1)} %get-tuple-element.19.refs_0_, bf16[128,256]{1,0:T(8,128)(2,1)S(1)} %get-tuple-element.20.refs_1_, bf16[128,1152]{1,0:T(8,128)(2,1)S(1)} %shard_map.67.refs_0_.refs_2_, bf16[128,1152]{1,0:T(8,128)(2,1)S(1)} %shard_map.72.refs_1_.refs_3_), custom_call_target="tpu_custom_call" | custom-call | flops 301989888 | bytes 2293760 | tf_op jit(solution)/shard_map/pallas_call | solution.py:29
  27.1 0.5 %collective-permute-start.11 = (bf16[256,1152]{1,0:T(8,128)(2,1)S(1)}, bf16[256,1152]{1,0:T(8,128)(2,1)S(1)}, u32[]{:S(2)}, u32[]{:S(2)}) collective-permute-start(bf16[256,1152]{1,0:T(8,128)(2,1)S(1)} %get-tuple-element.25), channel_id=1, source_target_pairs={{0,4},{4,0},{8,12},{12,8},{1,5},{5,1},{9,13},{13,9},{2,6},{6,2},{1... | collective-permute-start | bytes 1769480 | tf_op jit(solution)/shard_map/ppermute | solution.py:205
  27.6 0.1 collective-permute-start.9
  27.6 0.5 %shard_map.77 = (f32[128,1152]{1,0:T(8,128)S(1)}, f32[128,1152]{1,0:T(8,128)S(1)}, f32[128,1152]{1,0:T(8,128)S(1)}, f32[128,1152]{1,0:T(8,128)S(1)}) custom-call(bf16[896,256]{1,0:T(8,128)(2,1)S(1)} %get-tuple-element.19.refs_0_, bf16[128,256]{1,0:T(8,128)(2,1)S(1)} %get-tuple-element.20.refs_1_, bf16[128,1152]{1,0:T(8,128)(2,1)S(1)} %shard_map.67.refs_0_.refs_2_, ...), custom_call_target="tpu_custom_call" | custom-call | flops 301989888 | bytes 3473408 | tf_op jit(solution)/shard_map/pallas_call | solution.py:29
  28.1 0.9 %shard_map.80 = (f32[128,1152]{1,0:T(8,128)S(1)}, bf16[128,1152]{1,0:T(8,128)(2,1)S(1)}) custom-call(bf16[896,256]{1,0:T(8,128)(2,1)S(1)} %get-tuple-element.19.refs_0_, bf16[128,256]{1,0:T(8,128)(2,1)S(1)} %get-tuple-element.20.refs_1_, bf16[128,1152]{1,0:T(8,128)(2,1)S(1)} %shard_map.68.refs_0_.refs_2_.refs_4_, ...), custom_call_target="tpu_custom_call" | custom-call | flops 603979776 | bytes 3768320 | tf_op jit(solution)/shard_map/pallas_call | solution.py:29
  29.0 0.2 collective-permute-done.11.refs_1_
  29.2 0.1 shard_map.81
  29.3 0.6 %collective-permute-start.12 = (bf16[128,1152]{1,0:T(8,128)(2,1)S(1)}, bf16[128,1152]{1,0:T(8,128)(2,1)S(1)}, u32[]{:S(2)}, u32[]{:S(2)}) collective-permute-start(bf16[128,1152]{1,0:T(8,128)(2,1)S(1)} %shard_map.81), channel_id=1, source_target_pairs={{0,8},{4,12},{8,0},{12,4},{1,9},{5,13},{9,1},{13,5},{2,10},{6,14},... | collective-permute-start | bytes 884744 | tf_op jit(solution)/shard_map/ppermute | solution.py:205
  29.9 2.5 %collective-permute-start.16 = (bf16[128,1152]{1,0:T(8,128)(2,1)S(1)}, bf16[128,1152]{1,0:T(8,128)(2,1)S(1)}, u32[]{:S(2)}, u32[]{:S(2)}) collective-permute-start(bf16[128,1152]{1,0:T(8,128)(2,1)S(1)} %get-tuple-element.28.refs_3_), channel_id=1, source_target_pairs={{0,3},{1,2},{2,1},{3,0},{4,7},{5,6},{6,5},{7,4},{8,11},{9,10},{10,... | collective-permute-start | bytes 884744 | tf_op jit(solution)/shard_map/ppermute | solution.py:214
  32.3 0.0 collective-permute-start.13
  32.4 1.2 %collective-permute-done.13.refs_1_ = f32[8,128]{1,0:T(8,128)S(1)} collective-permute-done((f32[8,128]{1,0:T(8,128)S(1)}, f32[8,128]{1,0:T(8,128)S(1)}, u32[]{:S(2)}, u32[]{:S(2)}) %collective-permute-start.13) | collective-permute-done | bytes 4128 | tf_op jit(solution)/shard_map/ppermute | solution.py:205
  33.5 1.5 %collective-permute-start.14 = (f32[8,128]{1,0:T(8,128)S(1)}, f32[8,128]{1,0:T(8,128)S(1)}, u32[]{:S(2)}, u32[]{:S(2)}) collective-permute-start(f32[8,128]{1,0:T(8,128)S(1)} %shard_map.83.refs_0_), channel_id=1, source_target_pairs={{0,8},{4,12},{8,0},{12,4},{1,9},{5,13},{9,1},{13,5},{2,10},{6,14},... | collective-permute-start | bytes 12296 | tf_op jit(solution)/shard_map/ppermute | solution.py:205
  35.0 3.7 %collective-permute-done.14.refs_1_ = f32[8,128]{1,0:T(8,128)S(1)} collective-permute-done((f32[8,128]{1,0:T(8,128)S(1)}, f32[8,128]{1,0:T(8,128)S(1)}, u32[]{:S(2)}, u32[]{:S(2)}) %collective-permute-start.14) | collective-permute-done | bytes 4128 | tf_op jit(solution)/shard_map/ppermute | solution.py:205
  38.7 0.0 collective-permute-done.12.refs_2_
  38.7 0.1 shard_map.85
  38.8 1.0 %collective-permute-start.15 = (bf16[128,1152]{1,0:T(8,128)(2,1)S(1)}, bf16[128,1152]{1,0:T(8,128)(2,1)S(1)}, u32[]{:S(2)}, u32[]{:S(2)}) collective-permute-start(bf16[128,1152]{1,0:T(8,128)(2,1)S(1)} %shard_map.85), channel_id=1, source_target_pairs={{0,1},{1,0},{2,3},{3,2},{4,5},{5,4},{6,7},{7,6},{8,9},{9,8},{10,11... | collective-permute-start | bytes 884744 | tf_op jit(solution)/shard_map/ppermute | solution.py:214
  39.9 0.0 collective-permute-done.9.refs_1_
  39.9 0.0 copy-start.2
  39.9 0.1 shard_map.79
  39.9 1.6 %collective-permute-start.10 = (bf16[128,1152]{1,0:T(8,128)(2,1)S(1)}, bf16[128,1152]{1,0:T(8,128)(2,1)S(1)}, u32[]{:S(2)}, u32[]{:S(2)}) collective-permute-start(bf16[128,1152]{1,0:T(8,128)(2,1)S(1)} %shard_map.79), channel_id=1, source_target_pairs={{0,8},{4,12},{8,0},{12,4},{1,9},{5,13},{9,1},{13,5},{2,10},{6,14},... | collective-permute-start | bytes 884744 | tf_op jit(solution)/shard_map/ppermute | solution.py:205
  41.5 0.1 collective-permute-start.17
  41.6 1.8 %collective-permute-start.18 = (f32[8,128]{1,0:T(8,128)S(1)}, f32[8,128]{1,0:T(8,128)S(1)}, u32[]{:S(2)}, u32[]{:S(2)}) collective-permute-start(f32[8,128]{1,0:T(8,128)S(1)} %shard_map.84.refs_3_.refs_0_), channel_id=1, source_target_pairs={{0,2},{1,3},{2,0},{3,1},{4,6},{5,7},{6,4},{7,5},{8,10},{9,11},{10,... | collective-permute-start | bytes 12296 | tf_op jit(solution)/shard_map/ppermute | solution.py:214
  43.4 0.0 collective-permute-done.16.refs_1_
  43.4 2.5 %collective-permute-start.19 = (f32[8,128]{1,0:T(8,128)S(1)}, f32[8,128]{1,0:T(8,128)S(1)}, u32[]{:S(2)}, u32[]{:S(2)}) collective-permute-start(f32[8,128]{1,0:T(8,128)S(1)} %shard_map.84.refs_3_.refs_0_), channel_id=1, source_target_pairs={{0,3},{1,2},{2,1},{3,0},{4,7},{5,6},{6,5},{7,4},{8,11},{9,10},{10,... | collective-permute-start | bytes 12296 | tf_op jit(solution)/shard_map/ppermute | solution.py:214
  45.9 0.0 copy-done.2
  45.9 1.1 %shard_map.86 = (f32[128,1152]{1,0:T(8,128)}, f32[8,128]{1,0:T(8,128)S(1)}) custom-call(f32[1]{0:T(128)S(6)} %exp.3.refs_0_.scale_ref, f32[128,1152]{1,0:T(8,128)S(1)} %copy-done.2, f32[128,1152]{1,0:T(8,128)S(1)} %get-tuple-element.27.refs_2_.refs_0_, bf16[128,1152]{1,0:T(8,128)(2,1)S(1)} %collective-permute-done.16.refs_1_), custom_call_target="tpu_custom_call" | custom-call | flops 1001474560 | bytes 2068484 | tf_op jit(solution)/shard_map/pallas_call | solution.py:29
  46.9 0.6 %collective-permute-done.15.refs_1_.refs_3_ = bf16[128,1152]{1,0:T(8,128)(2,1)S(1)} collective-permute-done((bf16[128,1152]{1,0:T(8,128)(2,1)S(1)}, bf16[128,1152]{1,0:T(8,128)(2,1)S(1)}, u32[]{:S(2)}, u32[]{:S(2)}) %collective-permute-start.15) | collective-permute-done | bytes 294944 | tf_op jit(solution)/shard_map/ppermute | solution.py:214
  47.5 0.6 %collective-permute-done.10.refs_2_ = bf16[128,1152]{1,0:T(8,128)(2,1)S(1)} collective-permute-done((bf16[128,1152]{1,0:T(8,128)(2,1)S(1)}, bf16[128,1152]{1,0:T(8,128)(2,1)S(1)}, u32[]{:S(2)}, u32[]{:S(2)}) %collective-permute-start.10) | collective-permute-done | bytes 294944 | tf_op jit(solution)/shard_map/ppermute | solution.py:205
  48.2 1.1 %shard_map.88 = (f32[128,1152]{1,0:T(8,128)}, f32[8,128]{1,0:T(8,128)S(1)}) custom-call(f32[1]{0:T(128)S(6)} %exp.3.refs_0_.scale_ref, f32[128,1152]{1,0:T(8,128)S(1)} %copy-done, f32[128,1152]{1,0:T(8,128)S(1)} %get-tuple-element.21.refs_0_, bf16[256,1152]{1,0:T(8,128)(2,1)S(1)} %collective-permute-done.9.refs_1_, ...), custom_call_target="tpu_custom_call" | custom-call | flops 1474560 | bytes 2957316 | tf_op jit(solution)/shard_map/pallas_call | solution.py:29
  49.3 0.0 collective-permute-done.17.refs_1_
  49.3 0.0 collective-permute-done.18.refs_2_
  49.3 0.0 collective-permute-done.19.refs_3_
  49.3 0.6 %shard_map.89 = f32[3]{0:T(128)} custom-call(f32[8,128]{1,0:T(8,128)S(1)} %shard_map.84.refs_3_.refs_0_, f32[8,128]{1,0:T(8,128)S(1)} %collective-permute-done.17.refs_1_, f32[8,128]{1,0:T(8,128)S(1)} %collective-permute-done.18.refs_2_, f32[8,128]{1,0:T(8,128)S(1)} %collective-permute-done.19.refs_3_, f32[8,128]{1,0:T(8,128)S(1)} %get-tuple-element.34.refs_4_), custom_call_target="tpu_custom_call" | custom-call | tf_op jit(solution)/shard_map/pallas_call | solution.py:183
  (9 shorter events, 0.0 us)
Async XLA Ops:
  0.6 2.0 %copy-start = (f32[128,1152]{1,0:T(8,128)S(1)}, f32[128,1152]{1,0:T(8,128)}, u32[]{:S(2)}) copy-start(f32[128,1152]{1,0:T(8,128)} %feats_ref.7) | copy-start | bytes 1769476
  0.6 1.1 %copy-start.1 = (f32[128,1152]{1,0:T(8,128)S(1)}, f32[128,1152]{1,0:T(8,128)}, u32[]{:S(2)}) copy-start(f32[128,1152]{1,0:T(8,128)} %feats_ref.6) | copy-start | bytes 1769476
  1.9 12.9 %collective-permute-start = (bf16[128,1152]{1,0:T(8,128)(2,1)S(1)}, bf16[128,1152]{1,0:T(8,128)(2,1)S(1)}, u32[]{:S(2)}, u32[]{:S(2)}) collective-permute-start(bf16[128,1152]{1,0:T(8,128)(2,1)S(1)} %shard_map.67.refs_0_.refs_2_), channel_id=1, source_target_pairs={{1,2},{2,1},{5,6},{6,5},{9,10},{10,9},{13,14},{14,13},{17,18},{18,... | collective-permute-start | bytes 884744 | tf_op jit(solution)/shard_map/ppermute | solution.py:214
  2.7 13.3 %collective-permute-start.3 = (bf16[128,1152]{1,0:T(8,128)(2,1)S(1)}, bf16[128,1152]{1,0:T(8,128)(2,1)S(1)}, u32[]{:S(2)}, u32[]{:S(2)}) collective-permute-start(bf16[128,1152]{1,0:T(8,128)(2,1)S(1)} %shard_map.68.refs_0_.refs_2_.refs_4_), channel_id=1, source_target_pairs={{0,1},{1,0},{2,3},{3,2},{4,5},{5,4},{6,7},{7,6},{8,9},{9,8},{10,11... | collective-permute-start | bytes 884744 | tf_op jit(solution)/shard_map/ppermute | solution.py:214
  8.6 9.0 %collective-permute-start.2 = (bf16[128,1152]{1,0:T(8,128)(2,1)S(1)}, bf16[128,1152]{1,0:T(8,128)(2,1)S(1)}, u32[]{:S(2)}, u32[]{:S(2)}) collective-permute-start(bf16[128,1152]{1,0:T(8,128)(2,1)S(1)} %shard_map.68.refs_0_.refs_2_.refs_4_), channel_id=1, source_target_pairs={{0,8},{4,12},{8,0},{12,4},{1,9},{5,13},{9,1},{13,5},{2,10},{6,14},... | collective-permute-start | bytes 884744 | tf_op jit(solution)/shard_map/ppermute | solution.py:205
  10.1 12.6 %collective-permute-start.1 = (bf16[128,1152]{1,0:T(8,128)(2,1)S(1)}, bf16[128,1152]{1,0:T(8,128)(2,1)S(1)}, u32[]{:S(2)}, u32[]{:S(2)}) collective-permute-start(bf16[128,1152]{1,0:T(8,128)(2,1)S(1)} %shard_map.67.refs_0_.refs_2_), channel_id=1, source_target_pairs={{0,3},{3,0},{4,7},{7,4},{8,11},{11,8},{12,15},{15,12},{16,19},{19,... | collective-permute-start | bytes 884744 | tf_op jit(solution)/shard_map/ppermute | solution.py:214
  13.4 11.0 %collective-permute-start.5 = (bf16[128,1152]{1,0:T(8,128)(2,1)S(1)}, bf16[128,1152]{1,0:T(8,128)(2,1)S(1)}, u32[]{:S(2)}, u32[]{:S(2)}) collective-permute-start(bf16[128,1152]{1,0:T(8,128)(2,1)S(1)} %shard_map.68.refs_0_.refs_2_.refs_4_), channel_id=1, source_target_pairs={{0,4},{4,0},{8,12},{12,8},{1,5},{5,1},{9,13},{13,9},{2,6},{6,2},{1... | collective-permute-start | bytes 884744 | tf_op jit(solution)/shard_map/ppermute | solution.py:205
  16.1 8.2 %collective-permute-start.4 = (bf16[128,1152]{1,0:T(8,128)(2,1)S(1)}, bf16[128,1152]{1,0:T(8,128)(2,1)S(1)}, u32[]{:S(2)}, u32[]{:S(2)}) collective-permute-start(bf16[128,1152]{1,0:T(8,128)(2,1)S(1)} %collective-permute-done.3.refs_1_.refs_6_.refs_4_), channel_id=1, source_target_pairs={{0,8},{4,12},{8,0},{12,4},{1,9},{5,13},{9,1},{13,5},{2,10},{6,14},... | collective-permute-start | bytes 884744 | tf_op jit(solution)/shard_map/ppermute | solution.py:205
  17.6 6.8 %collective-permute-start.7 = (bf16[128,1152]{1,0:T(8,128)(2,1)S(1)}, bf16[128,1152]{1,0:T(8,128)(2,1)S(1)}, u32[]{:S(2)}, u32[]{:S(2)}) collective-permute-start(bf16[128,1152]{1,0:T(8,128)(2,1)S(1)} %collective-permute-done.3.refs_1_.refs_6_.refs_4_), channel_id=1, source_target_pairs={{0,4},{4,0},{8,12},{12,8},{1,5},{5,1},{9,13},{13,9},{2,6},{6,2},{1... | collective-permute-start | bytes 884744 | tf_op jit(solution)/shard_map/ppermute | solution.py:205
  17.6 6.8 %collective-permute-start.6 = (bf16[128,1152]{1,0:T(8,128)(2,1)S(1)}, bf16[128,1152]{1,0:T(8,128)(2,1)S(1)}, u32[]{:S(2)}, u32[]{:S(2)}) collective-permute-start(bf16[128,1152]{1,0:T(8,128)(2,1)S(1)} %collective-permute-done.2.refs_3_.refs_5_), channel_id=1, source_target_pairs={{0,4},{4,0},{8,12},{12,8},{1,5},{5,1},{9,13},{13,9},{2,6},{6,2},{1... | collective-permute-start | bytes 884744 | tf_op jit(solution)/shard_map/ppermute | solution.py:205
  24.3 1.6 %collective-permute-start.8 = (bf16[128,1152]{1,0:T(8,128)(2,1)S(1)}, bf16[128,1152]{1,0:T(8,128)(2,1)S(1)}, u32[]{:S(2)}, u32[]{:S(2)}) collective-permute-start(bf16[128,1152]{1,0:T(8,128)(2,1)S(1)} %shard_map.74.refs_7_.refs_5_), channel_id=1, source_target_pairs={{0,4},{4,0},{8,12},{12,8},{1,5},{5,1},{9,13},{13,9},{2,6},{6,2},{1... | collective-permute-start | bytes 884744 | tf_op jit(solution)/shard_map/ppermute | solution.py:205
  27.1 2.1 %collective-permute-start.11 = (bf16[256,1152]{1,0:T(8,128)(2,1)S(1)}, bf16[256,1152]{1,0:T(8,128)(2,1)S(1)}, u32[]{:S(2)}, u32[]{:S(2)}) collective-permute-start(bf16[256,1152]{1,0:T(8,128)(2,1)S(1)} %get-tuple-element.25), channel_id=1, source_target_pairs={{0,4},{4,0},{8,12},{12,8},{1,5},{5,1},{9,13},{13,9},{2,6},{6,2},{1... | collective-permute-start | bytes 1769480 | tf_op jit(solution)/shard_map/ppermute | solution.py:205
  27.6 12.3 %collective-permute-start.9 = (bf16[256,1152]{1,0:T(8,128)(2,1)S(1)}, bf16[256,1152]{1,0:T(8,128)(2,1)S(1)}, u32[]{:S(2)}, u32[]{:S(2)}) collective-permute-start(bf16[256,1152]{1,0:T(8,128)(2,1)S(1)} %get-tuple-element.22), channel_id=1, source_target_pairs={{0,4},{4,0},{8,12},{12,8},{1,5},{5,1},{9,13},{13,9},{2,6},{6,2},{1... | collective-permute-start | bytes 1769480 | tf_op jit(solution)/shard_map/ppermute | solution.py:205
  29.3 9.4 %collective-permute-start.12 = (bf16[128,1152]{1,0:T(8,128)(2,1)S(1)}, bf16[128,1152]{1,0:T(8,128)(2,1)S(1)}, u32[]{:S(2)}, u32[]{:S(2)}) collective-permute-start(bf16[128,1152]{1,0:T(8,128)(2,1)S(1)} %shard_map.81), channel_id=1, source_target_pairs={{0,8},{4,12},{8,0},{12,4},{1,9},{5,13},{9,1},{13,5},{2,10},{6,14},... | collective-permute-start | bytes 884744 | tf_op jit(solution)/shard_map/ppermute | solution.py:205
  29.9 13.5 %collective-permute-start.16 = (bf16[128,1152]{1,0:T(8,128)(2,1)S(1)}, bf16[128,1152]{1,0:T(8,128)(2,1)S(1)}, u32[]{:S(2)}, u32[]{:S(2)}) collective-permute-start(bf16[128,1152]{1,0:T(8,128)(2,1)S(1)} %get-tuple-element.28.refs_3_), channel_id=1, source_target_pairs={{0,3},{1,2},{2,1},{3,0},{4,7},{5,6},{6,5},{7,4},{8,11},{9,10},{10,... | collective-permute-start | bytes 884744 | tf_op jit(solution)/shard_map/ppermute | solution.py:214
  32.3 1.2 %collective-permute-start.13 = (f32[8,128]{1,0:T(8,128)S(1)}, f32[8,128]{1,0:T(8,128)S(1)}, u32[]{:S(2)}, u32[]{:S(2)}) collective-permute-start(f32[8,128]{1,0:T(8,128)S(1)} %shard_map.82.refs_0_), channel_id=1, source_target_pairs={{0,4},{4,0},{8,12},{12,8},{1,5},{5,1},{9,13},{13,9},{2,6},{6,2},{1... | collective-permute-start | bytes 12296 | tf_op jit(solution)/shard_map/ppermute | solution.py:205
  33.5 5.2 %collective-permute-start.14 = (f32[8,128]{1,0:T(8,128)S(1)}, f32[8,128]{1,0:T(8,128)S(1)}, u32[]{:S(2)}, u32[]{:S(2)}) collective-permute-start(f32[8,128]{1,0:T(8,128)S(1)} %shard_map.83.refs_0_), channel_id=1, source_target_pairs={{0,8},{4,12},{8,0},{12,4},{1,9},{5,13},{9,1},{13,5},{2,10},{6,14},... | collective-permute-start | bytes 12296 | tf_op jit(solution)/shard_map/ppermute | solution.py:205
  38.8 8.7 %collective-permute-start.15 = (bf16[128,1152]{1,0:T(8,128)(2,1)S(1)}, bf16[128,1152]{1,0:T(8,128)(2,1)S(1)}, u32[]{:S(2)}, u32[]{:S(2)}) collective-permute-start(bf16[128,1152]{1,0:T(8,128)(2,1)S(1)} %shard_map.85), channel_id=1, source_target_pairs={{0,1},{1,0},{2,3},{3,2},{4,5},{5,4},{6,7},{7,6},{8,9},{9,8},{10,11... | collective-permute-start | bytes 884744 | tf_op jit(solution)/shard_map/ppermute | solution.py:214
  39.9 6.0 %copy-start.2 = (f32[128,1152]{1,0:T(8,128)S(1)}, f32[128,1152]{1,0:T(8,128)}, u32[]{:S(2)}) copy-start(f32[128,1152]{1,0:T(8,128)} %feats_ref.6) | copy-start | bytes 1769476
  39.9 8.3 %collective-permute-start.10 = (bf16[128,1152]{1,0:T(8,128)(2,1)S(1)}, bf16[128,1152]{1,0:T(8,128)(2,1)S(1)}, u32[]{:S(2)}, u32[]{:S(2)}) collective-permute-start(bf16[128,1152]{1,0:T(8,128)(2,1)S(1)} %shard_map.79), channel_id=1, source_target_pairs={{0,8},{4,12},{8,0},{12,4},{1,9},{5,13},{9,1},{13,5},{2,10},{6,14},... | collective-permute-start | bytes 884744 | tf_op jit(solution)/shard_map/ppermute | solution.py:205
  41.5 7.8 %collective-permute-start.17 = (f32[8,128]{1,0:T(8,128)S(1)}, f32[8,128]{1,0:T(8,128)S(1)}, u32[]{:S(2)}, u32[]{:S(2)}) collective-permute-start(f32[8,128]{1,0:T(8,128)S(1)} %shard_map.84.refs_3_.refs_0_), channel_id=1, source_target_pairs={{0,1},{1,0},{2,3},{3,2},{4,5},{5,4},{6,7},{7,6},{8,9},{9,8},{10,11... | collective-permute-start | bytes 12296 | tf_op jit(solution)/shard_map/ppermute | solution.py:214
  41.6 7.8 %collective-permute-start.18 = (f32[8,128]{1,0:T(8,128)S(1)}, f32[8,128]{1,0:T(8,128)S(1)}, u32[]{:S(2)}, u32[]{:S(2)}) collective-permute-start(f32[8,128]{1,0:T(8,128)S(1)} %shard_map.84.refs_3_.refs_0_), channel_id=1, source_target_pairs={{0,2},{1,3},{2,0},{3,1},{4,6},{5,7},{6,4},{7,5},{8,10},{9,11},{10,... | collective-permute-start | bytes 12296 | tf_op jit(solution)/shard_map/ppermute | solution.py:214
  43.4 5.9 %collective-permute-start.19 = (f32[8,128]{1,0:T(8,128)S(1)}, f32[8,128]{1,0:T(8,128)S(1)}, u32[]{:S(2)}, u32[]{:S(2)}) collective-permute-start(f32[8,128]{1,0:T(8,128)S(1)} %shard_map.84.refs_3_.refs_0_), channel_id=1, source_target_pairs={{0,3},{1,2},{2,1},{3,0},{4,7},{5,6},{6,5},{7,4},{8,11},{9,10},{10,... | collective-permute-start | bytes 12296 | tf_op jit(solution)/shard_map/ppermute | solution.py:214

commit v5 on v4

--- a/solution.py
+++ b/solution.py
@@ -74,21 +74,28 @@
     scores = lax.dot_general(images, texts, ROW_DOT, preferred_element_type=WIDE)
     scaled = scale_ref[0] * scores
     logits = scaled + bias_ref[0]
+    grown = jnp.exp(logits)
+    pair_grad = grown / (1.0 + grown)
+    joint = grown
+    for _ in range(2):
+        half = joint.shape[0] // 2
+        if half % 8 == 0:
+            upper, lower = joint[:half], joint[half:]
+            joint = upper + lower + upper * lower
+    loss = jnp.sum(jnp.log1p(joint))
     if own:
-        row = lax.broadcasted_iota(jnp.int32, logits.shape, 0)
-        col = lax.broadcasted_iota(jnp.int32, logits.shape, 1)
-        sign = jnp.where((row == col) & (row < own), 1.0, -1.0).astype(WIDE)
-    else:
-        sign = jnp.full(logits.shape, -1.0, WIDE)
-    against = -sign * logits
-    small = jnp.exp(-jnp.abs(against))
-    above = jnp.where(against >= 0, 1.0, small) / (1.0 + small)
-    pair_grad = -sign * above
-    loss = jnp.maximum(against, 0.0) + jnp.log1p(small)
+        row = lax.broadcasted_iota(jnp.int32, (own, own), 0)
+        col = lax.broadcasted_iota(jnp.int32, (own, own), 1)
+        same = jnp.where(row == col, 1.0, 0.0).astype(WIDE)
+        loss = loss - jnp.sum(same * logits[:own, :own])
+        top = pair_grad[:own, :own] - same
+        if pair_grad.shape[1] > own:
+            top = jnp.concatenate([top, pair_grad[:own, own:]], axis=1)
+        pair_grad = jnp.concatenate([top, pair_grad[own:]], axis=0) if pair_grad.shape[0] > own else top
     which = lax.broadcasted_iota(jnp.int32, stats_ref.shape, 0)
     stats_ref[...] = jnp.where(
         which == 0,
-        jnp.sum(loss),
+        loss,
         jnp.where(which == 1, jnp.sum(pair_grad * scaled), jnp.sum(pair_grad)),
     )
     grad_ref[...] = pair_grad.astype(LOW)

time: 50.1 us -> 49.5 us (0.988)
  no operation moved by 1% of the time
where the time goes in v5:
time: 49.5 us; the launch traced here: 49.3 us
  starting transfers between devices  25.6 us (52%)
  waiting for transfers between devices  13.5 us (27%)
  Pallas kernels  6.95 us (14%)
  between operations  2.15 us (4%)
  local copies, waits for them, and re-layouts  1.13 us (2%)
    ppermute x8, starting transfers between devices, rows_shift(): return lax.ppermute(value, 'rows', pairs)  17.7 us
    ppermute x12, starting transfers between devices, loop_shift(): return lax.ppermute(value, 'loop', pairs)  7.87 us
    ppermute x12, waiting for transfers between devices, loop_shift(): return lax.ppermute(value, 'loop', pairs)  7.23 us
    pallas_call x22, Pallas kernels, call(): pl.pallas_call(kernel, out_shape=outs[0] if single else tuple(outs), in_s...  6.39 us
    ppermute x8, waiting for transfers between devices, rows_shift(): return lax.ppermute(value, 'rows', pairs)  6.26 us
    unnamed x6, local copies, waits for them, and re-layouts  1.13 us
  transfers between devices with their start and end apart: 20, of which 9 were waited for; matrix products, arithmetic and copies ran while one was open for 0% of the time, Pallas kernels for 11%

profile of v5, /device:TPU:0, one launch (start us, length us, event | category | flops | bytes accessed | tf_op | source)
XLA Modules:
  0.0 49.3 jit_solution(10681294500660256920)
XLA Ops:
  0.6 0.0 copy-start
  0.6 0.0 copy-start.1
  0.7 1.1 %copy-done.1 = f32[128,1152]{1,0:T(8,128)S(1)} copy-done((f32[128,1152]{1,0:T(8,128)S(1)}, f32[128,1152]{1,0:T(8,128)}, u32[]{:S(2)}) %copy-start.1) | copy-done | bytes 589848
  1.8 0.1 shard_map.67.refs_0_.refs_2_
  1.9 0.7 %collective-permute-start = (bf16[128,1152]{1,0:T(8,128)(2,1)S(1)}, bf16[128,1152]{1,0:T(8,128)(2,1)S(1)}, u32[]{:S(2)}, u32[]{:S(2)}) collective-permute-start(bf16[128,1152]{1,0:T(8,128)(2,1)S(1)} %shard_map.67.refs_0_.refs_2_), channel_id=1, source_target_pairs={{1,2},{2,1},{5,6},{6,5},{9,10},{10,9},{13,14},{14,13},{17,18},{18,... | collective-permute-start | bytes 884744 | tf_op jit(solution)/shard_map/ppermute | solution.py:221
  2.6 0.0 copy-done
  2.6 0.1 shard_map.68.refs_0_.refs_2_.refs_4_
  2.7 5.9 %collective-permute-start.3 = (bf16[128,1152]{1,0:T(8,128)(2,1)S(1)}, bf16[128,1152]{1,0:T(8,128)(2,1)S(1)}, u32[]{:S(2)}, u32[]{:S(2)}) collective-permute-start(bf16[128,1152]{1,0:T(8,128)(2,1)S(1)} %shard_map.68.refs_0_.refs_2_.refs_4_), channel_id=1, source_target_pairs={{0,1},{1,0},{2,3},{3,2},{4,5},{5,4},{6,7},{7,6},{8,9},{9,8},{10,11... | collective-permute-start | bytes 884744 | tf_op jit(solution)/shard_map/ppermute | solution.py:221
  8.6 1.5 %collective-permute-start.2 = (bf16[128,1152]{1,0:T(8,128)(2,1)S(1)}, bf16[128,1152]{1,0:T(8,128)(2,1)S(1)}, u32[]{:S(2)}, u32[]{:S(2)}) collective-permute-start(bf16[128,1152]{1,0:T(8,128)(2,1)S(1)} %shard_map.68.refs_0_.refs_2_.refs_4_), channel_id=1, source_target_pairs={{0,8},{4,12},{8,0},{12,4},{1,9},{5,13},{9,1},{13,5},{2,10},{6,14},... | collective-permute-start | bytes 884744 | tf_op jit(solution)/shard_map/ppermute | solution.py:212
  10.1 3.2 %collective-permute-start.1 = (bf16[128,1152]{1,0:T(8,128)(2,1)S(1)}, bf16[128,1152]{1,0:T(8,128)(2,1)S(1)}, u32[]{:S(2)}, u32[]{:S(2)}) collective-permute-start(bf16[128,1152]{1,0:T(8,128)(2,1)S(1)} %shard_map.67.refs_0_.refs_2_), channel_id=1, source_target_pairs={{0,3},{3,0},{4,7},{7,4},{8,11},{11,8},{12,15},{15,12},{16,19},{19,... | collective-permute-start | bytes 884744 | tf_op jit(solution)/shard_map/ppermute | solution.py:221
  13.4 0.1 collective-permute-start.5
  14.8 0.0 collective-permute-done.refs_0_
  14.8 1.3 %collective-permute-done.3.refs_1_.refs_6_.refs_4_ = bf16[128,1152]{1,0:T(8,128)(2,1)S(1)} collective-permute-done((bf16[128,1152]{1,0:T(8,128)(2,1)S(1)}, bf16[128,1152]{1,0:T(8,128)(2,1)S(1)}, u32[]{:S(2)}, u32[]{:S(2)}) %collective-permute-start.3) | collective-permute-done | bytes 294944 | tf_op jit(solution)/shard_map/ppermute | solution.py:221
  16.1 1.5 %collective-permute-start.4 = (bf16[128,1152]{1,0:T(8,128)(2,1)S(1)}, bf16[128,1152]{1,0:T(8,128)(2,1)S(1)}, u32[]{:S(2)}, u32[]{:S(2)}) collective-permute-start(bf16[128,1152]{1,0:T(8,128)(2,1)S(1)} %collective-permute-done.3.refs_1_.refs_6_.refs_4_), channel_id=1, source_target_pairs={{0,8},{4,12},{8,0},{12,4},{1,9},{5,13},{9,1},{13,5},{2,10},{6,14},... | collective-permute-start | bytes 884744 | tf_op jit(solution)/shard_map/ppermute | solution.py:212
  17.6 0.0 collective-permute-start.7
  17.6 0.0 collective-permute-done.2.refs_3_.refs_5_
  17.6 0.5 %collective-permute-start.6 = (bf16[128,1152]{1,0:T(8,128)(2,1)S(1)}, bf16[128,1152]{1,0:T(8,128)(2,1)S(1)}, u32[]{:S(2)}, u32[]{:S(2)}) collective-permute-start(bf16[128,1152]{1,0:T(8,128)(2,1)S(1)} %collective-permute-done.2.refs_3_.refs_5_), channel_id=1, source_target_pairs={{0,4},{4,0},{8,12},{12,8},{1,5},{5,1},{9,13},{13,9},{2,6},{6,2},{1... | collective-permute-start | bytes 884744 | tf_op jit(solution)/shard_map/ppermute | solution.py:212
  18.1 4.6 %collective-permute-done.1.refs_1_ = bf16[128,1152]{1,0:T(8,128)(2,1)S(1)} collective-permute-done((bf16[128,1152]{1,0:T(8,128)(2,1)S(1)}, bf16[128,1152]{1,0:T(8,128)(2,1)S(1)}, u32[]{:S(2)}, u32[]{:S(2)}) %collective-permute-start.1) | collective-permute-done | bytes 294944 | tf_op jit(solution)/shard_map/ppermute | solution.py:221
  22.7 0.1 shard_map.72.refs_1_.refs_3_
  22.8 1.5 %collective-permute-done.4.refs_0_ = bf16[128,1152]{1,0:T(8,128)(2,1)S(1)} collective-permute-done((bf16[128,1152]{1,0:T(8,128)(2,1)S(1)}, bf16[128,1152]{1,0:T(8,128)(2,1)S(1)}, u32[]{:S(2)}, u32[]{:S(2)}) %collective-permute-start.4) | collective-permute-done | bytes 294944 | tf_op jit(solution)/shard_map/ppermute | solution.py:212
  24.3 0.1 collective-permute-start.8
  24.4 0.0 collective-permute-done.5.refs_8_.refs_6_
  24.4 0.0 collective-permute-done.7.refs_10_.refs_8_
  24.4 0.0 collective-permute-done.6.refs_9_.refs_7_
  24.4 1.2 %shard_map.75 = (bf16[896,256]{1,0:T(8,128)(2,1)S(1)}, f32[8,128]{1,0:T(8,128)S(1)}) custom-call(f32[1]{0:T(128)S(6)} %exp.3.refs_0_.scale_ref, f32[1]{0:T(128)S(6)} %copy.8.refs_1_, bf16[128,1152]{1,0:T(8,128)(2,1)S(1)} %shard_map.67.refs_0_.refs_2_, bf16[128,1152]{1,0:T(8,128)(2,1)S(1)} %shard_map.72.refs_1_.refs_3_, ...), custom_call_target="tpu_custom_call" | custom-call | flops 528482304 | bytes 3121160 | tf_op jit(solution)/shard_map/pallas_call | solution.py:29
  25.6 0.3 collective-permute-done.8.refs_4_.refs_9_
  26.0 0.5 %shard_map.76 = (bf16[128,256]{1,0:T(8,128)(2,1)S(1)}, f32[8,128]{1,0:T(8,128)S(1)}) custom-call(f32[1]{0:T(128)S(6)} %exp.3.refs_0_.scale_ref, f32[1]{0:T(128)S(6)} %copy.8.refs_1_, bf16[128,1152]{1,0:T(8,128)(2,1)S(1)} %shard_map.67.refs_0_.refs_2_, bf16[128,1152]{1,0:T(8,128)(2,1)S(1)} %shard_map.72.refs_1_.refs_3_, ...), custom_call_target="tpu_custom_call" | custom-call | flops 75497472 | bytes 958472 | tf_op jit(solution)/shard_map/pallas_call | solution.py:29
  26.5 0.5 %shard_map.78 = (bf16[256,1152]{1,0:T(8,128)(2,1)S(1)}, bf16[256,1152]{1,0:T(8,128)(2,1)S(1)}) custom-call(bf16[896,256]{1,0:T(8,128)(2,1)S(1)} %get-tuple-element.19.refs_0_, bf16[128,256]{1,0:T(8,128)(2,1)S(1)} %get-tuple-element.20.refs_1_, bf16[128,1152]{1,0:T(8,128)(2,1)S(1)} %shard_map.67.refs_0_.refs_2_, bf16[128,1152]{1,0:T(8,128)(2,1)S(1)} %shard_map.72.refs_1_.refs_3_), custom_call_target="tpu_custom_call" | custom-call | flops 301989888 | bytes 2293760 | tf_op jit(solution)/shard_map/pallas_call | solution.py:29
  27.0 0.2 collective-permute-start.11
  27.2 0.4 collective-permute-start.9
  27.6 0.5 %shard_map.77 = (f32[128,1152]{1,0:T(8,128)S(1)}, f32[128,1152]{1,0:T(8,128)S(1)}, f32[128,1152]{1,0:T(8,128)S(1)}, f32[128,1152]{1,0:T(8,128)S(1)}) custom-call(bf16[896,256]{1,0:T(8,128)(2,1)S(1)} %get-tuple-element.19.refs_0_, bf16[128,256]{1,0:T(8,128)(2,1)S(1)} %get-tuple-element.20.refs_1_, bf16[128,1152]{1,0:T(8,128)(2,1)S(1)} %shard_map.67.refs_0_.refs_2_, ...), custom_call_target="tpu_custom_call" | custom-call | flops 301989888 | bytes 3473408 | tf_op jit(solution)/shard_map/pallas_call | solution.py:29
  28.1 0.9 %shard_map.80 = (f32[128,1152]{1,0:T(8,128)S(1)}, bf16[128,1152]{1,0:T(8,128)(2,1)S(1)}) custom-call(bf16[896,256]{1,0:T(8,128)(2,1)S(1)} %get-tuple-element.19.refs_0_, bf16[128,256]{1,0:T(8,128)(2,1)S(1)} %get-tuple-element.20.refs_1_, bf16[128,1152]{1,0:T(8,128)(2,1)S(1)} %shard_map.68.refs_0_.refs_2_.refs_4_, ...), custom_call_target="tpu_custom_call" | custom-call | flops 603979776 | bytes 3768320 | tf_op jit(solution)/shard_map/pallas_call | solution.py:29
  29.0 0.1 collective-permute-done.11.refs_1_
  29.1 0.1 shard_map.81
  29.1 0.6 %collective-permute-start.12 = (bf16[128,1152]{1,0:T(8,128)(2,1)S(1)}, bf16[128,1152]{1,0:T(8,128)(2,1)S(1)}, u32[]{:S(2)}, u32[]{:S(2)}) collective-permute-start(bf16[128,1152]{1,0:T(8,128)(2,1)S(1)} %shard_map.81), channel_id=1, source_target_pairs={{0,8},{4,12},{8,0},{12,4},{1,9},{5,13},{9,1},{13,5},{2,10},{6,14},... | collective-permute-start | bytes 884744 | tf_op jit(solution)/shard_map/ppermute | solution.py:212
  29.7 2.5 %collective-permute-start.16 = (bf16[128,1152]{1,0:T(8,128)(2,1)S(1)}, bf16[128,1152]{1,0:T(8,128)(2,1)S(1)}, u32[]{:S(2)}, u32[]{:S(2)}) collective-permute-start(bf16[128,1152]{1,0:T(8,128)(2,1)S(1)} %get-tuple-element.28.refs_3_), channel_id=1, source_target_pairs={{0,3},{1,2},{2,1},{3,0},{4,7},{5,6},{6,5},{7,4},{8,11},{9,10},{10,... | collective-permute-start | bytes 884744 | tf_op jit(solution)/shard_map/ppermute | solution.py:221
  32.2 0.0 collective-permute-start.13
  32.2 1.2 %collective-permute-done.13.refs_1_ = f32[8,128]{1,0:T(8,128)S(1)} collective-permute-done((f32[8,128]{1,0:T(8,128)S(1)}, f32[8,128]{1,0:T(8,128)S(1)}, u32[]{:S(2)}, u32[]{:S(2)}) %collective-permute-start.13) | collective-permute-done | bytes 4128 | tf_op jit(solution)/shard_map/ppermute | solution.py:212
  33.4 1.5 %collective-permute-start.14 = (f32[8,128]{1,0:T(8,128)S(1)}, f32[8,128]{1,0:T(8,128)S(1)}, u32[]{:S(2)}, u32[]{:S(2)}) collective-permute-start(f32[8,128]{1,0:T(8,128)S(1)} %shard_map.83.refs_0_), channel_id=1, source_target_pairs={{0,8},{4,12},{8,0},{12,4},{1,9},{5,13},{9,1},{13,5},{2,10},{6,14},... | collective-permute-start | bytes 12296 | tf_op jit(solution)/shard_map/ppermute | solution.py:212
  34.9 3.5 %collective-permute-done.14.refs_1_ = f32[8,128]{1,0:T(8,128)S(1)} collective-permute-done((f32[8,128]{1,0:T(8,128)S(1)}, f32[8,128]{1,0:T(8,128)S(1)}, u32[]{:S(2)}, u32[]{:S(2)}) %collective-permute-start.14) | collective-permute-done | bytes 4128 | tf_op jit(solution)/shard_map/ppermute | solution.py:212
  38.3 0.0 collective-permute-done.12.refs_2_
  38.4 0.1 shard_map.85
  38.5 1.1 %collective-permute-start.15 = (bf16[128,1152]{1,0:T(8,128)(2,1)S(1)}, bf16[128,1152]{1,0:T(8,128)(2,1)S(1)}, u32[]{:S(2)}, u32[]{:S(2)}) collective-permute-start(bf16[128,1152]{1,0:T(8,128)(2,1)S(1)} %shard_map.85), channel_id=1, source_target_pairs={{0,1},{1,0},{2,3},{3,2},{4,5},{5,4},{6,7},{7,6},{8,9},{9,8},{10,11... | collective-permute-start | bytes 884744 | tf_op jit(solution)/shard_map/ppermute | solution.py:221
  39.5 0.0 collective-permute-done.9.refs_1_
  39.5 0.0 copy-start.2
  39.5 0.1 shard_map.79
  39.6 1.6 %collective-permute-start.10 = (bf16[128,1152]{1,0:T(8,128)(2,1)S(1)}, bf16[128,1152]{1,0:T(8,128)(2,1)S(1)}, u32[]{:S(2)}, u32[]{:S(2)}) collective-permute-start(bf16[128,1152]{1,0:T(8,128)(2,1)S(1)} %shard_map.79), channel_id=1, source_target_pairs={{0,8},{4,12},{8,0},{12,4},{1,9},{5,13},{9,1},{13,5},{2,10},{6,14},... | collective-permute-start | bytes 884744 | tf_op jit(solution)/shard_map/ppermute | solution.py:212
  41.1 0.1 collective-permute-start.17
  41.2 1.8 %collective-permute-start.18 = (f32[8,128]{1,0:T(8,128)S(1)}, f32[8,128]{1,0:T(8,128)S(1)}, u32[]{:S(2)}, u32[]{:S(2)}) collective-permute-start(f32[8,128]{1,0:T(8,128)S(1)} %shard_map.84.refs_3_.refs_0_), channel_id=1, source_target_pairs={{0,2},{1,3},{2,0},{3,1},{4,6},{5,7},{6,4},{7,5},{8,10},{9,11},{10,... | collective-permute-start | bytes 12296 | tf_op jit(solution)/shard_map/ppermute | solution.py:221
  43.1 0.0 collective-permute-done.16.refs_1_
  43.1 2.5 %collective-permute-start.19 = (f32[8,128]{1,0:T(8,128)S(1)}, f32[8,128]{1,0:T(8,128)S(1)}, u32[]{:S(2)}, u32[]{:S(2)}) collective-permute-start(f32[8,128]{1,0:T(8,128)S(1)} %shard_map.84.refs_3_.refs_0_), channel_id=1, source_target_pairs={{0,3},{1,2},{2,1},{3,0},{4,7},{5,6},{6,5},{7,4},{8,11},{9,10},{10,... | collective-permute-start | bytes 12296 | tf_op jit(solution)/shard_map/ppermute | solution.py:221
  45.5 0.0 copy-done.2
  45.5 1.1 %shard_map.86 = (f32[128,1152]{1,0:T(8,128)}, f32[8,128]{1,0:T(8,128)S(1)}) custom-call(f32[1]{0:T(128)S(6)} %exp.3.refs_0_.scale_ref, f32[128,1152]{1,0:T(8,128)S(1)} %copy-done.2, f32[128,1152]{1,0:T(8,128)S(1)} %get-tuple-element.27.refs_2_.refs_0_, bf16[128,1152]{1,0:T(8,128)(2,1)S(1)} %collective-permute-done.16.refs_1_), custom_call_target="tpu_custom_call" | custom-call | flops 1001474560 | bytes 2068484 | tf_op jit(solution)/shard_map/pallas_call | solution.py:29
  46.6 0.3 collective-permute-done.15.refs_1_.refs_3_
  46.9 0.7 %collective-permute-done.10.refs_2_ = bf16[128,1152]{1,0:T(8,128)(2,1)S(1)} collective-permute-done((bf16[128,1152]{1,0:T(8,128)(2,1)S(1)}, bf16[128,1152]{1,0:T(8,128)(2,1)S(1)}, u32[]{:S(2)}, u32[]{:S(2)}) %collective-permute-start.10) | collective-permute-done | bytes 294944 | tf_op jit(solution)/shard_map/ppermute | solution.py:212
  47.6 1.1 %shard_map.88 = (f32[128,1152]{1,0:T(8,128)}, f32[8,128]{1,0:T(8,128)S(1)}) custom-call(f32[1]{0:T(128)S(6)} %exp.3.refs_0_.scale_ref, f32[128,1152]{1,0:T(8,128)S(1)} %copy-done, f32[128,1152]{1,0:T(8,128)S(1)} %get-tuple-element.21.refs_0_, bf16[256,1152]{1,0:T(8,128)(2,1)S(1)} %collective-permute-done.9.refs_1_, ...), custom_call_target="tpu_custom_call" | custom-call | flops 1474560 | bytes 2957316 | tf_op jit(solution)/shard_map/pallas_call | solution.py:29
  48.7 0.0 collective-permute-done.17.refs_1_
  48.7 0.0 collective-permute-done.18.refs_2_
  48.7 0.0 collective-permute-done.19.refs_3_
  48.8 0.6 %shard_map.89 = f32[3]{0:T(128)} custom-call(f32[8,128]{1,0:T(8,128)S(1)} %shard_map.84.refs_3_.refs_0_, f32[8,128]{1,0:T(8,128)S(1)} %collective-permute-done.17.refs_1_, f32[8,128]{1,0:T(8,128)S(1)} %collective-permute-done.18.refs_2_, f32[8,128]{1,0:T(8,128)S(1)} %collective-permute-done.19.refs_3_, f32[8,128]{1,0:T(8,128)S(1)} %get-tuple-element.34.refs_4_), custom_call_target="tpu_custom_call" | custom-call | tf_op jit(solution)/shard_map/pallas_call | solution.py:190
  (9 shorter events, 0.0 us)
Async XLA Ops:
  0.6 2.0 %copy-start = (f32[128,1152]{1,0:T(8,128)S(1)}, f32[128,1152]{1,0:T(8,128)}, u32[]{:S(2)}) copy-start(f32[128,1152]{1,0:T(8,128)} %feats_ref.7) | copy-start | bytes 1769476
  0.6 1.1 %copy-start.1 = (f32[128,1152]{1,0:T(8,128)S(1)}, f32[128,1152]{1,0:T(8,128)}, u32[]{:S(2)}) copy-start(f32[128,1152]{1,0:T(8,128)} %feats_ref.6) | copy-start | bytes 1769476
  1.9 12.9 %collective-permute-start = (bf16[128,1152]{1,0:T(8,128)(2,1)S(1)}, bf16[128,1152]{1,0:T(8,128)(2,1)S(1)}, u32[]{:S(2)}, u32[]{:S(2)}) collective-permute-start(bf16[128,1152]{1,0:T(8,128)(2,1)S(1)} %shard_map.67.refs_0_.refs_2_), channel_id=1, source_target_pairs={{1,2},{2,1},{5,6},{6,5},{9,10},{10,9},{13,14},{14,13},{17,18},{18,... | collective-permute-start | bytes 884744 | tf_op jit(solution)/shard_map/ppermute | solution.py:221
  2.7 13.3 %collective-permute-start.3 = (bf16[128,1152]{1,0:T(8,128)(2,1)S(1)}, bf16[128,1152]{1,0:T(8,128)(2,1)S(1)}, u32[]{:S(2)}, u32[]{:S(2)}) collective-permute-start(bf16[128,1152]{1,0:T(8,128)(2,1)S(1)} %shard_map.68.refs_0_.refs_2_.refs_4_), channel_id=1, source_target_pairs={{0,1},{1,0},{2,3},{3,2},{4,5},{5,4},{6,7},{7,6},{8,9},{9,8},{10,11... | collective-permute-start | bytes 884744 | tf_op jit(solution)/shard_map/ppermute | solution.py:221
  8.6 9.0 %collective-permute-start.2 = (bf16[128,1152]{1,0:T(8,128)(2,1)S(1)}, bf16[128,1152]{1,0:T(8,128)(2,1)S(1)}, u32[]{:S(2)}, u32[]{:S(2)}) collective-permute-start(bf16[128,1152]{1,0:T(8,128)(2,1)S(1)} %shard_map.68.refs_0_.refs_2_.refs_4_), channel_id=1, source_target_pairs={{0,8},{4,12},{8,0},{12,4},{1,9},{5,13},{9,1},{13,5},{2,10},{6,14},... | collective-permute-start | bytes 884744 | tf_op jit(solution)/shard_map/ppermute | solution.py:212
  10.1 12.6 %collective-permute-start.1 = (bf16[128,1152]{1,0:T(8,128)(2,1)S(1)}, bf16[128,1152]{1,0:T(8,128)(2,1)S(1)}, u32[]{:S(2)}, u32[]{:S(2)}) collective-permute-start(bf16[128,1152]{1,0:T(8,128)(2,1)S(1)} %shard_map.67.refs_0_.refs_2_), channel_id=1, source_target_pairs={{0,3},{3,0},{4,7},{7,4},{8,11},{11,8},{12,15},{15,12},{16,19},{19,... | collective-permute-start | bytes 884744 | tf_op jit(solution)/shard_map/ppermute | solution.py:221
  13.4 11.0 %collective-permute-start.5 = (bf16[128,1152]{1,0:T(8,128)(2,1)S(1)}, bf16[128,1152]{1,0:T(8,128)(2,1)S(1)}, u32[]{:S(2)}, u32[]{:S(2)}) collective-permute-start(bf16[128,1152]{1,0:T(8,128)(2,1)S(1)} %shard_map.68.refs_0_.refs_2_.refs_4_), channel_id=1, source_target_pairs={{0,4},{4,0},{8,12},{12,8},{1,5},{5,1},{9,13},{13,9},{2,6},{6,2},{1... | collective-permute-start | bytes 884744 | tf_op jit(solution)/shard_map/ppermute | solution.py:212
  16.1 8.2 %collective-permute-start.4 = (bf16[128,1152]{1,0:T(8,128)(2,1)S(1)}, bf16[128,1152]{1,0:T(8,128)(2,1)S(1)}, u32[]{:S(2)}, u32[]{:S(2)}) collective-permute-start(bf16[128,1152]{1,0:T(8,128)(2,1)S(1)} %collective-permute-done.3.refs_1_.refs_6_.refs_4_), channel_id=1, source_target_pairs={{0,8},{4,12},{8,0},{12,4},{1,9},{5,13},{9,1},{13,5},{2,10},{6,14},... | collective-permute-start | bytes 884744 | tf_op jit(solution)/shard_map/ppermute | solution.py:212
  17.6 6.8 %collective-permute-start.7 = (bf16[128,1152]{1,0:T(8,128)(2,1)S(1)}, bf16[128,1152]{1,0:T(8,128)(2,1)S(1)}, u32[]{:S(2)}, u32[]{:S(2)}) collective-permute-start(bf16[128,1152]{1,0:T(8,128)(2,1)S(1)} %collective-permute-done.3.refs_1_.refs_6_.refs_4_), channel_id=1, source_target_pairs={{0,4},{4,0},{8,12},{12,8},{1,5},{5,1},{9,13},{13,9},{2,6},{6,2},{1... | collective-permute-start | bytes 884744 | tf_op jit(solution)/shard_map/ppermute | solution.py:212
  17.6 6.8 %collective-permute-start.6 = (bf16[128,1152]{1,0:T(8,128)(2,1)S(1)}, bf16[128,1152]{1,0:T(8,128)(2,1)S(1)}, u32[]{:S(2)}, u32[]{:S(2)}) collective-permute-start(bf16[128,1152]{1,0:T(8,128)(2,1)S(1)} %collective-permute-done.2.refs_3_.refs_5_), channel_id=1, source_target_pairs={{0,4},{4,0},{8,12},{12,8},{1,5},{5,1},{9,13},{13,9},{2,6},{6,2},{1... | collective-permute-start | bytes 884744 | tf_op jit(solution)/shard_map/ppermute | solution.py:212
  24.3 1.6 %collective-permute-start.8 = (bf16[128,1152]{1,0:T(8,128)(2,1)S(1)}, bf16[128,1152]{1,0:T(8,128)(2,1)S(1)}, u32[]{:S(2)}, u32[]{:S(2)}) collective-permute-start(bf16[128,1152]{1,0:T(8,128)(2,1)S(1)} %shard_map.74.refs_7_.refs_5_), channel_id=1, source_target_pairs={{0,4},{4,0},{8,12},{12,8},{1,5},{5,1},{9,13},{13,9},{2,6},{6,2},{1... | collective-permute-start | bytes 884744 | tf_op jit(solution)/shard_map/ppermute | solution.py:212
  27.0 2.1 %collective-permute-start.11 = (bf16[256,1152]{1,0:T(8,128)(2,1)S(1)}, bf16[256,1152]{1,0:T(8,128)(2,1)S(1)}, u32[]{:S(2)}, u32[]{:S(2)}) collective-permute-start(bf16[256,1152]{1,0:T(8,128)(2,1)S(1)} %get-tuple-element.25), channel_id=1, source_target_pairs={{0,4},{4,0},{8,12},{12,8},{1,5},{5,1},{9,13},{13,9},{2,6},{6,2},{1... | collective-permute-start | bytes 1769480 | tf_op jit(solution)/shard_map/ppermute | solution.py:212
  27.2 12.3 %collective-permute-start.9 = (bf16[256,1152]{1,0:T(8,128)(2,1)S(1)}, bf16[256,1152]{1,0:T(8,128)(2,1)S(1)}, u32[]{:S(2)}, u32[]{:S(2)}) collective-permute-start(bf16[256,1152]{1,0:T(8,128)(2,1)S(1)} %get-tuple-element.22), channel_id=1, source_target_pairs={{0,4},{4,0},{8,12},{12,8},{1,5},{5,1},{9,13},{13,9},{2,6},{6,2},{1... | collective-permute-start | bytes 1769480 | tf_op jit(solution)/shard_map/ppermute | solution.py:212
  29.1 9.2 %collective-permute-start.12 = (bf16[128,1152]{1,0:T(8,128)(2,1)S(1)}, bf16[128,1152]{1,0:T(8,128)(2,1)S(1)}, u32[]{:S(2)}, u32[]{:S(2)}) collective-permute-start(bf16[128,1152]{1,0:T(8,128)(2,1)S(1)} %shard_map.81), channel_id=1, source_target_pairs={{0,8},{4,12},{8,0},{12,4},{1,9},{5,13},{9,1},{13,5},{2,10},{6,14},... | collective-permute-start | bytes 884744 | tf_op jit(solution)/shard_map/ppermute | solution.py:212
  29.7 13.3 %collective-permute-start.16 = (bf16[128,1152]{1,0:T(8,128)(2,1)S(1)}, bf16[128,1152]{1,0:T(8,128)(2,1)S(1)}, u32[]{:S(2)}, u32[]{:S(2)}) collective-permute-start(bf16[128,1152]{1,0:T(8,128)(2,1)S(1)} %get-tuple-element.28.refs_3_), channel_id=1, source_target_pairs={{0,3},{1,2},{2,1},{3,0},{4,7},{5,6},{6,5},{7,4},{8,11},{9,10},{10,... | collective-permute-start | bytes 884744 | tf_op jit(solution)/shard_map/ppermute | solution.py:221
  32.2 1.2 %collective-permute-start.13 = (f32[8,128]{1,0:T(8,128)S(1)}, f32[8,128]{1,0:T(8,128)S(1)}, u32[]{:S(2)}, u32[]{:S(2)}) collective-permute-start(f32[8,128]{1,0:T(8,128)S(1)} %shard_map.82.refs_0_), channel_id=1, source_target_pairs={{0,4},{4,0},{8,12},{12,8},{1,5},{5,1},{9,13},{13,9},{2,6},{6,2},{1... | collective-permute-start | bytes 12296 | tf_op jit(solution)/shard_map/ppermute | solution.py:212
  33.4 5.0 %collective-permute-start.14 = (f32[8,128]{1,0:T(8,128)S(1)}, f32[8,128]{1,0:T(8,128)S(1)}, u32[]{:S(2)}, u32[]{:S(2)}) collective-permute-start(f32[8,128]{1,0:T(8,128)S(1)} %shard_map.83.refs_0_), channel_id=1, source_target_pairs={{0,8},{4,12},{8,0},{12,4},{1,9},{5,13},{9,1},{13,5},{2,10},{6,14},... | collective-permute-start | bytes 12296 | tf_op jit(solution)/shard_map/ppermute | solution.py:212
  38.5 8.5 %collective-permute-start.15 = (bf16[128,1152]{1,0:T(8,128)(2,1)S(1)}, bf16[128,1152]{1,0:T(8,128)(2,1)S(1)}, u32[]{:S(2)}, u32[]{:S(2)}) collective-permute-start(bf16[128,1152]{1,0:T(8,128)(2,1)S(1)} %shard_map.85), channel_id=1, source_target_pairs={{0,1},{1,0},{2,3},{3,2},{4,5},{5,4},{6,7},{7,6},{8,9},{9,8},{10,11... | collective-permute-start | bytes 884744 | tf_op jit(solution)/shard_map/ppermute | solution.py:221
  39.5 6.0 %copy-start.2 = (f32[128,1152]{1,0:T(8,128)S(1)}, f32[128,1152]{1,0:T(8,128)}, u32[]{:S(2)}) copy-start(f32[128,1152]{1,0:T(8,128)} %feats_ref.6) | copy-start | bytes 1769476
  39.6 8.0 %collective-permute-start.10 = (bf16[128,1152]{1,0:T(8,128)(2,1)S(1)}, bf16[128,1152]{1,0:T(8,128)(2,1)S(1)}, u32[]{:S(2)}, u32[]{:S(2)}) collective-permute-start(bf16[128,1152]{1,0:T(8,128)(2,1)S(1)} %shard_map.79), channel_id=1, source_target_pairs={{0,8},{4,12},{8,0},{12,4},{1,9},{5,13},{9,1},{13,5},{2,10},{6,14},... | collective-permute-start | bytes 884744 | tf_op jit(solution)/shard_map/ppermute | solution.py:212
  41.1 7.6 %collective-permute-start.17 = (f32[8,128]{1,0:T(8,128)S(1)}, f32[8,128]{1,0:T(8,128)S(1)}, u32[]{:S(2)}, u32[]{:S(2)}) collective-permute-start(f32[8,128]{1,0:T(8,128)S(1)} %shard_map.84.refs_3_.refs_0_), channel_id=1, source_target_pairs={{0,1},{1,0},{2,3},{3,2},{4,5},{5,4},{6,7},{7,6},{8,9},{9,8},{10,11... | collective-permute-start | bytes 12296 | tf_op jit(solution)/shard_map/ppermute | solution.py:221
  41.2 7.5 %collective-permute-start.18 = (f32[8,128]{1,0:T(8,128)S(1)}, f32[8,128]{1,0:T(8,128)S(1)}, u32[]{:S(2)}, u32[]{:S(2)}) collective-permute-start(f32[8,128]{1,0:T(8,128)S(1)} %shard_map.84.refs_3_.refs_0_), channel_id=1, source_target_pairs={{0,2},{1,3},{2,0},{3,1},{4,6},{5,7},{6,4},{7,5},{8,10},{9,11},{10,... | collective-permute-start | bytes 12296 | tf_op jit(solution)/shard_map/ppermute | solution.py:221
  43.1 5.7 %collective-permute-start.19 = (f32[8,128]{1,0:T(8,128)S(1)}, f32[8,128]{1,0:T(8,128)S(1)}, u32[]{:S(2)}, u32[]{:S(2)}) collective-permute-start(f32[8,128]{1,0:T(8,128)S(1)} %shard_map.84.refs_3_.refs_0_), channel_id=1, source_target_pairs={{0,3},{1,2},{2,1},{3,0},{4,7},{5,6},{6,5},{7,4},{8,11},{9,10},{10,... | collective-permute-start | bytes 12296 | tf_op jit(solution)/shard_map/ppermute | solution.py:221

commit v6 on v5

--- a/solution.py
+++ b/solution.py
@@ -328,9 +328,9 @@
                 (ranks.loop_shift(add(shape, LOW, here(low, x), *text_parts.values()), x=-x), 0)
                 for x in range(1, ranks.x)
             ]
-            ahead.append(ranks.rows_shift(add(shape, LOW, here(low, 0) + got, stats), low=-low))
+            ahead.append(ranks.rows_shift(add(shape, LOW, here(low, 0) + got), low=-low))
         for x in range(1, ranks.x):
-            image_sums.append((ranks.loop_shift(add(shape, LOW, here(0, x)), x=-x), 0))
+            image_sums.append((ranks.loop_shift(add(shape, LOW, here(0, x), stats), x=-x), 0))
         image_sums += [(v, 0) for v in ahead]
         text_sums = [(text_parts[0], 0)]
         for high in range(1, ranks.high):

time: 49.5 us -> 49.5 us (level)
  no operation moved by 1% of the time
where the time goes in v6:
time: 49.5 us; the launch traced here: 49.3 us
  starting transfers between devices  25.6 us (52%)
  waiting for transfers between devices  13.5 us (27%)
  Pallas kernels  6.93 us (14%)
  between operations  2.15 us (4%)
  local copies, waits for them, and re-layouts  1.13 us (2%)
    ppermute x8, starting transfers between devices, rows_shift(): return lax.ppermute(value, 'rows', pairs)  17.7 us
    ppermute x12, starting transfers between devices, loop_shift(): return lax.ppermute(value, 'loop', pairs)  7.87 us
    ppermute x12, waiting for transfers between devices, loop_shift(): return lax.ppermute(value, 'loop', pairs)  7.22 us
    pallas_call x22, Pallas kernels, call(): pl.pallas_call(kernel, out_shape=outs[0] if single else tuple(outs), in_s...  6.37 us
    ppermute x8, waiting for transfers between devices, rows_shift(): return lax.ppermute(value, 'rows', pairs)  6.27 us
    unnamed x6, local copies, waits for them, and re-layouts  1.13 us
  transfers between devices with their start and end apart: 20, of which 9 were waited for; matrix products, arithmetic and copies ran while one was open for 0% of the time, Pallas kernels for 11%

profile of v6, /device:TPU:0, one launch (start us, length us, event | category | flops | bytes accessed | tf_op | source)
XLA Modules:
  0.0 49.3 jit_solution(8978840942445856671)
XLA Ops:
  0.6 0.0 copy-start
  0.6 0.0 copy-start.1
  0.7 1.1 %copy-done.1 = f32[128,1152]{1,0:T(8,128)S(1)} copy-done((f32[128,1152]{1,0:T(8,128)S(1)}, f32[128,1152]{1,0:T(8,128)}, u32[]{:S(2)}) %copy-start.1) | copy-done | bytes 589848
  1.8 0.1 shard_map.67.refs_0_.refs_2_
  1.9 0.7 %collective-permute-start = (bf16[128,1152]{1,0:T(8,128)(2,1)S(1)}, bf16[128,1152]{1,0:T(8,128)(2,1)S(1)}, u32[]{:S(2)}, u32[]{:S(2)}) collective-permute-start(bf16[128,1152]{1,0:T(8,128)(2,1)S(1)} %shard_map.67.refs_0_.refs_2_), channel_id=1, source_target_pairs={{1,2},{2,1},{5,6},{6,5},{9,10},{10,9},{13,14},{14,13},{17,18},{18,... | collective-permute-start | bytes 884744 | tf_op jit(solution)/shard_map/ppermute | solution.py:221
  2.6 0.0 copy-done
  2.6 0.1 shard_map.68.refs_0_.refs_2_.refs_4_
  2.7 5.9 %collective-permute-start.3 = (bf16[128,1152]{1,0:T(8,128)(2,1)S(1)}, bf16[128,1152]{1,0:T(8,128)(2,1)S(1)}, u32[]{:S(2)}, u32[]{:S(2)}) collective-permute-start(bf16[128,1152]{1,0:T(8,128)(2,1)S(1)} %shard_map.68.refs_0_.refs_2_.refs_4_), channel_id=1, source_target_pairs={{0,1},{1,0},{2,3},{3,2},{4,5},{5,4},{6,7},{7,6},{8,9},{9,8},{10,11... | collective-permute-start | bytes 884744 | tf_op jit(solution)/shard_map/ppermute | solution.py:221
  8.6 1.5 %collective-permute-start.2 = (bf16[128,1152]{1,0:T(8,128)(2,1)S(1)}, bf16[128,1152]{1,0:T(8,128)(2,1)S(1)}, u32[]{:S(2)}, u32[]{:S(2)}) collective-permute-start(bf16[128,1152]{1,0:T(8,128)(2,1)S(1)} %shard_map.68.refs_0_.refs_2_.refs_4_), channel_id=1, source_target_pairs={{0,8},{4,12},{8,0},{12,4},{1,9},{5,13},{9,1},{13,5},{2,10},{6,14},... | collective-permute-start | bytes 884744 | tf_op jit(solution)/shard_map/ppermute | solution.py:212
  10.1 3.2 %collective-permute-start.1 = (bf16[128,1152]{1,0:T(8,128)(2,1)S(1)}, bf16[128,1152]{1,0:T(8,128)(2,1)S(1)}, u32[]{:S(2)}, u32[]{:S(2)}) collective-permute-start(bf16[128,1152]{1,0:T(8,128)(2,1)S(1)} %shard_map.67.refs_0_.refs_2_), channel_id=1, source_target_pairs={{0,3},{3,0},{4,7},{7,4},{8,11},{11,8},{12,15},{15,12},{16,19},{19,... | collective-permute-start | bytes 884744 | tf_op jit(solution)/shard_map/ppermute | solution.py:221
  13.4 0.1 collective-permute-start.5
  14.8 0.0 collective-permute-done.refs_0_
  14.8 1.3 %collective-permute-done.3.refs_1_.refs_6_.refs_4_ = bf16[128,1152]{1,0:T(8,128)(2,1)S(1)} collective-permute-done((bf16[128,1152]{1,0:T(8,128)(2,1)S(1)}, bf16[128,1152]{1,0:T(8,128)(2,1)S(1)}, u32[]{:S(2)}, u32[]{:S(2)}) %collective-permute-start.3) | collective-permute-done | bytes 294944 | tf_op jit(solution)/shard_map/ppermute | solution.py:221
  16.1 1.5 %collective-permute-start.4 = (bf16[128,1152]{1,0:T(8,128)(2,1)S(1)}, bf16[128,1152]{1,0:T(8,128)(2,1)S(1)}, u32[]{:S(2)}, u32[]{:S(2)}) collective-permute-start(bf16[128,1152]{1,0:T(8,128)(2,1)S(1)} %collective-permute-done.3.refs_1_.refs_6_.refs_4_), channel_id=1, source_target_pairs={{0,8},{4,12},{8,0},{12,4},{1,9},{5,13},{9,1},{13,5},{2,10},{6,14},... | collective-permute-start | bytes 884744 | tf_op jit(solution)/shard_map/ppermute | solution.py:212
  17.6 0.0 collective-permute-start.7
  17.6 0.0 collective-permute-done.2.refs_3_.refs_5_
  17.6 0.5 %collective-permute-start.6 = (bf16[128,1152]{1,0:T(8,128)(2,1)S(1)}, bf16[128,1152]{1,0:T(8,128)(2,1)S(1)}, u32[]{:S(2)}, u32[]{:S(2)}) collective-permute-start(bf16[128,1152]{1,0:T(8,128)(2,1)S(1)} %collective-permute-done.2.refs_3_.refs_5_), channel_id=1, source_target_pairs={{0,4},{4,0},{8,12},{12,8},{1,5},{5,1},{9,13},{13,9},{2,6},{6,2},{1... | collective-permute-start | bytes 884744 | tf_op jit(solution)/shard_map/ppermute | solution.py:212
  18.1 4.6 %collective-permute-done.1.refs_1_ = bf16[128,1152]{1,0:T(8,128)(2,1)S(1)} collective-permute-done((bf16[128,1152]{1,0:T(8,128)(2,1)S(1)}, bf16[128,1152]{1,0:T(8,128)(2,1)S(1)}, u32[]{:S(2)}, u32[]{:S(2)}) %collective-permute-start.1) | collective-permute-done | bytes 294944 | tf_op jit(solution)/shard_map/ppermute | solution.py:221
  22.7 0.1 shard_map.72.refs_1_.refs_3_
  22.8 1.5 %collective-permute-done.4.refs_0_ = bf16[128,1152]{1,0:T(8,128)(2,1)S(1)} collective-permute-done((bf16[128,1152]{1,0:T(8,128)(2,1)S(1)}, bf16[128,1152]{1,0:T(8,128)(2,1)S(1)}, u32[]{:S(2)}, u32[]{:S(2)}) %collective-permute-start.4) | collective-permute-done | bytes 294944 | tf_op jit(solution)/shard_map/ppermute | solution.py:212
  24.3 0.1 collective-permute-start.8
  24.4 0.0 collective-permute-done.5.refs_8_.refs_6_
  24.4 0.0 collective-permute-done.7.refs_10_.refs_8_
  24.4 0.0 collective-permute-done.6.refs_9_.refs_7_
  24.4 1.2 %shard_map.75 = (bf16[896,256]{1,0:T(8,128)(2,1)S(1)}, f32[8,128]{1,0:T(8,128)S(1)}) custom-call(f32[1]{0:T(128)S(6)} %exp.3.refs_0_.scale_ref, f32[1]{0:T(128)S(6)} %copy.8.refs_1_, bf16[128,1152]{1,0:T(8,128)(2,1)S(1)} %shard_map.67.refs_0_.refs_2_, bf16[128,1152]{1,0:T(8,128)(2,1)S(1)} %shard_map.72.refs_1_.refs_3_, ...), custom_call_target="tpu_custom_call" | custom-call | flops 528482304 | bytes 3121160 | tf_op jit(solution)/shard_map/pallas_call | solution.py:29
  25.6 0.3 collective-permute-done.8.refs_4_.refs_9_
  26.0 0.5 %shard_map.76 = (bf16[128,256]{1,0:T(8,128)(2,1)S(1)}, f32[8,128]{1,0:T(8,128)S(1)}) custom-call(f32[1]{0:T(128)S(6)} %exp.3.refs_0_.scale_ref, f32[1]{0:T(128)S(6)} %copy.8.refs_1_, bf16[128,1152]{1,0:T(8,128)(2,1)S(1)} %shard_map.67.refs_0_.refs_2_, bf16[128,1152]{1,0:T(8,128)(2,1)S(1)} %shard_map.72.refs_1_.refs_3_, ...), custom_call_target="tpu_custom_call" | custom-call | flops 75497472 | bytes 958472 | tf_op jit(solution)/shard_map/pallas_call | solution.py:29
  26.5 0.5 %shard_map.78 = (bf16[256,1152]{1,0:T(8,128)(2,1)S(1)}, bf16[256,1152]{1,0:T(8,128)(2,1)S(1)}) custom-call(bf16[896,256]{1,0:T(8,128)(2,1)S(1)} %get-tuple-element.19.refs_0_, bf16[128,256]{1,0:T(8,128)(2,1)S(1)} %get-tuple-element.20.refs_1_, bf16[128,1152]{1,0:T(8,128)(2,1)S(1)} %shard_map.67.refs_0_.refs_2_, bf16[128,1152]{1,0:T(8,128)(2,1)S(1)} %shard_map.72.refs_1_.refs_3_), custom_call_target="tpu_custom_call" | custom-call | flops 301989888 | bytes 2293760 | tf_op jit(solution)/shard_map/pallas_call | solution.py:29
  27.0 0.2 collective-permute-start.13
  27.2 0.4 collective-permute-start.9
  27.6 0.5 %shard_map.77 = (f32[128,1152]{1,0:T(8,128)S(1)}, f32[128,1152]{1,0:T(8,128)S(1)}, f32[128,1152]{1,0:T(8,128)S(1)}, f32[128,1152]{1,0:T(8,128)S(1)}) custom-call(bf16[896,256]{1,0:T(8,128)(2,1)S(1)} %get-tuple-element.19.refs_0_, bf16[128,256]{1,0:T(8,128)(2,1)S(1)} %get-tuple-element.20.refs_1_, bf16[128,1152]{1,0:T(8,128)(2,1)S(1)} %shard_map.67.refs_0_.refs_2_, ...), custom_call_target="tpu_custom_call" | custom-call | flops 301989888 | bytes 3473408 | tf_op jit(solution)/shard_map/pallas_call | solution.py:29
  28.1 0.9 %shard_map.83 = (f32[128,1152]{1,0:T(8,128)S(1)}, bf16[128,1152]{1,0:T(8,128)(2,1)S(1)}) custom-call(bf16[896,256]{1,0:T(8,128)(2,1)S(1)} %get-tuple-element.19.refs_0_, bf16[128,256]{1,0:T(8,128)(2,1)S(1)} %get-tuple-element.20.refs_1_, bf16[128,1152]{1,0:T(8,128)(2,1)S(1)} %shard_map.68.refs_0_.refs_2_.refs_4_, ...), custom_call_target="tpu_custom_call" | custom-call | flops 603979776 | bytes 3768320 | tf_op jit(solution)/shard_map/pallas_call | solution.py:29
  29.0 0.1 collective-permute-done.13.refs_1_
  29.1 0.1 shard_map.84
  29.1 0.6 %collective-permute-start.14 = (bf16[128,1152]{1,0:T(8,128)(2,1)S(1)}, bf16[128,1152]{1,0:T(8,128)(2,1)S(1)}, u32[]{:S(2)}, u32[]{:S(2)}) collective-permute-start(bf16[128,1152]{1,0:T(8,128)(2,1)S(1)} %shard_map.84), channel_id=1, source_target_pairs={{0,8},{4,12},{8,0},{12,4},{1,9},{5,13},{9,1},{13,5},{2,10},{6,14},... | collective-permute-start | bytes 884744 | tf_op jit(solution)/shard_map/ppermute | solution.py:212
  29.7 2.5 %collective-permute-start.16 = (bf16[128,1152]{1,0:T(8,128)(2,1)S(1)}, bf16[128,1152]{1,0:T(8,128)(2,1)S(1)}, u32[]{:S(2)}, u32[]{:S(2)}) collective-permute-start(bf16[128,1152]{1,0:T(8,128)(2,1)S(1)} %get-tuple-element.30.refs_3_), channel_id=1, source_target_pairs={{0,3},{1,2},{2,1},{3,0},{4,7},{5,6},{6,5},{7,4},{8,11},{9,10},{10,... | collective-permute-start | bytes 884744 | tf_op jit(solution)/shard_map/ppermute | solution.py:221
  32.2 0.0 collective-permute-start.10
  32.2 1.2 %collective-permute-done.10.refs_1_ = f32[8,128]{1,0:T(8,128)S(1)} collective-permute-done((f32[8,128]{1,0:T(8,128)S(1)}, f32[8,128]{1,0:T(8,128)S(1)}, u32[]{:S(2)}, u32[]{:S(2)}) %collective-permute-start.10) | collective-permute-done | bytes 4128 | tf_op jit(solution)/shard_map/ppermute | solution.py:212
  33.4 1.5 %collective-permute-start.11 = (f32[8,128]{1,0:T(8,128)S(1)}, f32[8,128]{1,0:T(8,128)S(1)}, u32[]{:S(2)}, u32[]{:S(2)}) collective-permute-start(f32[8,128]{1,0:T(8,128)S(1)} %shard_map.80.refs_0_), channel_id=1, source_target_pairs={{0,8},{4,12},{8,0},{12,4},{1,9},{5,13},{9,1},{13,5},{2,10},{6,14},... | collective-permute-start | bytes 12296 | tf_op jit(solution)/shard_map/ppermute | solution.py:212
  34.9 3.5 %collective-permute-done.11.refs_1_ = f32[8,128]{1,0:T(8,128)S(1)} collective-permute-done((f32[8,128]{1,0:T(8,128)S(1)}, f32[8,128]{1,0:T(8,128)S(1)}, u32[]{:S(2)}, u32[]{:S(2)}) %collective-permute-start.11) | collective-permute-done | bytes 4128 | tf_op jit(solution)/shard_map/ppermute | solution.py:212
  38.3 0.0 collective-permute-done.14.refs_2_
  38.4 0.1 shard_map.85
  38.4 1.1 %collective-permute-start.15 = (bf16[128,1152]{1,0:T(8,128)(2,1)S(1)}, bf16[128,1152]{1,0:T(8,128)(2,1)S(1)}, u32[]{:S(2)}, u32[]{:S(2)}) collective-permute-start(bf16[128,1152]{1,0:T(8,128)(2,1)S(1)} %shard_map.85), channel_id=1, source_target_pairs={{0,1},{1,0},{2,3},{3,2},{4,5},{5,4},{6,7},{7,6},{8,9},{9,8},{10,11... | collective-permute-start | bytes 884744 | tf_op jit(solution)/shard_map/ppermute | solution.py:221
  39.5 0.0 collective-permute-done.9.refs_1_
  39.5 0.0 copy-start.2
  39.5 0.1 shard_map.82
  39.6 1.6 %collective-permute-start.12 = (bf16[128,1152]{1,0:T(8,128)(2,1)S(1)}, bf16[128,1152]{1,0:T(8,128)(2,1)S(1)}, u32[]{:S(2)}, u32[]{:S(2)}) collective-permute-start(bf16[128,1152]{1,0:T(8,128)(2,1)S(1)} %shard_map.82), channel_id=1, source_target_pairs={{0,8},{4,12},{8,0},{12,4},{1,9},{5,13},{9,1},{13,5},{2,10},{6,14},... | collective-permute-start | bytes 884744 | tf_op jit(solution)/shard_map/ppermute | solution.py:212
  41.1 0.1 collective-permute-start.17
  41.2 1.8 %collective-permute-start.18 = (f32[8,128]{1,0:T(8,128)S(1)}, f32[8,128]{1,0:T(8,128)S(1)}, u32[]{:S(2)}, u32[]{:S(2)}) collective-permute-start(f32[8,128]{1,0:T(8,128)S(1)} %shard_map.81.refs_2_.refs_0_), channel_id=1, source_target_pairs={{0,2},{1,3},{2,0},{3,1},{4,6},{5,7},{6,4},{7,5},{8,10},{9,11},{10,... | collective-permute-start | bytes 12296 | tf_op jit(solution)/shard_map/ppermute | solution.py:221
  43.0 0.0 collective-permute-done.16.refs_1_
  43.0 2.5 %collective-permute-start.19 = (f32[8,128]{1,0:T(8,128)S(1)}, f32[8,128]{1,0:T(8,128)S(1)}, u32[]{:S(2)}, u32[]{:S(2)}) collective-permute-start(f32[8,128]{1,0:T(8,128)S(1)} %shard_map.81.refs_2_.refs_0_), channel_id=1, source_target_pairs={{0,3},{1,2},{2,1},{3,0},{4,7},{5,6},{6,5},{7,4},{8,11},{9,10},{10,... | collective-permute-start | bytes 12296 | tf_op jit(solution)/shard_map/ppermute | solution.py:221
  45.5 0.0 copy-done.2
  45.5 1.1 %shard_map.86 = (f32[128,1152]{1,0:T(8,128)}, f32[8,128]{1,0:T(8,128)S(1)}) custom-call(f32[1]{0:T(128)S(6)} %exp.3.refs_0_.scale_ref, f32[128,1152]{1,0:T(8,128)S(1)} %copy-done.2, f32[128,1152]{1,0:T(8,128)S(1)} %get-tuple-element.29.refs_2_.refs_0_, bf16[128,1152]{1,0:T(8,128)(2,1)S(1)} %collective-permute-done.16.refs_1_), custom_call_target="tpu_custom_call" | custom-call | flops 1001474560 | bytes 2068484 | tf_op jit(solution)/shard_map/pallas_call | solution.py:29
  46.6 0.3 collective-permute-done.15.refs_1_.refs_3_
  46.9 0.7 %collective-permute-done.12.refs_2_ = bf16[128,1152]{1,0:T(8,128)(2,1)S(1)} collective-permute-done((bf16[128,1152]{1,0:T(8,128)(2,1)S(1)}, bf16[128,1152]{1,0:T(8,128)(2,1)S(1)}, u32[]{:S(2)}, u32[]{:S(2)}) %collective-permute-start.12) | collective-permute-done | bytes 294944 | tf_op jit(solution)/shard_map/ppermute | solution.py:212
  47.6 1.1 %shard_map.88 = (f32[128,1152]{1,0:T(8,128)}, f32[8,128]{1,0:T(8,128)S(1)}) custom-call(f32[1]{0:T(128)S(6)} %exp.3.refs_0_.scale_ref, f32[128,1152]{1,0:T(8,128)S(1)} %copy-done, f32[128,1152]{1,0:T(8,128)S(1)} %get-tuple-element.21.refs_0_, bf16[256,1152]{1,0:T(8,128)(2,1)S(1)} %collective-permute-done.9.refs_1_, ...), custom_call_target="tpu_custom_call" | custom-call | flops 1474560 | bytes 2957316 | tf_op jit(solution)/shard_map/pallas_call | solution.py:29
  48.7 0.0 collective-permute-done.17.refs_1_
  48.7 0.0 collective-permute-done.18.refs_2_
  48.7 0.0 collective-permute-done.19.refs_3_
  48.7 0.6 %shard_map.89 = f32[3]{0:T(128)} custom-call(f32[8,128]{1,0:T(8,128)S(1)} %shard_map.81.refs_2_.refs_0_, f32[8,128]{1,0:T(8,128)S(1)} %collective-permute-done.17.refs_1_, f32[8,128]{1,0:T(8,128)S(1)} %collective-permute-done.18.refs_2_, f32[8,128]{1,0:T(8,128)S(1)} %collective-permute-done.19.refs_3_, f32[8,128]{1,0:T(8,128)S(1)} %get-tuple-element.34.refs_4_), custom_call_target="tpu_custom_call" | custom-call | tf_op jit(solution)/shard_map/pallas_call | solution.py:190
  (9 shorter events, 0.0 us)
Async XLA Ops:
  0.6 2.0 %copy-start = (f32[128,1152]{1,0:T(8,128)S(1)}, f32[128,1152]{1,0:T(8,128)}, u32[]{:S(2)}) copy-start(f32[128,1152]{1,0:T(8,128)} %feats_ref.7) | copy-start | bytes 1769476
  0.6 1.1 %copy-start.1 = (f32[128,1152]{1,0:T(8,128)S(1)}, f32[128,1152]{1,0:T(8,128)}, u32[]{:S(2)}) copy-start(f32[128,1152]{1,0:T(8,128)} %feats_ref.6) | copy-start | bytes 1769476
  1.9 12.9 %collective-permute-start = (bf16[128,1152]{1,0:T(8,128)(2,1)S(1)}, bf16[128,1152]{1,0:T(8,128)(2,1)S(1)}, u32[]{:S(2)}, u32[]{:S(2)}) collective-permute-start(bf16[128,1152]{1,0:T(8,128)(2,1)S(1)} %shard_map.67.refs_0_.refs_2_), channel_id=1, source_target_pairs={{1,2},{2,1},{5,6},{6,5},{9,10},{10,9},{13,14},{14,13},{17,18},{18,... | collective-permute-start | bytes 884744 | tf_op jit(solution)/shard_map/ppermute | solution.py:221
  2.7 13.3 %collective-permute-start.3 = (bf16[128,1152]{1,0:T(8,128)(2,1)S(1)}, bf16[128,1152]{1,0:T(8,128)(2,1)S(1)}, u32[]{:S(2)}, u32[]{:S(2)}) collective-permute-start(bf16[128,1152]{1,0:T(8,128)(2,1)S(1)} %shard_map.68.refs_0_.refs_2_.refs_4_), channel_id=1, source_target_pairs={{0,1},{1,0},{2,3},{3,2},{4,5},{5,4},{6,7},{7,6},{8,9},{9,8},{10,11... | collective-permute-start | bytes 884744 | tf_op jit(solution)/shard_map/ppermute | solution.py:221
  8.6 9.0 %collective-permute-start.2 = (bf16[128,1152]{1,0:T(8,128)(2,1)S(1)}, bf16[128,1152]{1,0:T(8,128)(2,1)S(1)}, u32[]{:S(2)}, u32[]{:S(2)}) collective-permute-start(bf16[128,1152]{1,0:T(8,128)(2,1)S(1)} %shard_map.68.refs_0_.refs_2_.refs_4_), channel_id=1, source_target_pairs={{0,8},{4,12},{8,0},{12,4},{1,9},{5,13},{9,1},{13,5},{2,10},{6,14},... | collective-permute-start | bytes 884744 | tf_op jit(solution)/shard_map/ppermute | solution.py:212
  10.1 12.6 %collective-permute-start.1 = (bf16[128,1152]{1,0:T(8,128)(2,1)S(1)}, bf16[128,1152]{1,0:T(8,128)(2,1)S(1)}, u32[]{:S(2)}, u32[]{:S(2)}) collective-permute-start(bf16[128,1152]{1,0:T(8,128)(2,1)S(1)} %shard_map.67.refs_0_.refs_2_), channel_id=1, source_target_pairs={{0,3},{3,0},{4,7},{7,4},{8,11},{11,8},{12,15},{15,12},{16,19},{19,... | collective-permute-start | bytes 884744 | tf_op jit(solution)/shard_map/ppermute | solution.py:221
  13.4 11.0 %collective-permute-start.5 = (bf16[128,1152]{1,0:T(8,128)(2,1)S(1)}, bf16[128,1152]{1,0:T(8,128)(2,1)S(1)}, u32[]{:S(2)}, u32[]{:S(2)}) collective-permute-start(bf16[128,1152]{1,0:T(8,128)(2,1)S(1)} %shard_map.68.refs_0_.refs_2_.refs_4_), channel_id=1, source_target_pairs={{0,4},{4,0},{8,12},{12,8},{1,5},{5,1},{9,13},{13,9},{2,6},{6,2},{1... | collective-permute-start | bytes 884744 | tf_op jit(solution)/shard_map/ppermute | solution.py:212
  16.1 8.2 %collective-permute-start.4 = (bf16[128,1152]{1,0:T(8,128)(2,1)S(1)}, bf16[128,1152]{1,0:T(8,128)(2,1)S(1)}, u32[]{:S(2)}, u32[]{:S(2)}) collective-permute-start(bf16[128,1152]{1,0:T(8,128)(2,1)S(1)} %collective-permute-done.3.refs_1_.refs_6_.refs_4_), channel_id=1, source_target_pairs={{0,8},{4,12},{8,0},{12,4},{1,9},{5,13},{9,1},{13,5},{2,10},{6,14},... | collective-permute-start | bytes 884744 | tf_op jit(solution)/shard_map/ppermute | solution.py:212
  17.6 6.8 %collective-permute-start.7 = (bf16[128,1152]{1,0:T(8,128)(2,1)S(1)}, bf16[128,1152]{1,0:T(8,128)(2,1)S(1)}, u32[]{:S(2)}, u32[]{:S(2)}) collective-permute-start(bf16[128,1152]{1,0:T(8,128)(2,1)S(1)} %collective-permute-done.3.refs_1_.refs_6_.refs_4_), channel_id=1, source_target_pairs={{0,4},{4,0},{8,12},{12,8},{1,5},{5,1},{9,13},{13,9},{2,6},{6,2},{1... | collective-permute-start | bytes 884744 | tf_op jit(solution)/shard_map/ppermute | solution.py:212
  17.6 6.8 %collective-permute-start.6 = (bf16[128,1152]{1,0:T(8,128)(2,1)S(1)}, bf16[128,1152]{1,0:T(8,128)(2,1)S(1)}, u32[]{:S(2)}, u32[]{:S(2)}) collective-permute-start(bf16[128,1152]{1,0:T(8,128)(2,1)S(1)} %collective-permute-done.2.refs_3_.refs_5_), channel_id=1, source_target_pairs={{0,4},{4,0},{8,12},{12,8},{1,5},{5,1},{9,13},{13,9},{2,6},{6,2},{1... | collective-permute-start | bytes 884744 | tf_op jit(solution)/shard_map/ppermute | solution.py:212
  24.3 1.6 %collective-permute-start.8 = (bf16[128,1152]{1,0:T(8,128)(2,1)S(1)}, bf16[128,1152]{1,0:T(8,128)(2,1)S(1)}, u32[]{:S(2)}, u32[]{:S(2)}) collective-permute-start(bf16[128,1152]{1,0:T(8,128)(2,1)S(1)} %shard_map.74.refs_7_.refs_5_), channel_id=1, source_target_pairs={{0,4},{4,0},{8,12},{12,8},{1,5},{5,1},{9,13},{13,9},{2,6},{6,2},{1... | collective-permute-start | bytes 884744 | tf_op jit(solution)/shard_map/ppermute | solution.py:212
  27.0 2.1 %collective-permute-start.13 = (bf16[256,1152]{1,0:T(8,128)(2,1)S(1)}, bf16[256,1152]{1,0:T(8,128)(2,1)S(1)}, u32[]{:S(2)}, u32[]{:S(2)}) collective-permute-start(bf16[256,1152]{1,0:T(8,128)(2,1)S(1)} %get-tuple-element.27), channel_id=1, source_target_pairs={{0,4},{4,0},{8,12},{12,8},{1,5},{5,1},{9,13},{13,9},{2,6},{6,2},{1... | collective-permute-start | bytes 1769480 | tf_op jit(solution)/shard_map/ppermute | solution.py:212
  27.2 12.3 %collective-permute-start.9 = (bf16[256,1152]{1,0:T(8,128)(2,1)S(1)}, bf16[256,1152]{1,0:T(8,128)(2,1)S(1)}, u32[]{:S(2)}, u32[]{:S(2)}) collective-permute-start(bf16[256,1152]{1,0:T(8,128)(2,1)S(1)} %get-tuple-element.22), channel_id=1, source_target_pairs={{0,4},{4,0},{8,12},{12,8},{1,5},{5,1},{9,13},{13,9},{2,6},{6,2},{1... | collective-permute-start | bytes 1769480 | tf_op jit(solution)/shard_map/ppermute | solution.py:212
  29.1 9.2 %collective-permute-start.14 = (bf16[128,1152]{1,0:T(8,128)(2,1)S(1)}, bf16[128,1152]{1,0:T(8,128)(2,1)S(1)}, u32[]{:S(2)}, u32[]{:S(2)}) collective-permute-start(bf16[128,1152]{1,0:T(8,128)(2,1)S(1)} %shard_map.84), channel_id=1, source_target_pairs={{0,8},{4,12},{8,0},{12,4},{1,9},{5,13},{9,1},{13,5},{2,10},{6,14},... | collective-permute-start | bytes 884744 | tf_op jit(solution)/shard_map/ppermute | solution.py:212
  29.7 13.3 %collective-permute-start.16 = (bf16[128,1152]{1,0:T(8,128)(2,1)S(1)}, bf16[128,1152]{1,0:T(8,128)(2,1)S(1)}, u32[]{:S(2)}, u32[]{:S(2)}) collective-permute-start(bf16[128,1152]{1,0:T(8,128)(2,1)S(1)} %get-tuple-element.30.refs_3_), channel_id=1, source_target_pairs={{0,3},{1,2},{2,1},{3,0},{4,7},{5,6},{6,5},{7,4},{8,11},{9,10},{10,... | collective-permute-start | bytes 884744 | tf_op jit(solution)/shard_map/ppermute | solution.py:221
  32.2 1.2 %collective-permute-start.10 = (f32[8,128]{1,0:T(8,128)S(1)}, f32[8,128]{1,0:T(8,128)S(1)}, u32[]{:S(2)}, u32[]{:S(2)}) collective-permute-start(f32[8,128]{1,0:T(8,128)S(1)} %shard_map.79.refs_0_), channel_id=1, source_target_pairs={{0,4},{4,0},{8,12},{12,8},{1,5},{5,1},{9,13},{13,9},{2,6},{6,2},{1... | collective-permute-start | bytes 12296 | tf_op jit(solution)/shard_map/ppermute | solution.py:212
  33.4 5.0 %collective-permute-start.11 = (f32[8,128]{1,0:T(8,128)S(1)}, f32[8,128]{1,0:T(8,128)S(1)}, u32[]{:S(2)}, u32[]{:S(2)}) collective-permute-start(f32[8,128]{1,0:T(8,128)S(1)} %shard_map.80.refs_0_), channel_id=1, source_target_pairs={{0,8},{4,12},{8,0},{12,4},{1,9},{5,13},{9,1},{13,5},{2,10},{6,14},... | collective-permute-start | bytes 12296 | tf_op jit(solution)/shard_map/ppermute | solution.py:212
  38.4 8.5 %collective-permute-start.15 = (bf16[128,1152]{1,0:T(8,128)(2,1)S(1)}, bf16[128,1152]{1,0:T(8,128)(2,1)S(1)}, u32[]{:S(2)}, u32[]{:S(2)}) collective-permute-start(bf16[128,1152]{1,0:T(8,128)(2,1)S(1)} %shard_map.85), channel_id=1, source_target_pairs={{0,1},{1,0},{2,3},{3,2},{4,5},{5,4},{6,7},{7,6},{8,9},{9,8},{10,11... | collective-permute-start | bytes 884744 | tf_op jit(solution)/shard_map/ppermute | solution.py:221
  39.5 6.0 %copy-start.2 = (f32[128,1152]{1,0:T(8,128)S(1)}, f32[128,1152]{1,0:T(8,128)}, u32[]{:S(2)}) copy-start(f32[128,1152]{1,0:T(8,128)} %feats_ref.6) | copy-start | bytes 1769476
  39.6 8.0 %collective-permute-start.12 = (bf16[128,1152]{1,0:T(8,128)(2,1)S(1)}, bf16[128,1152]{1,0:T(8,128)(2,1)S(1)}, u32[]{:S(2)}, u32[]{:S(2)}) collective-permute-start(bf16[128,1152]{1,0:T(8,128)(2,1)S(1)} %shard_map.82), channel_id=1, source_target_pairs={{0,8},{4,12},{8,0},{12,4},{1,9},{5,13},{9,1},{13,5},{2,10},{6,14},... | collective-permute-start | bytes 884744 | tf_op jit(solution)/shard_map/ppermute | solution.py:212
  41.1 7.6 %collective-permute-start.17 = (f32[8,128]{1,0:T(8,128)S(1)}, f32[8,128]{1,0:T(8,128)S(1)}, u32[]{:S(2)}, u32[]{:S(2)}) collective-permute-start(f32[8,128]{1,0:T(8,128)S(1)} %shard_map.81.refs_2_.refs_0_), channel_id=1, source_target_pairs={{0,1},{1,0},{2,3},{3,2},{4,5},{5,4},{6,7},{7,6},{8,9},{9,8},{10,11... | collective-permute-start | bytes 12296 | tf_op jit(solution)/shard_map/ppermute | solution.py:221
  41.2 7.5 %collective-permute-start.18 = (f32[8,128]{1,0:T(8,128)S(1)}, f32[8,128]{1,0:T(8,128)S(1)}, u32[]{:S(2)}, u32[]{:S(2)}) collective-permute-start(f32[8,128]{1,0:T(8,128)S(1)} %shard_map.81.refs_2_.refs_0_), channel_id=1, source_target_pairs={{0,2},{1,3},{2,0},{3,1},{4,6},{5,7},{6,4},{7,5},{8,10},{9,11},{10,... | collective-permute-start | bytes 12296 | tf_op jit(solution)/shard_map/ppermute | solution.py:221
  43.0 5.7 %collective-permute-start.19 = (f32[8,128]{1,0:T(8,128)S(1)}, f32[8,128]{1,0:T(8,128)S(1)}, u32[]{:S(2)}, u32[]{:S(2)}) collective-permute-start(f32[8,128]{1,0:T(8,128)S(1)} %shard_map.81.refs_2_.refs_0_), channel_id=1, source_target_pairs={{0,3},{1,2},{2,1},{3,0},{4,7},{5,6},{6,5},{7,4},{8,11},{9,10},{10,... | collective-permute-start | bytes 12296 | tf_op jit(solution)/shard_map/ppermute | solution.py:221
